TPU v7x, 128 devices: a whole 4x4x4 slice. The times are simulated.
128 devices in a mesh: rows: 16 (over x, z_hi, core), blk: 8 (over z_lo, y).
Axes of the slice: x: 4, y: 4, z: 4 (z_hi: 2, z_lo: 2; z = z_hi * 2 + z_lo), core: 2. Of those that a mesh axis runs over, the one named last changes fastest.
Arguments:
- p2_tiles: bfloat16 [16, 8, 128, 16384], P('rows', 'blk'), may hold values from -6 to 6
- window_tiles: bfloat16 [8, 64, 16384], P('blk'), may hold values from -0.09375 to 0.09375
- square_tiles: bfloat16 [16, 8, 64, 16384], P('rows', 'blk'), may hold values from -4 to 4
- pairs: int32 [16, 8, 8, 2, 256], P('rows', 'blk'), may hold values from -1 to 127, as said below
- tasks: int32 [16, 8, 16, 16, 3], P('rows', 'blk'), may hold values from -1 to 63, as said below
- basis: bfloat16 [16, 32, 128, 128], P('rows'), may hold values from -0.052978516 to 0.052978516
Outputs:
- purified: bfloat16 [16, 8, 64, 16384], P('rows', 'blk')
- density_grid: float32 [2048], P(('rows', 'blk'))
Inputs may be any that keep to these rules, and one draw needn't show every extreme that they name: Row 0 holds -1 or an A tile below 128; row 1 a window tile below 64. The share of live pairs differs between devices. `tasks`: tile ids are -1 or below 64, live slots come first; basis ids are below 32. Some owner receives 16 live slots from every device.
All inputs are finite; a program needn't handle non-finite values.
Results may differ from a plain program's by a relative error of at most 0.0029.
Values may be sent and summed in bfloat16 or wider, within the bound.
No kernel may reach another device: no remote copies, remote signals or barrier semaphores. Data moves between devices by JAX's collectives and lax.ppermute only.
A program may use at most 320 MiB of HBM per device.

v0:
```python
import jax
import jax.numpy as jnp
from jax import lax
from jax.sharding import PartitionSpec as P

BS = 128


def passed_along(value, axis, steps):
    count = lax.axis_size(axis)
    pairs = [(source, (source + steps) % count) for source in range(count)]
    return lax.ppermute(value, axis, pairs)


def step_product(total, a_tiles, piece, step_pairs):
    left = step_pairs[0]
    right = step_pairs[1]
    gathered_a = jnp.take(a_tiles, jnp.maximum(left, 0), axis=0)
    gathered_a = jnp.where((left >= 0)[:, None], gathered_a, jnp.zeros_like(gathered_a))
    gathered_b = jnp.take(piece, right, axis=0)
    count = total.shape[0]
    lhs = gathered_a.reshape(count, -1, BS, BS)
    rhs = gathered_b.reshape(count, -1, BS, BS)
    return total + jnp.einsum("ckij,ckjl->cil", lhs, rhs, preferred_element_type=jnp.float32)


def body(p2_tiles, window_tiles, square_tiles, pairs, tasks, basis):
    a_tiles = p2_tiles[0, 0]
    plan = pairs[0, 0]
    cycle_size = lax.axis_size("blk")
    tile_count = square_tiles.shape[2]
    total = jnp.zeros((tile_count, BS, BS), jnp.float32)
    piece = window_tiles[0]
    total = step_product(total, a_tiles, piece, plan[0])
    for step in range(1, cycle_size):
        piece = passed_along(piece, "blk", 1)
        total = step_product(total, a_tiles, piece, plan[step])
    square = square_tiles[0, 0].reshape(tile_count, BS, BS).astype(jnp.float32)
    purified = (3.0 * square - 2.0 * total).astype(jnp.bfloat16)
    flat_tiles = purified.reshape(tile_count, BS * BS)
    task = tasks[0, 0]
    tile_ids = task[..., 0]
    outgoing = jnp.take(flat_tiles, jnp.maximum(tile_ids, 0), axis=0)
    outgoing = jnp.where((tile_ids >= 0)[..., None], outgoing, jnp.zeros_like(outgoing))
    labels = task[..., 1:3]
    tables = basis[0]
    tiles = lax.all_to_all(outgoing, "rows", split_axis=0, concat_axis=0, tiled=True)
    which = lax.all_to_all(labels, "rows", split_axis=0, concat_axis=0, tiled=True)

    def per_source(item):
        blocks, ids = item
        row_basis = jnp.take(tables, ids[:, 0], axis=0)
        col_basis = jnp.take(tables, ids[:, 1], axis=0)
        mats = blocks.reshape(-1, BS, BS)
        spread = jnp.einsum("kij,kjg->kig", mats, col_basis, preferred_element_type=jnp.float32)
        return jnp.sum(row_basis.astype(jnp.float32) * spread, axis=1)

    values = lax.map(per_source, (tiles, which))
    partial_grid = jnp.sum(values, axis=(0, 1))
    shares = lax.psum_scatter(partial_grid, "blk", scatter_dimension=0, tiled=True)
    return (purified.reshape(1, 1, tile_count, BS * BS), shares)


def solution(mesh):
    return jax.shard_map(
        body,
        mesh=mesh,
        in_specs=(
            P("rows", "blk", None, None),
            P("blk", None, None),
            P("rows", "blk", None, None),
            P("rows", "blk", None, None, None),
            P("rows", "blk", None, None, None),
            P("rows", None, None, None),
        ),
        out_specs=(P("rows", "blk", None, None), P(("rows", "blk"))),
        check_vma=False,
    )
```

profile of v0, /device:TPU:1, one launch (start us, length us, event | category | flops | bytes accessed | tf_op | source)
XLA Modules:
  0.0 937.8 jit_solution(15123988534539269607)
XLA Ops:
  24.2 19.5 %gather_fusion.15 = bf16[256,16384]{1,0:T(8,128)(2,1)} fusion(bf16[128,16384]{1,0:T(8,128)(2,1)} %bitcast.185, s32[1024]{0:T(1024)S(1)} %pad_clamp_fusion.6), kind=kCustom, calls=%fused_computation.8.clone | custom fusion | bytes 16778240 | tf_op jit(solution)/shard_map/jit(_take)/gather | solution.py:18
  43.7 19.3 %gather_fusion.17 = bf16[256,16384]{1,0:T(8,128)(2,1)} fusion(bf16[128,16384]{1,0:T(8,128)(2,1)} %bitcast.186, s32[1024]{0:T(1024)S(1)} %pad_clamp_fusion.4), kind=kCustom, calls=%fused_computation.9.clone | custom fusion | bytes 16778240 | tf_op jit(solution)/shard_map/jit(_take)/gather | solution.py:18
  63.6 19.3 %gather_fusion.11 = bf16[256,16384]{1,0:T(8,128)(2,1)} fusion(bf16[128,16384]{1,0:T(8,128)(2,1)} %bitcast.187, s32[1024]{0:T(1024)S(1)} %pad_clamp_fusion.10), kind=kCustom, calls=%fused_computation.6.clone | custom fusion | bytes 16778240 | tf_op jit(solution)/shard_map/jit(_take)/gather | solution.py:18
  83.0 19.5 %gather_fusion.13 = bf16[256,16384]{1,0:T(8,128)(2,1)} fusion(bf16[128,16384]{1,0:T(8,128)(2,1)} %bitcast.188, s32[1024]{0:T(1024)S(1)} %pad_clamp_fusion.8), kind=kCustom, calls=%fused_computation.7.clone | custom fusion | bytes 16778240 | tf_op jit(solution)/shard_map/jit(_take)/gather | solution.py:18
  103.7 19.3 %gather_fusion.7 = bf16[256,16384]{1,0:T(8,128)(2,1)} fusion(bf16[128,16384]{1,0:T(8,128)(2,1)} %bitcast.189, s32[1024]{0:T(1024)S(1)} %pad_clamp_fusion.14), kind=kCustom, calls=%fused_computation.4.clone | custom fusion | bytes 16778240 | tf_op jit(solution)/shard_map/jit(_take)/gather | solution.py:18
  123.0 19.4 %gather_fusion.9 = bf16[256,16384]{1,0:T(8,128)(2,1)} fusion(bf16[128,16384]{1,0:T(8,128)(2,1)} %bitcast.190, s32[1024]{0:T(1024)S(1)} %pad_clamp_fusion.12), kind=kCustom, calls=%fused_computation.5.clone | custom fusion | bytes 16778240 | tf_op jit(solution)/shard_map/jit(_take)/gather | solution.py:18
  143.5 19.7 %gather_fusion.3 = bf16[256,16384]{1,0:T(8,128)(2,1)} fusion(bf16[128,16384]{1,0:T(8,128)(2,1)} %bitcast.191, s32[1024]{0:T(1024)S(1)} %pad_clamp_fusion.18), kind=kCustom, calls=%fused_computation.clone | custom fusion | bytes 16778240 | tf_op jit(solution)/shard_map/jit(_take)/gather | solution.py:18
  163.2 19.5 %gather_fusion.5 = bf16[256,16384]{1,0:T(8,128)(2,1)} fusion(bf16[128,16384]{1,0:T(8,128)(2,1)} %bitcast.192, s32[1024]{0:T(1024)S(1)} %pad_clamp_fusion.16), kind=kCustom, calls=%fused_computation.3.clone | custom fusion | bytes 16778240 | tf_op jit(solution)/shard_map/jit(_take)/gather | solution.py:18
  182.8 9.1 gather_fusion.4
  204.2 13.0 %fusion.5 = (bf16[32,8,128,128]{3,1,2,0:T(8,128)(2,1)}, bf16[32,8,128,128]{3,1,2,0:T(8,128)(2,1)}) fusion(bf16[256,16384]{1,0:T(8,128)(2,1)} %gather_fusion.17, pred[256]{0:T(512)(128)(4,1)S(1)} %copy-done.29, pred[256]{0:T(512)(128)(4,1)S(1)} %copy-done.21, bf16[256,16384]{1,0:T(8,128)(2,1)} %gather_fusion.15, pred[256]{0:T(512)(128)(4,1)S(1)} %copy-done.31, ...), kind=kLoop, calls=%fused_computation.36 | loop fusion | flops 16777216 | bytes 33555456
  217.3 11.9 %fusion.7 = (bf16[32,8,128,128]{3,1,2,0:T(8,128)(2,1)}, bf16[32,8,128,128]{3,1,2,0:T(8,128)(2,1)}) fusion(bf16[256,16384]{1,0:T(8,128)(2,1)} %gather_fusion.13, pred[256]{0:T(512)(128)(4,1)S(1)} %copy-done.32, pred[256]{0:T(512)(128)(4,1)S(1)} %copy-done.19, bf16[256,16384]{1,0:T(8,128)(2,1)S(1)} %bitcast.214, pred[256]{0:T(512)(128)(4,1)S(1)} %copy-done.33, ...), kind=kLoop, calls=%fused_computation.42 | loop fusion | flops 16777216 | bytes 33555456
  229.2 11.4 %fusion.9 = (bf16[32,8,128,128]{3,1,2,0:T(8,128)(2,1)}, bf16[32,8,128,128]{3,1,2,0:T(8,128)(2,1)}) fusion(bf16[256,16384]{1,0:T(8,128)(2,1)} %gather_fusion.9, pred[256]{0:T(512)(128)(4,1)S(1)} %copy-done.34, pred[256]{0:T(512)(128)(4,1)S(1)} %copy-done.17, bf16[256,16384]{1,0:T(8,128)(2,1)S(1)} %bitcast.218, pred[256]{0:T(512)(128)(4,1)S(1)} %copy-done.35, ...), kind=kLoop, calls=%fused_computation.48 | loop fusion | flops 16777216 | bytes 33555456
  248.5 41.6 %collective-permute-done.1 = bf16[64,16384]{1,0:T(8,128)(2,1)} collective-permute-done((bf16[64,16384]{1,0:T(8,128)(2,1)}, bf16[64,16384]{1,0:T(8,128)(2,1)}, u32[]{:S(2)}, u32[]{:S(2)}) %collective-permute-start.1) | collective-permute-done | bytes 2097184 | tf_op jit(solution)/shard_map/ppermute | solution.py:12
  291.2 9.3 copy.33
  300.4 9.3 copy.31
  309.7 9.2 copy.29
  318.9 9.2 copy.27
  328.1 9.2 copy.25
  337.3 9.2 copy.23
  346.6 9.2 copy.21
  355.8 9.3 copy.22
  365.1 9.2 copy.35
  389.5 18.4 %gather_fusion.6 = bf16[256,16384]{1,0:T(8,128)(2,1)} fusion(bf16[64,16384]{1,0:T(8,128)(2,1)} %collective-permute-done, s32[1024]{0:T(1024)S(1)} %pad_clamp_fusion.15), kind=kCustom, calls=%fused_computation.10.clone | custom fusion | bytes 16778240 | tf_op jit(solution)/shard_map/jit(_take)/gather | solution.py:20
  415.6 9.2 copy.24
  424.8 10.1 %fusion.17 = f32[64,128,128,1]{2,1,3,0:T(8,128)} fusion(bf16[64,4,128,128]{3,2,1,0:T(8,128)(2,1)} %bitcast.201, bf16[64,4,128,128]{3,2,1,0:T(8,128)(2,1)} %bitcast.206), kind=kOutput, calls=%fused_computation.141 | convolution fusion | flops 1073741824 | bytes 20971520 | tf_op jit(solution)/shard_map/ckij,ckjl->cil/dot_general | solution.py:24
  434.9 18.8 %gather_fusion.8 = bf16[256,16384]{1,0:T(8,128)(2,1)} fusion(bf16[64,16384]{1,0:T(8,128)(2,1)} %collective-permute-done.1, s32[1024]{0:T(1024)} %pad_clamp_fusion.13), kind=kCustom, calls=%fused_computation.11.clone | custom fusion | bytes 16778240 | tf_op jit(solution)/shard_map/jit(_take)/gather | solution.py:20
  461.2 9.2 copy.26
  471.5 10.1 %fusion.18 = f32[64,128,128,1]{2,1,3,0:T(8,128)} fusion(bf16[64,4,128,128]{3,2,1,0:T(8,128)(2,1)} %bitcast.200, bf16[64,4,128,128]{3,2,1,0:T(8,128)(2,1)} %bitcast.205), kind=kOutput, calls=%fused_computation.142 | convolution fusion | flops 1073741824 | bytes 20971520 | tf_op jit(solution)/shard_map/ckij,ckjl->cil/dot_general | solution.py:24
  481.6 9.2 gather_fusion.10
  498.3 9.2 copy.28
  507.5 10.1 %fusion.19 = f32[64,128,128,1]{2,1,3,0:T(8,128)} fusion(bf16[64,4,128,128]{3,2,1,0:T(8,128)(2,1)} %bitcast.199, bf16[64,4,128,128]{3,2,1,0:T(8,128)(2,1)} %bitcast.207), kind=kOutput, calls=%fused_computation.143 | convolution fusion | flops 1073741824 | bytes 20971520 | tf_op jit(solution)/shard_map/ckij,ckjl->cil/dot_general | solution.py:24
  517.6 19.0 %gather_fusion.12 = bf16[256,16384]{1,0:T(8,128)(2,1)} fusion(bf16[64,16384]{1,0:T(8,128)(2,1)} %collective-permute-done.3, s32[1024]{0:T(1024)} %pad_clamp_fusion.9), kind=kCustom, calls=%fused_computation.13.clone | custom fusion | bytes 16778240 | tf_op jit(solution)/shard_map/jit(_take)/gather | solution.py:20
  546.9 9.2 copy.30
  556.1 10.1 %fusion.20 = f32[64,128,128,1]{2,1,3,0:T(8,128)} fusion(bf16[64,4,128,128]{3,2,1,0:T(8,128)(2,1)} %bitcast.198, bf16[64,4,128,128]{3,2,1,0:T(8,128)(2,1)} %bitcast.208), kind=kOutput, calls=%fused_computation.144 | convolution fusion | flops 1073741824 | bytes 20971520 | tf_op jit(solution)/shard_map/ckij,ckjl->cil/dot_general | solution.py:24
  566.2 18.6 %gather_fusion.14 = bf16[256,16384]{1,0:T(8,128)(2,1)} fusion(bf16[64,16384]{1,0:T(8,128)(2,1)} %collective-permute-done.4, s32[1024]{0:T(1024)} %pad_clamp_fusion.7), kind=kCustom, calls=%fused_computation.14.clone | custom fusion | bytes 16778240 | tf_op jit(solution)/shard_map/jit(_take)/gather | solution.py:20
  592.3 9.2 copy.32
  601.9 10.1 %fusion.21 = f32[64,128,128,1]{2,1,3,0:T(8,128)} fusion(bf16[64,4,128,128]{3,2,1,0:T(8,128)(2,1)} %bitcast.197, bf16[64,4,128,128]{3,2,1,0:T(8,128)(2,1)} %bitcast.204), kind=kOutput, calls=%fused_computation.145 | convolution fusion | flops 1073741824 | bytes 20971520 | tf_op jit(solution)/shard_map/ckij,ckjl->cil/dot_general | solution.py:24
  612.1 9.4 %gather_fusion.16 = bf16[256,16384]{1,0:T(8,128)(2,1)} fusion(bf16[64,16384]{1,0:T(8,128)(2,1)S(1)} %collective-permute-done.5, s32[1024]{0:T(1024)} %pad_clamp_fusion.5), kind=kCustom, calls=%fused_computation.15.clone | custom fusion | bytes 16778240 | tf_op jit(solution)/shard_map/jit(_take)/gather | solution.py:20
  629.0 9.3 copy.34
  638.2 10.1 %fusion.22 = f32[64,128,128,1]{2,1,3,0:T(8,128)} fusion(bf16[64,4,128,128]{3,2,1,0:T(8,128)(2,1)} %bitcast.196, bf16[64,4,128,128]{3,2,1,0:T(8,128)(2,1)} %bitcast.209), kind=kOutput, calls=%fused_computation.146 | convolution fusion | flops 1073741824 | bytes 20971520 | tf_op jit(solution)/shard_map/ckij,ckjl->cil/dot_general | solution.py:24
  649.2 18.8 %gather_fusion.18 = bf16[256,16384]{1,0:T(8,128)(2,1)} fusion(bf16[64,16384]{1,0:T(8,128)(2,1)} %collective-permute-done.6, s32[1024]{0:T(1024)} %pad_clamp_fusion.3), kind=kCustom, calls=%fused_computation.16.clone | custom fusion | bytes 16778240 | tf_op jit(solution)/shard_map/jit(_take)/gather | solution.py:20
  675.5 9.3 copy.36
  684.8 18.6 %fusion.13 = bf16[64,128,128]{2,1,0:T(8,128)(2,1)} fusion(f32[8,8,128,128]{3,2,1,0:T(8,128)} %copy.20, f32[64,128,128,1]{2,1,3,0:T(8,128)} %fusion.22, f32[64,128,128,1]{2,1,3,0:T(8,128)} %fusion.21, f32[64,128,128,1]{2,1,3,0:T(8,128)} %fusion.20, f32[64,128,128,1]{2,1,3,0:T(8,128)} %fusion.19, f32[64,128,128,1]{2,1,3,0:T(8,128)} %fusion.18, ...), kind=kOutput, calls=%fused_computation.60 | convolution fusion | flops 1084227584 | bytes 52428800 | tf_op jit(solution)/shard_map/ckij,ckjl->cil/dot_general | solution.py:24
  706.3 9.1 gather_fusion.2
  723.1 10.5 %all-to-all-start.1 = ((bf16[16,16,16384]{2,1,0:T(8,128)(2,1)}), bf16[16,16,16384]{2,1,0:T(8,128)(2,1)}, u32[]{:S(2)}, u32[]{:S(2)}) async-start(bf16[16,16,16384]{2,1,0:T(8,128)(2,1)} %select_select_fusion.8), calls=%async_computation.1 | async-start | bytes 16777216 | tf_op jit(solution)/shard_map/all_to_all | solution.py:47
  737.1 128.0 %all-to-all-done.1 = bf16[16,16,16384]{2,1,0:T(8,128)(2,1)} async-done(((bf16[16,16,16384]{2,1,0:T(8,128)(2,1)}), bf16[16,16,16384]{2,1,0:T(8,128)(2,1)}, u32[]{:S(2)}, u32[]{:S(2)}) %all-to-all-start.1) | async-done | bytes 8388640 | tf_op jit(solution)/shard_map/all_to_all | solution.py:47
  865.1 57.5 %while.10 = (s32[]{:T(128)}, f32[16,16,128]{2,1,0:T(8,128)S(1)}, s32[16,16,2]{1,2,0:T(2,128)}, bf16[32,128,128]{2,1,0:T(8,128)(2,1)S(1)}, bf16[16,16,16384]{2,1,0:T(8,128)(2,1)}, /*index=5*/s32[]{:T(128)}) while((s32[]{:T(128)}, f32[16,16,128]{2,1,0:T(8,128)S(1)}, s32[16,16,2]{1,2,0:T(2,128)}, bf16[32,128,128]{2,1,0:T(8,128)(2,1)S(1)}, ...), condition=%wide.region_2.6_spmd, body=%wide.region_0.5_spmd.sunk | while | flops 68419776 | bytes 5800849 | solution.py:58
  922.6 14.2 %all-reduce = f32[128]{0:T(128)S(1)} all-reduce(f32[128]{0:T(128)S(1)} %reduce_sum.18), channel_id=2, replica_groups=mesh['rows'=16,'blk'=8] {'blk'}, use_global_device_ids=true, to_apply=%region_4.8.clone | all-reduce | flops 128 | bytes 1024
  (328 shorter events, 191.3 us)
Async XLA Ops:
  0.6 240.0 %collective-permute-start = (bf16[64,16384]{1,0:T(8,128)(2,1)}, bf16[64,16384]{1,0:T(8,128)(2,1)}, u32[]{:S(2)}, u32[]{:S(2)}) collective-permute-start(bf16[64,16384]{1,0:T(8,128)(2,1)} %bitcast.194), channel_id=1, source_target_pairs={{0,1},{1,2},{2,3},{3,4},{4,5},{5,6},{6,7},{7,0},{8,9},{9,10},{10,1... | collective-permute-start | bytes 6291464 | tf_op jit(solution)/shard_map/ppermute | solution.py:12
  4.2 718.9 %all-to-all-start = ((s32[16,16,2]{1,2,0:T(2,128)}), s32[16,16,2]{1,2,0:T(2,128)}, u32[]{:S(2)}, u32[]{:S(2)}) async-start(s32[16,16,2]{1,2,0:T(2,128)} %copy.10), calls=%async_computation | async-start | bytes 32768 | tf_op jit(solution)/shard_map/all_to_all | solution.py:48
  14.2 128.1 %copy-start.12 = (s32[1,1,1,1,256]{4,3,2,1,0:T(1,128)}, s32[1,1,1,1,256]{4,3,2,1,0:T(1,128)S(1)}, u32[]{:S(2)}) copy-start(s32[1,1,1,1,256]{4,3,2,1,0:T(1,128)S(1)} %get-tuple-element.74) | copy-start | bytes 3076
  14.2 128.7 %copy-start.10 = (s32[1,1,1,1,256]{4,3,2,1,0:T(1,128)}, s32[1,1,1,1,256]{4,3,2,1,0:T(1,128)S(1)}, u32[]{:S(2)}) copy-start(s32[1,1,1,1,256]{4,3,2,1,0:T(1,128)S(1)} %get-tuple-element.76) | copy-start | bytes 3076
  163.2 19.5 %copy-start.9 = (s32[1,1,1,1,256]{4,3,2,1,0:T(1,128)S(1)}, s32[1,1,1,1,256]{4,3,2,1,0:T(1,128)}, u32[]{:S(2)}) copy-start(s32[1,1,1,1,256]{4,3,2,1,0:T(1,128)} %get-tuple-element.78) | copy-start | bytes 3076
  163.2 19.5 %copy-start.14 = (s32[256]{0:T(256)S(1)}, s32[256]{0:T(256)}, u32[]{:S(2)}) copy-start(s32[256]{0:T(256)} %compare_select_fusion.16) | copy-start | bytes 3076
  163.2 19.6 %copy-start = (bf16[1,64,16384]{2,1,0:T(8,128)(2,1)S(1)}, bf16[1,64,16384]{2,1,0:T(8,128)(2,1)}, u32[]{:S(2)}) copy-start(bf16[1,64,16384]{2,1,0:T(8,128)(2,1)} %param.15) | copy-start | bytes 6291460
  182.8 9.1 copy-start.8
  182.8 13.5 %copy-start.5 = (s32[16,16,1]{1,0,2:T(8,128)S(1)}, s32[16,16,1]{1,0,2:T(8,128)}, u32[]{:S(2)}) copy-start(s32[16,16,1]{1,0,2:T(8,128)} %slice_maximum_fusion) | copy-start | bytes 3076
  182.8 13.6 %copy-start.27 = (pred[256]{0:T(512)(128)(4,1)S(1)}, pred[256]{0:T(512)(128)(4,1)}, u32[]{:S(2)}) copy-start(pred[256]{0:T(512)(128)(4,1)} %compare_and_fusion.16) | copy-start | bytes 772
  196.4 20.7 %slice-start = ((s8[8388608]{0:T(1024)(128)(4,1)}), s8[4194304]{0:T(1024)(128)(4,1)S(1)}, s32[]{:S(2)}) async-start(s8[8388608]{0:T(1024)(128)(4,1)} %bitcast.213), calls=%async_computation.2 | async-start | bytes 8388608
  204.1 13.0 %slice-start.1 = ((s8[8388608]{0:T(1024)(128)(4,1)}), s8[4194304]{0:T(1024)(128)(4,1)S(1)}, s32[]{:S(2)}) async-start(s8[8388608]{0:T(1024)(128)(4,1)} %bitcast.213), calls=%async_computation.3 | async-start | bytes 8388608
  204.1 13.0 %copy-start.19 = (pred[256]{0:T(512)(128)(4,1)S(1)}, pred[256]{0:T(512)(128)(4,1)}, u32[]{:S(2)}) copy-start(pred[256]{0:T(512)(128)(4,1)} %get-tuple-element.40) | copy-start | bytes 772
  204.2 13.0 %copy-start.20 = (pred[256]{0:T(512)(128)(4,1)S(1)}, pred[256]{0:T(512)(128)(4,1)}, u32[]{:S(2)}) copy-start(pred[256]{0:T(512)(128)(4,1)} %get-tuple-element.41) | copy-start | bytes 772
  204.2 13.0 %copy-start.32 = (pred[256]{0:T(512)(128)(4,1)S(1)}, pred[256]{0:T(512)(128)(4,1)}, u32[]{:S(2)}) copy-start(pred[256]{0:T(512)(128)(4,1)} %compare_and_fusion.7) | copy-start | bytes 772
  204.2 13.0 %copy-start.33 = (pred[256]{0:T(512)(128)(4,1)S(1)}, pred[256]{0:T(512)(128)(4,1)}, u32[]{:S(2)}) copy-start(pred[256]{0:T(512)(128)(4,1)} %compare_and_fusion.9) | copy-start | bytes 772
  204.2 25.0 %slice-start.4 = ((s8[8388608]{0:T(1024)(128)(4,1)}), s8[4194304]{0:T(1024)(128)(4,1)S(1)}, s32[]{:S(2)}) async-start(s8[8388608]{0:T(1024)(128)(4,1)} %bitcast.217), calls=%async_computation.6 | async-start | bytes 8388608
  217.2 11.9 %slice-start.5 = ((s8[8388608]{0:T(1024)(128)(4,1)}), s8[4194304]{0:T(1024)(128)(4,1)S(1)}, s32[]{:S(2)}) async-start(s8[8388608]{0:T(1024)(128)(4,1)} %bitcast.217), calls=%async_computation.7 | async-start | bytes 8388608
  217.2 11.9 %copy-start.17 = (pred[256]{0:T(512)(128)(4,1)S(1)}, pred[256]{0:T(512)(128)(4,1)}, u32[]{:S(2)}) copy-start(pred[256]{0:T(512)(128)(4,1)} %get-tuple-element.42) | copy-start | bytes 772
  217.2 11.9 %copy-start.18 = (pred[256]{0:T(512)(128)(4,1)S(1)}, pred[256]{0:T(512)(128)(4,1)}, u32[]{:S(2)}) copy-start(pred[256]{0:T(512)(128)(4,1)} %get-tuple-element.43) | copy-start | bytes 772
  217.2 11.9 %copy-start.34 = (pred[256]{0:T(512)(128)(4,1)S(1)}, pred[256]{0:T(512)(128)(4,1)}, u32[]{:S(2)}) copy-start(pred[256]{0:T(512)(128)(4,1)} %compare_and_fusion.11) | copy-start | bytes 772
  217.3 11.9 %copy-start.35 = (pred[256]{0:T(512)(128)(4,1)S(1)}, pred[256]{0:T(512)(128)(4,1)}, u32[]{:S(2)}) copy-start(pred[256]{0:T(512)(128)(4,1)} %compare_and_fusion.13) | copy-start | bytes 772
  217.3 24.7 %slice-start.2 = ((s8[8388608]{0:T(1024)(128)(4,1)}), s8[4194304]{0:T(1024)(128)(4,1)S(1)}, s32[]{:S(2)}) async-start(s8[8388608]{0:T(1024)(128)(4,1)} %bitcast.215), calls=%async_computation.4 | async-start | bytes 8388608
  217.3 24.7 %slice-start.6 = ((s8[8388608]{0:T(1024)(128)(4,1)}), s8[4194304]{0:T(1024)(128)(4,1)S(1)}, s32[]{:S(2)}) async-start(s8[8388608]{0:T(1024)(128)(4,1)} %bitcast.219), calls=%async_computation.8 | async-start | bytes 8388608
  229.2 12.8 %slice-start.3 = ((s8[8388608]{0:T(1024)(128)(4,1)}), s8[4194304]{0:T(1024)(128)(4,1)S(1)}, s32[]{:S(2)}) async-start(s8[8388608]{0:T(1024)(128)(4,1)} %bitcast.215), calls=%async_computation.5 | async-start | bytes 8388608
  229.2 12.8 %slice-start.7 = ((s8[8388608]{0:T(1024)(128)(4,1)}), s8[4194304]{0:T(1024)(128)(4,1)S(1)}, s32[]{:S(2)}) async-start(s8[8388608]{0:T(1024)(128)(4,1)} %bitcast.219), calls=%async_computation.9 | async-start | bytes 8388608
  229.2 12.8 %copy-start.15 = (pred[256]{0:T(512)(128)(4,1)S(1)}, pred[256]{0:T(512)(128)(4,1)}, u32[]{:S(2)}) copy-start(pred[256]{0:T(512)(128)(4,1)} %get-tuple-element.44) | copy-start | bytes 772
  229.2 12.8 %copy-start.16 = (pred[256]{0:T(512)(128)(4,1)S(1)}, pred[256]{0:T(512)(128)(4,1)}, u32[]{:S(2)}) copy-start(pred[256]{0:T(512)(128)(4,1)} %get-tuple-element.45) | copy-start | bytes 772
  229.2 12.8 %copy-start.28 = (pred[256]{0:T(512)(128)(4,1)S(1)}, pred[256]{0:T(512)(128)(4,1)}, u32[]{:S(2)}) copy-start(pred[256]{0:T(512)(128)(4,1)} %compare_and_fusion.15) | copy-start | bytes 772
  229.2 12.8 %copy-start.30 = (pred[256]{0:T(512)(128)(4,1)S(1)}, pred[256]{0:T(512)(128)(4,1)}, u32[]{:S(2)}) copy-start(pred[256]{0:T(512)(128)(4,1)} %compare_and_fusion.17) | copy-start | bytes 772
  240.7 49.5 %collective-permute-start.1 = (bf16[64,16384]{1,0:T(8,128)(2,1)}, bf16[64,16384]{1,0:T(8,128)(2,1)}, u32[]{:S(2)}, u32[]{:S(2)}) collective-permute-start(bf16[64,16384]{1,0:T(8,128)(2,1)} %collective-permute-done), channel_id=1, source_target_pairs={{0,1},{1,2},{2,3},{3,4},{4,5},{5,6},{6,7},{7,0},{8,9},{9,10},{10,1... | collective-permute-start | bytes 6291464 | tf_op jit(solution)/shard_map/ppermute | solution.py:12
  290.2 117.7 %collective-permute-start.2 = (bf16[64,16384]{1,0:T(8,128)(2,1)}, bf16[64,16384]{1,0:T(8,128)(2,1)S(1)}, u32[]{:S(2)}, u32[]{:S(2)}) collective-permute-start(bf16[64,16384]{1,0:T(8,128)(2,1)} %collective-permute-done.1), channel_id=1, source_target_pairs={{0,1},{1,2},{2,3},{3,4},{4,5},{5,6},{6,7},{7,0},{8,9},{9,10},{10,1... | collective-permute-start | bytes 6291464 | tf_op jit(solution)/shard_map/ppermute | solution.py:12
  365.1 14.4 %copy-start.13 = (s32[1,1,1,1,256]{4,3,2,1,0:T(1,128)S(1)}, s32[1,1,1,1,256]{4,3,2,1,0:T(1,128)}, u32[]{:S(2)}) copy-start(s32[1,1,1,1,256]{4,3,2,1,0:T(1,128)} %copy-done.12) | copy-start | bytes 3076
  407.9 62.4 %collective-permute-start.3 = (bf16[64,16384]{1,0:T(8,128)(2,1)S(1)}, bf16[64,16384]{1,0:T(8,128)(2,1)}, u32[]{:S(2)}, u32[]{:S(2)}) collective-permute-start(bf16[64,16384]{1,0:T(8,128)(2,1)S(1)} %collective-permute-done.2), channel_id=1, source_target_pairs={{0,1},{1,2},{2,3},{3,4},{4,5},{5,6},{6,7},{7,0},{8,9},{9,10},{10,1... | collective-permute-start | bytes 6291464 | tf_op jit(solution)/shard_map/ppermute | solution.py:12
  470.4 66.3 %collective-permute-start.4 = (bf16[64,16384]{1,0:T(8,128)(2,1)}, bf16[64,16384]{1,0:T(8,128)(2,1)}, u32[]{:S(2)}, u32[]{:S(2)}) collective-permute-start(bf16[64,16384]{1,0:T(8,128)(2,1)} %collective-permute-done.3), channel_id=1, source_target_pairs={{0,1},{1,2},{2,3},{3,4},{4,5},{5,6},{6,7},{7,0},{8,9},{9,10},{10,1... | collective-permute-start | bytes 6291464 | tf_op jit(solution)/shard_map/ppermute | solution.py:12
  517.6 21.8 %copy-start.25 = (pred[256]{0:T(512)(128)(4,1)S(1)}, pred[256]{0:T(512)(128)(4,1)}, u32[]{:S(2)}) copy-start(pred[256]{0:T(512)(128)(4,1)} %compare_and_fusion.8) | copy-start | bytes 772
  536.6 64.9 %collective-permute-start.5 = (bf16[64,16384]{1,0:T(8,128)(2,1)}, bf16[64,16384]{1,0:T(8,128)(2,1)S(1)}, u32[]{:S(2)}, u32[]{:S(2)}) collective-permute-start(bf16[64,16384]{1,0:T(8,128)(2,1)} %collective-permute-done.4), channel_id=1, source_target_pairs={{0,1},{1,2},{2,3},{3,4},{4,5},{5,6},{6,7},{7,0},{8,9},{9,10},{10,1... | collective-permute-start | bytes 6291464 | tf_op jit(solution)/shard_map/ppermute | solution.py:12
  566.2 18.6 %copy-start.24 = (pred[256]{0:T(512)(128)(4,1)S(1)}, pred[256]{0:T(512)(128)(4,1)}, u32[]{:S(2)}) copy-start(pred[256]{0:T(512)(128)(4,1)} %compare_and_fusion.6) | copy-start | bytes 772
  601.5 47.6 %collective-permute-start.6 = (bf16[64,16384]{1,0:T(8,128)(2,1)S(1)}, bf16[64,16384]{1,0:T(8,128)(2,1)}, u32[]{:S(2)}, u32[]{:S(2)}) collective-permute-start(bf16[64,16384]{1,0:T(8,128)(2,1)S(1)} %collective-permute-done.5), channel_id=1, source_target_pairs={{0,1},{1,2},{2,3},{3,4},{4,5},{5,6},{6,7},{7,0},{8,9},{9,10},{10,1... | collective-permute-start | bytes 6291464 | tf_op jit(solution)/shard_map/ppermute | solution.py:12
  612.1 9.4 %copy-start.23 = (pred[256]{0:T(512)(128)(4,1)S(1)}, pred[256]{0:T(512)(128)(4,1)}, u32[]{:S(2)}) copy-start(pred[256]{0:T(512)(128)(4,1)} %compare_and_fusion.4) | copy-start | bytes 772
  648.4 19.6 %copy-start.26 = (pred[256]{0:T(512)(128)(4,1)S(1)}, pred[256]{0:T(512)(128)(4,1)}, u32[]{:S(2)}) copy-start(pred[256]{0:T(512)(128)(4,1)} %compare_and_fusion.2) | copy-start | bytes 772
  684.8 21.5 %copy-start.4 = (s32[1024]{0:T(1024)S(1)}, s32[1024]{0:T(1024)}, u32[]{:S(2)}) copy-start(s32[1024]{0:T(1024)} %pad_clamp_fusion.2) | copy-start | bytes 12292
  706.3 9.1 copy-start.6
  706.3 9.1 copy-start.7
  723.1 10.5 %copy-start.36 = (u32[128]{0:T(128)S(1)}, u32[128]{0:T(128)}, u32[]{:S(2)}) copy-start(u32[128]{0:T(128)} %constant.81) | copy-start | bytes 1540
  723.1 11.7 %copy-start.3 = (bf16[64,128,128]{2,1,0:T(8,128)(2,1)S(1)}, bf16[64,128,128]{2,1,0:T(8,128)(2,1)}, u32[]{:S(2)}) copy-start(bf16[64,128,128]{2,1,0:T(8,128)(2,1)} %fusion.13) | copy-start | bytes 6291460
  723.1 142.0 %copy-start.2 = (bf16[1,32,128,128]{3,2,1,0:T(8,128)(2,1)S(1)}, bf16[1,32,128,128]{3,2,1,0:T(8,128)(2,1)}, u32[]{:S(2)}) copy-start(bf16[1,32,128,128]{3,2,1,0:T(8,128)(2,1)} %param.19) | copy-start | bytes 3145732
  723.1 142.0 %all-to-all-start.1 = ((bf16[16,16,16384]{2,1,0:T(8,128)(2,1)}), bf16[16,16,16384]{2,1,0:T(8,128)(2,1)}, u32[]{:S(2)}, u32[]{:S(2)}) async-start(bf16[16,16,16384]{2,1,0:T(8,128)(2,1)} %select_select_fusion.8), calls=%async_computation.1 | async-start | bytes 16777216 | tf_op jit(solution)/shard_map/all_to_all | solution.py:47
  (6 other events, 43.0 us)
where the time goes:
time: 954 us; the launch traced here: 938 us
  local copies, waits for them, and re-layouts  497 us (52%)
  waiting for transfers between devices  170 us (18%)
  other arithmetic  132 us (14%)
  matrix products  93.5 us (10%)
  starting transfers between devices  27.5 us (3%)
  blocking collectives  14.2 us (1%)
    unnamed x110, local copies, waits for them, and re-layouts  157 us
    gather x8, local copies, waits for them, and re-layouts, step_product(): gathered_a = jnp.take(a_tiles, jnp.maximum(left, 0), axis=0)  155 us
    all_to_all x1, waiting for transfers between devices, body(): lax.all_to_all(outgoing, 'rows', split_axis=0, concat_axis=0, tiled=True)  128 us
    gather x8, local copies, waits for them, and re-layouts, step_product(): gathered_b = jnp.take(piece, right, axis=0)  121 us
    unnamed x17, other arithmetic  107 us
    dot_general x8, matrix products, step_product(): jnp.einsum('ckij,ckjl->cil', lhs, rhs, preferred_element_type=jnp.float32)  87.4 us
    ppermute x7, waiting for transfers between devices, passed_along(): return lax.ppermute(value, axis, pairs)  42.5 us
  transfers between devices with their start and end apart: 9, of which 3 were waited for; matrix products, arithmetic and copies ran while one was open for 71% of the time, Pallas kernels for 0%

commit v1 on v0

v1 whole, which is shorter than its diff:
```python
import jax
import jax.numpy as jnp
from jax import lax
from jax.experimental import pallas as pl
from jax.experimental.pallas import tpu as pltpu
from jax.sharding import Mesh
from jax.sharding import PartitionSpec as P

BS = 128
A_TILES = 128
B_TILES = 64
C_TILES = 64
KSTEP = 4
SLOT = 16
NBAS = 32
OWNERS = 16
HALF = 32
ROWS = ("x", "zh", "core")
BLK = ("zl", "y")
MIB = 1 << 20


def around(value, axis):
    pairs = []
    for core in range(2):
        for place in range(4):
            to = (place + 1) % 4 if core == 0 else (place + 3) % 4
            if axis == "x":
                pairs.append((place * 2 + core, to * 2 + core))
            else:
                pairs.append((core * 4 + place, core * 4 + to))
    return lax.ppermute(value, ("x", "core") if axis == "x" else ("core", axis), pairs)


def across(value, axes):
    count = 2 ** len(axes)
    return lax.ppermute(value, axes, [(i, count - 1 - i) for i in range(count)])


def swapped(value):
    return across(value, ("core",))


def gather_shares(mine, other, axis, link):
    near_a = around(mine, axis)
    pair_a = across(mine, link)
    near_b = around(other, axis)
    pair_b = swapped(pair_a)
    far_a = around(near_a, axis)
    pnear_a = around(pair_a, axis)
    pfar_a = across(far_a, link)
    pnear_b = around(pair_b, axis)
    return [
        mine, other, near_a, near_b, swapped(near_a), swapped(near_b), far_a, swapped(far_a),
        pair_a, pair_b, pnear_a, pnear_b, swapped(pnear_a), swapped(pnear_b), pfar_a, swapped(pfar_a),
    ]


def slot_of(pair, hop, half, core):
    rel = half ^ core
    ahead = jnp.where(core == 0, 3, 1)
    place = jnp.where(hop == 0, rel, jnp.where(hop == 2, 6 + rel, jnp.where(hop == ahead, 2 + rel, 5 - rel)))
    return pair * 8 + place


def tile_sums(total, c, group, first, a_ref, w_ref, left_ref, right_ref):
    for share in range(first, first + group):
        for k in range(0, KSTEP, 2):
            at = share * (C_TILES * KSTEP) + c * KSTEP + k
            lhs = jnp.concatenate([a_ref[left_ref[at]], a_ref[left_ref[at + 1]]], axis=1)
            rhs = jnp.concatenate([w_ref[right_ref[at]], w_ref[right_ref[at + 1]]], axis=0)
            total = total + jnp.dot(lhs, rhs, preferred_element_type=jnp.float32)
    return total


def early_kernel(count, left_ref, right_ref, a_hbm, *rest):
    pieces = rest[: 2 * count]
    out_ref, a_ref, w_ref, sems = rest[2 * count :]
    copies = [pltpu.make_async_copy(a_hbm, a_ref.at[pl.ds(0, A_TILES)], sems.at[0])]
    for i, piece in enumerate(pieces):
        copies.append(pltpu.make_async_copy(piece, w_ref.at[pl.ds(i * HALF, HALF)], sems.at[1 + i]))
    for copy in copies:
        copy.start()
    a_ref[A_TILES] = jnp.zeros((BS, BS), jnp.bfloat16)
    for copy in copies:
        copy.wait()

    def one(c, carry):
        total = tile_sums(jnp.zeros((BS, BS), jnp.float32), c, count, 0, a_ref, w_ref, left_ref, right_ref)
        out_ref[c] = total
        return carry

    lax.fori_loop(0, C_TILES, one, 0)


def late_kernel(count, left_ref, right_ref, tile_ref, row_ref, col_ref, a_hbm, acc_hbm, sq_hbm, *rest):
    pieces = rest[: 2 * count]
    slabs = rest[2 * count : 2 * count + 16]
    out_ref, grid_ref, a_ref, w_ref, acc_ref, sq_ref, p_ref, b_ref, sems = rest[2 * count + 16 :]
    copies = [
        pltpu.make_async_copy(a_hbm, a_ref.at[pl.ds(0, A_TILES)], sems.at[0]),
        pltpu.make_async_copy(acc_hbm, acc_ref, sems.at[1]),
        pltpu.make_async_copy(sq_hbm, sq_ref, sems.at[2]),
    ]
    for i, piece in enumerate(pieces):
        copies.append(pltpu.make_async_copy(piece, w_ref.at[pl.ds(i * HALF, HALF)], sems.at[3 + i]))
    tables = []
    for i, slab in enumerate(slabs):
        tables.append(pltpu.make_async_copy(slab, b_ref.at[pl.ds(i * NBAS, NBAS)], sems.at[3 + 2 * count + i]))
    for copy in copies + tables:
        copy.start()
    a_ref[A_TILES] = jnp.zeros((BS, BS), jnp.bfloat16)
    p_ref[C_TILES] = jnp.zeros((BS, BS), jnp.bfloat16)
    for copy in copies:
        copy.wait()

    def one(c, carry):
        total = tile_sums(acc_ref[c], c, count, 0, a_ref, w_ref, left_ref, right_ref)
        pure = (3.0 * sq_ref[c].astype(jnp.float32) - 2.0 * total).astype(jnp.bfloat16)
        p_ref[c] = pure
        out_ref[c] = pure
        return carry

    lax.fori_loop(0, C_TILES, one, 0)
    for copy in tables:
        copy.wait()

    def owner(s, carry):
        live = jnp.int32(0)
        for t in range(SLOT):
            live = live + jnp.where(tile_ref[s * SLOT + t] < C_TILES, 1, 0)

        def four(g, total):
            for t in range(4):
                at = s * SLOT + g * 4 + t
                spread = jnp.dot(p_ref[tile_ref[at]], b_ref[col_ref[at]], preferred_element_type=jnp.float32)
                total = total + b_ref[row_ref[at]].astype(jnp.float32) * spread
            return total

        total = lax.fori_loop(0, (live + 3) // 4, four, jnp.zeros((BS, BS), jnp.float32))
        grid_ref[pl.ds(s, 1), :] = jnp.sum(total, axis=0, keepdims=True)
        return carry

    lax.fori_loop(0, OWNERS, owner, 0)


def smem():
    return pl.BlockSpec(memory_space=pltpu.SMEM)


def hbm():
    return pl.BlockSpec(memory_space=pl.ANY)


def vmem():
    return pl.BlockSpec(memory_space=pltpu.VMEM)


def early_product(left, right, a_tiles, pieces):
    count = len(pieces) // 2
    flops = 2 * count * C_TILES * KSTEP * BS**3
    return pl.pallas_call(
        lambda *refs: early_kernel(count, *refs),
        out_shape=jax.ShapeDtypeStruct((C_TILES, BS, BS), jnp.float32),
        in_specs=[smem(), smem(), hbm()] + [hbm()] * len(pieces),
        out_specs=vmem(),
        scratch_shapes=[
            pltpu.VMEM((A_TILES + 1, BS, BS), jnp.bfloat16),
            pltpu.VMEM((len(pieces) * HALF, BS, BS), jnp.bfloat16),
            pltpu.SemaphoreType.DMA((1 + len(pieces),)),
        ],
        compiler_params=pltpu.CompilerParams(vmem_limit_bytes=24 * MIB),
        cost_estimate=pl.CostEstimate(flops=3 * flops, bytes_accessed=(8 + len(pieces)) * MIB, transcendentals=0),
        name="early_product",
    )(left, right, a_tiles, *pieces)


def late_product(left, right, tile, row, col, a_tiles, acc, square, pieces, slabs):
    count = len(pieces) // 2
    flops = 2 * count * C_TILES * KSTEP * BS**3
    return pl.pallas_call(
        lambda *refs: late_kernel(count, *refs),
        out_shape=(
            jax.ShapeDtypeStruct((C_TILES, BS, BS), jnp.bfloat16),
            jax.ShapeDtypeStruct((OWNERS, BS), jnp.float32),
        ),
        in_specs=[smem()] * 5 + [hbm()] * 3 + [hbm()] * (len(pieces) + len(slabs)),
        out_specs=(vmem(), vmem()),
        scratch_shapes=[
            pltpu.VMEM((A_TILES + 1, BS, BS), jnp.bfloat16),
            pltpu.VMEM((len(pieces) * HALF, BS, BS), jnp.bfloat16),
            pltpu.VMEM((C_TILES, BS, BS), jnp.float32),
            pltpu.VMEM((C_TILES, BS, BS), jnp.bfloat16),
            pltpu.VMEM((C_TILES + 1, BS, BS), jnp.bfloat16),
            pltpu.VMEM((OWNERS * NBAS, BS, BS), jnp.bfloat16),
            pltpu.SemaphoreType.DMA((3 + len(pieces) + len(slabs),)),
        ],
        compiler_params=pltpu.CompilerParams(vmem_limit_bytes=48 * MIB),
        cost_estimate=pl.CostEstimate(flops=3 * flops, bytes_accessed=40 * MIB, transcendentals=0),
        name="late_product",
    )(left, right, tile, row, col, a_tiles, acc, square, *pieces, *slabs)


EARLY_SLOTS = (0, 1, 2, 3, 4, 5, 6, 7, 8, 9)
LATE_SLOTS = (10, 11, 12, 13, 14, 15)
EARLY_SHARES = ((0, 0), (0, 1), (0, 3), (0, 2), (1, 0))
LATE_SHARES = ((1, 1), (1, 3), (1, 2))


def plans(pairs, core, zl, y, shares, slots):
    lefts, rights = [], []
    for pair, hop in shares:
        source = (zl ^ pair) * 4 + ((y + hop) & 3)
        step = ((zl * 4 + y) - source) & 7
        plan = lax.dynamic_index_in_dim(pairs, step, 0, keepdims=False)
        tile = plan[1]
        slot = slot_of(pair, jnp.int32(hop), tile // HALF, core) - slots[0]
        lefts.append(jnp.where(plan[0] < 0, A_TILES, plan[0]))
        rights.append(slot * HALF + tile % HALF)
    return jnp.concatenate(lefts), jnp.concatenate(rights)


def body(p2_tiles, window_tiles, square_tiles, pairs, tasks, basis):
    core = lax.axis_index("core")
    x, zh, zl, y = (lax.axis_index(name) for name in ("x", "zh", "zl", "y"))
    slab = basis[0]
    share = window_tiles[0]
    mine = lax.dynamic_slice_in_dim(share, core * HALF, HALF, 0).reshape(HALF, BS, BS)
    other = lax.dynamic_slice_in_dim(share, (1 - core) * HALF, HALF, 0).reshape(HALF, BS, BS)
    window = gather_shares(mine, other, "y", ("zl",))
    tables = gather_shares(slab, swapped(slab), "x", ("zh", "zl"))

    a_tiles = p2_tiles[0, 0].reshape(A_TILES, BS, BS)
    square = square_tiles[0, 0].reshape(C_TILES, BS, BS)
    early = plans(pairs[0, 0], core, zl, y, EARLY_SHARES, EARLY_SLOTS)
    late = plans(pairs[0, 0], core, zl, y, LATE_SHARES, LATE_SLOTS)

    task = tasks[0, 0]
    owner = jnp.arange(OWNERS, dtype=jnp.int32)[:, None]
    place = slot_of((owner // 2 % 2) ^ zh, (owner // 4 - x) & 3, owner % 2, core) * NBAS
    tile = jnp.where(task[..., 0] < 0, C_TILES, task[..., 0]).reshape(-1)
    row = (place + jnp.clip(task[..., 1], 0, NBAS - 1)).reshape(-1)
    col = (place + jnp.clip(task[..., 2], 0, NBAS - 1)).reshape(-1)

    acc = early_product(*early, a_tiles, [window[i] for i in EARLY_SLOTS])
    pure, grid = late_product(*late, tile, row, col, a_tiles, acc, square, [window[i] for i in LATE_SLOTS], tables)
    parts = lax.all_to_all(grid.reshape(128, 16), ROWS + BLK, split_axis=0, concat_axis=0, tiled=True)
    return pure.reshape(1, 1, C_TILES, BS * BS), jnp.sum(parts, axis=0)


def solution(mesh):
    split = Mesh(mesh.devices.reshape(4, 2, 2, 2, 4), ("x", "zh", "core", "zl", "y"))
    return jax.shard_map(
        body,
        mesh=split,
        in_specs=(
            P(ROWS, BLK, None, None),
            P(BLK, None, None),
            P(ROWS, BLK, None, None),
            P(ROWS, BLK, None, None, None),
            P(ROWS, BLK, None, None, None),
            P(ROWS, None, None, None),
        ),
        out_specs=(P(ROWS, BLK, None, None), P(ROWS + BLK)),
        check_vma=False,
    )
```

time: 954 us -> 200 us (0.21); the launches traced: 938 us -> 200 us
  local copies, waits for them, and re-layouts: 497 us -> 27.8 us
  other arithmetic: 132 us -> 0.86 us
  waiting for transfers between devices: 170 us -> 65.6 us
  matrix products: 93.5 us -> 0 us
  Pallas kernels: 0 us -> 57.3 us
  starting transfers between devices: 27.5 us -> 47.3 us
  blocking collectives: 14.2 us -> 0 us
    gather x49 -> x0, local copies, waits for them, and re-layouts: 307 us -> none  [the longest x8 155 us: step_product(): gathered_a = jnp.take(a_tiles, jnp.maximum(left, 0), axis=0)]
    unnamed x110 -> x39, local copies, waits for them, and re-layouts: 157 us -> 22.6 us
    all_to_all x2 -> x1, waiting for transfers between devices: 128 us -> 5.71 us  [body(): lax.all_to_all(grid.reshape(128, 16), ROWS + BLK, split_axis=0, concat_ax...]
    unnamed x17 -> x10, other arithmetic: 107 us -> 0.09 us
    dot_general x24 -> x0, matrix products: 93.5 us -> none  [the longest x8 87.4 us: step_product(): jnp.einsum('ckij,ckjl->cil', lhs, rhs, preferred_element_type=jnp.float32)]
    pallas_call x0 -> x2, Pallas kernels: none -> 57.3 us  [the longest x1 33.2 us: late_product(): pl.pallas_call(lambda *refs: late_kernel(count, *refs), out_shape=(jax.Sh...]
    ppermute x7 -> x29, starting transfers between devices: 8.41 us -> 42.3 us  [the longest x19 27.8 us: across(): return lax.ppermute(value, axes, [(i, count - 1 - i) for i in range(count)])]
    while x32 -> x0, local copies, waits for them, and re-layouts: 18.8 us -> none
  transfers between devices with their start and end apart: 9 -> 30, of which waited for: 3 -> 11; matrix products, arithmetic and copies ran while one was open for 71% -> 7% of each run, Pallas kernels for 0% -> 12%
where the time goes in v1:
time: 200 us
  waiting for transfers between devices  65.6 us (33%)
  Pallas kernels  57.3 us (29%)
  starting transfers between devices  47.3 us (24%)
  local copies, waits for them, and re-layouts  27.8 us (14%)
    ppermute x10, waiting for transfers between devices, around(): lax.ppermute(value, ('x', 'core') if axis == 'x' else ('core', axis), pairs)  34.4 us
    pallas_call x1, Pallas kernels, late_product(): pl.pallas_call(lambda *refs: late_kernel(count, *refs), out_shape=(jax.Sh...  33.2 us
    ppermute x19, starting transfers between devices, across(): return lax.ppermute(value, axes, [(i, count - 1 - i) for i in range(count)])  27.8 us
    ppermute x19, waiting for transfers between devices, across(): return lax.ppermute(value, axes, [(i, count - 1 - i) for i in range(count)])  25.5 us
    pallas_call x1, Pallas kernels, early_product(): pl.pallas_call(lambda *refs: early_kernel(count, *refs), out_shape=jax.Sh...  24.1 us
    unnamed x39, local copies, waits for them, and re-layouts  22.6 us
    ppermute x10, starting transfers between devices, around(): lax.ppermute(value, ('x', 'core') if axis == 'x' else ('core', axis), pairs)  14.4 us
    all_to_all x1, waiting for transfers between devices, body(): lax.all_to_all(grid.reshape(128, 16), ROWS + BLK, split_axis=0, concat_ax...  5.71 us
  transfers between devices with their start and end apart: 30, of which 11 were waited for; matrix products, arithmetic and copies ran while one was open for 7% of the time, Pallas kernels for 12%

profile of v1, /device:TPU:1, one launch (start us, length us, event | category | flops | bytes accessed | tf_op | source)
XLA Modules:
  0.0 199.8 jit_solution(10679679791928087382)
XLA Ops:
  0.6 1.7 dynamic-slice_bitcast_fusion
  2.6 3.6 %collective-permute-start = (bf16[32,128,128]{2,1,0:T(8,128)(2,1)S(1)}, bf16[32,128,128]{2,1,0:T(8,128)(2,1)S(1)}, u32[]{:S(2)}, u32[]{:S(2)}) collective-permute-start(bf16[32,128,128]{2,1,0:T(8,128)(2,1)S(1)} %bitcast.43), channel_id=1, source_target_pairs={{0,1},{1,2},{2,3},{3,0},{8,11},{9,8},{10,9},{11,10},{4,5},{5,6},{6... | collective-permute-start | bytes 3145736 | tf_op jit(solution)/shard_map/ppermute | solution.py:32
  6.2 1.6 collective-permute-start.6
  8.1 0.5 collective-permute-start.1
  8.6 2.5 %collective-permute-start.15 = (bf16[32,128,128]{2,1,0:T(8,128)(2,1)}, bf16[32,128,128]{2,1,0:T(8,128)(2,1)S(1)}, u32[]{:S(2)}, u32[]{:S(2)}) collective-permute-start(bf16[32,128,128]{2,1,0:T(8,128)(2,1)} %bitcast.17.refs_14_), channel_id=1, source_target_pairs={{0,32},{32,64},{64,96},{96,0},{8,104},{40,8},{72,40},{104,72},{1,3... | collective-permute-start | bytes 3145736 | tf_op jit(solution)/shard_map/ppermute | solution.py:32
  11.1 2.2 %collective-permute-start.21 = (bf16[32,128,128]{2,1,0:T(8,128)(2,1)}, bf16[32,128,128]{2,1,0:T(8,128)(2,1)}, u32[]{:S(2)}, u32[]{:S(2)}) collective-permute-start(bf16[32,128,128]{2,1,0:T(8,128)(2,1)} %bitcast.17.refs_14_), channel_id=1, source_target_pairs={{0,20},{4,16},{16,4},{20,0},{1,21},{5,17},{17,5},{21,1},{2,22},{6,... | collective-permute-start | bytes 3145736 | tf_op jit(solution)/shard_map/ppermute | solution.py:37
  13.4 4.6 %collective-permute-done.refs_5_ = bf16[32,128,128]{2,1,0:T(8,128)(2,1)S(1)} collective-permute-done((bf16[32,128,128]{2,1,0:T(8,128)(2,1)S(1)}, bf16[32,128,128]{2,1,0:T(8,128)(2,1)S(1)}, u32[]{:S(2)}, u32[]{:S(2)}) %collective-permute-start) | collective-permute-done | bytes 1048608 | tf_op jit(solution)/shard_map/ppermute | solution.py:32
  18.0 2.1 %collective-permute-start.14 = (bf16[32,128,128]{2,1,0:T(8,128)(2,1)}, bf16[32,128,128]{2,1,0:T(8,128)(2,1)}, u32[]{:S(2)}, u32[]{:S(2)}) collective-permute-start(bf16[32,128,128]{2,1,0:T(8,128)(2,1)} %bitcast.17.refs_14_), channel_id=1, source_target_pairs={{0,8},{8,0},{1,9},{9,1},{2,10},{10,2},{3,11},{11,3},{4,12},{12,4},... | collective-permute-start | bytes 3145736 | tf_op jit(solution)/shard_map/ppermute | solution.py:37
  20.1 11.4 %collective-permute-done.6.refs_11_ = bf16[32,128,128]{2,1,0:T(8,128)(2,1)} collective-permute-done((bf16[32,128,128]{2,1,0:T(8,128)(2,1)S(1)}, bf16[32,128,128]{2,1,0:T(8,128)(2,1)}, u32[]{:S(2)}, u32[]{:S(2)}) %collective-permute-start.6) | collective-permute-done | bytes 1048608 | tf_op jit(solution)/shard_map/ppermute | solution.py:37
  31.8 0.7 copy-done.1
  32.5 1.0 copy-done.10
  33.7 3.8 %collective-permute-done.21.refs_22_ = bf16[32,128,128]{2,1,0:T(8,128)(2,1)} collective-permute-done((bf16[32,128,128]{2,1,0:T(8,128)(2,1)}, bf16[32,128,128]{2,1,0:T(8,128)(2,1)}, u32[]{:S(2)}, u32[]{:S(2)}) %collective-permute-start.21) | collective-permute-done | bytes 1048608 | tf_op jit(solution)/shard_map/ppermute | solution.py:37
  37.5 2.0 collective-permute-start.22
  39.5 6.0 %collective-permute-done.4.refs_9_ = bf16[32,128,128]{2,1,0:T(8,128)(2,1)} collective-permute-done((bf16[32,128,128]{2,1,0:T(8,128)(2,1)S(1)}, bf16[32,128,128]{2,1,0:T(8,128)(2,1)}, u32[]{:S(2)}, u32[]{:S(2)}) %collective-permute-start.4) | collective-permute-done | bytes 1048608 | tf_op jit(solution)/shard_map/ppermute | solution.py:32
  45.5 2.5 %collective-permute-start.23 = (bf16[32,128,128]{2,1,0:T(8,128)(2,1)}, bf16[32,128,128]{2,1,0:T(8,128)(2,1)}, u32[]{:S(2)}, u32[]{:S(2)}) collective-permute-start(bf16[32,128,128]{2,1,0:T(8,128)(2,1)} %collective-permute-done.21.refs_22_), channel_id=1, source_target_pairs={{0,32},{32,64},{64,96},{96,0},{8,104},{40,8},{72,40},{104,72},{1,3... | collective-permute-start | bytes 3145736 | tf_op jit(solution)/shard_map/ppermute | solution.py:32
  48.0 1.3 collective-permute-start.3
  49.3 1.5 collective-permute-start.19
  50.8 0.9 collective-permute-done.3.refs_8_
  51.8 1.0 copy-done.3
  53.1 3.6 %collective-permute-done.8.refs_8_ = bf16[32,128,128]{2,1,0:T(8,128)(2,1)} collective-permute-done((bf16[32,128,128]{2,1,0:T(8,128)(2,1)}, bf16[32,128,128]{2,1,0:T(8,128)(2,1)}, u32[]{:S(2)}, u32[]{:S(2)}) %collective-permute-start.8) | collective-permute-done | bytes 1048608 | tf_op jit(solution)/shard_map/ppermute | solution.py:32
  56.8 2.5 %collective-permute-start.16 = (bf16[32,128,128]{2,1,0:T(8,128)(2,1)}, bf16[32,128,128]{2,1,0:T(8,128)(2,1)S(1)}, u32[]{:S(2)}, u32[]{:S(2)}) collective-permute-start(bf16[32,128,128]{2,1,0:T(8,128)(2,1)} %collective-permute-done.14.refs_15_), channel_id=1, source_target_pairs={{0,32},{32,64},{64,96},{96,0},{8,104},{40,8},{72,40},{104,72},{1,3... | collective-permute-start | bytes 3145736 | tf_op jit(solution)/shard_map/ppermute | solution.py:32
  59.2 12.1 %collective-permute-done.19.refs_20_ = bf16[32,128,128]{2,1,0:T(8,128)(2,1)} collective-permute-done((bf16[32,128,128]{2,1,0:T(8,128)(2,1)}, bf16[32,128,128]{2,1,0:T(8,128)(2,1)}, u32[]{:S(2)}, u32[]{:S(2)}) %collective-permute-start.19) | collective-permute-done | bytes 1048608 | tf_op jit(solution)/shard_map/ppermute | solution.py:32
  71.3 4.0 %collective-permute-start.5 = (bf16[32,128,128]{2,1,0:T(8,128)(2,1)}, bf16[32,128,128]{2,1,0:T(8,128)(2,1)S(1)}, u32[]{:S(2)}, u32[]{:S(2)}) collective-permute-start(bf16[32,128,128]{2,1,0:T(8,128)(2,1)} %collective-permute-done.4.refs_9_), channel_id=1, source_target_pairs={{0,8},{8,0},{1,9},{9,1},{2,10},{10,2},{3,11},{11,3},{4,12},{12,4},... | collective-permute-start | bytes 3145736 | tf_op jit(solution)/shard_map/ppermute | solution.py:37
  75.4 1.8 collective-permute-start.12
  77.3 5.3 %collective-permute-done.16.refs_17_ = bf16[32,128,128]{2,1,0:T(8,128)(2,1)S(1)} collective-permute-done((bf16[32,128,128]{2,1,0:T(8,128)(2,1)}, bf16[32,128,128]{2,1,0:T(8,128)(2,1)S(1)}, u32[]{:S(2)}, u32[]{:S(2)}) %collective-permute-start.16) | collective-permute-done | bytes 1048608 | tf_op jit(solution)/shard_map/ppermute | solution.py:32
  82.5 3.8 %collective-permute-start.27 = (bf16[32,128,128]{2,1,0:T(8,128)(2,1)}, bf16[32,128,128]{2,1,0:T(8,128)(2,1)}, u32[]{:S(2)}, u32[]{:S(2)}) collective-permute-start(bf16[32,128,128]{2,1,0:T(8,128)(2,1)} %collective-permute-done.19.refs_20_), channel_id=1, source_target_pairs={{0,20},{4,16},{16,4},{20,0},{1,21},{5,17},{17,5},{21,1},{2,22},{6,... | collective-permute-start | bytes 3145736 | tf_op jit(solution)/shard_map/ppermute | solution.py:37
  86.3 4.4 %collective-permute-start.20 = (bf16[32,128,128]{2,1,0:T(8,128)(2,1)}, bf16[32,128,128]{2,1,0:T(8,128)(2,1)}, u32[]{:S(2)}, u32[]{:S(2)}) collective-permute-start(bf16[32,128,128]{2,1,0:T(8,128)(2,1)} %collective-permute-done.19.refs_20_), channel_id=1, source_target_pairs={{0,8},{8,0},{1,9},{9,1},{2,10},{10,2},{3,11},{11,3},{4,12},{12,4},... | collective-permute-start | bytes 3145736 | tf_op jit(solution)/shard_map/ppermute | solution.py:37
  90.7 1.0 copy-done.5
  91.7 9.3 %collective-permute-done.12.refs_12_ = bf16[32,128,128]{2,1,0:T(8,128)(2,1)} collective-permute-done((bf16[32,128,128]{2,1,0:T(8,128)(2,1)}, bf16[32,128,128]{2,1,0:T(8,128)(2,1)}, u32[]{:S(2)}, u32[]{:S(2)}) %collective-permute-start.12) | collective-permute-done | bytes 1048608 | tf_op jit(solution)/shard_map/ppermute | solution.py:37
  101.0 1.3 collective-permute-start.24
  102.3 5.4 %copy.9 = bf16[16,8,128,128]{3,2,1,0:T(8,128)(2,1)} copy(bf16[16,8,128,128]{3,1,2,0:T(8,128)(2,1)} %bitcast.48) | data formatting | bytes 8388608
  108.1 3.7 %copy.12 = bf16[8,8,128,128]{3,2,1,0:T(8,128)(2,1)} copy(bf16[8,8,128,128]{3,1,2,0:T(8,128)(2,1)} %bitcast.49) | data formatting | bytes 4194304
  111.9 0.6 collective-permute-start.18
  112.5 2.7 %collective-permute-done.24.refs_25_ = bf16[32,128,128]{2,1,0:T(8,128)(2,1)} collective-permute-done((bf16[32,128,128]{2,1,0:T(8,128)(2,1)}, bf16[32,128,128]{2,1,0:T(8,128)(2,1)}, u32[]{:S(2)}, u32[]{:S(2)}) %collective-permute-start.24) | collective-permute-done | bytes 1048608 | tf_op jit(solution)/shard_map/ppermute | solution.py:32
  115.3 2.6 %collective-permute-start.11 = (bf16[32,128,128]{2,1,0:T(8,128)(2,1)}, bf16[32,128,128]{2,1,0:T(8,128)(2,1)S(1)}, u32[]{:S(2)}, u32[]{:S(2)}) collective-permute-start(bf16[32,128,128]{2,1,0:T(8,128)(2,1)} %collective-permute-done.9.refs_9_), channel_id=1, source_target_pairs={{0,8},{8,0},{1,9},{9,1},{2,10},{10,2},{3,11},{11,3},{4,12},{12,4},... | collective-permute-start | bytes 3145736 | tf_op jit(solution)/shard_map/ppermute | solution.py:37
  117.9 0.5 collective-permute-start.26
  118.4 1.2 copy-done.2
  119.7 1.2 copy-done.4
  120.9 1.2 copy-done.6
  122.1 24.1 %early_product.1.refs_6_ = f32[64,128,128]{2,1,0:T(8,128)S(1)} custom-call(s32[1280]{0:T(1024)S(1)} %get-tuple-element.29.refs_0_, s32[1280]{0:T(1024)S(1)} %get-tuple-element.30.refs_1_, bf16[128,128,128]{2,1,0:T(8,128)(2,1)S(1)} %bitcast.42, bf16[32,128,128]{2,1,0:T(8,128)(2,1)S(1)} %bitcast.45, bf16[32,128,128]{2,1,0:T(8,128)(2,1)S(1)} %bitcast.47, ...), custom_call_target="tpu_custom_call" | custom-call | flops 16106127360 | bytes 18874368 | tf_op jit(solution)/shard_map/early_product/pallas_call | solution.py:162
  146.3 2.0 %copy-done.7 = f32[64,128,128]{2,1,0:T(8,128)} copy-done((f32[64,128,128]{2,1,0:T(8,128)}, f32[64,128,128]{2,1,0:T(8,128)S(1)}, u32[]{:S(2)}) %copy-start.7) | copy-done | bytes 4194328
  148.4 1.0 copy-done.13
  150.3 33.2 %late_product.1 = (bf16[64,128,128]{2,1,0:T(8,128)(2,1)}, f32[16,128]{1,0:T(8,128)S(1)}) custom-call(s32[768]{0:T(1024)S(1)} %get-tuple-element.31.refs_0_, s32[768]{0:T(1024)S(1)} %get-tuple-element.32.refs_1_, s32[256]{0:T(256)S(1)} %get-tuple-element.33.refs_2_, s32[256]{0:T(256)S(1)} %get-tuple-element.28.refs_3_, s32[256]{0:T(256)S(1)} %get-tuple-element.27.refs_4_, ...), custom_call_target="tpu_custom_call" | custom-call | flops 9663676416 | bytes 41943040 | tf_op jit(solution)/shard_map/late_product/pallas_call | solution.py:181
  183.5 0.7 all_to_all.6
  184.2 5.0 %all-to-all-start = ((f32[128,1,16]{2,1,0:T(1,128)}), f32[128,1,16]{2,1,0:T(1,128)S(1)}, u32[]{:S(2)}, u32[]{:S(2)}) async-start(f32[128,1,16]{2,1,0:T(1,128)} %bitcast.18), calls=%async_computation | async-start | bytes 131072 | tf_op jit(solution)/shard_map/all_to_all | solution.py:247
  189.2 4.2 %reshape.216 = bf16[1,1,64,16384]{3,2,1,0:T(8,128)(2,1)} reshape(bf16[64,128,128]{2,1,0:T(8,128)(2,1)} %get-tuple-element.4) | data formatting | bytes 4194304 | tf_op jit(solution)/shard_map/reshape | solution.py:248
  193.4 5.7 %all-to-all-done = f32[128,1,16]{2,1,0:T(1,128)S(1)} async-done(((f32[128,1,16]{2,1,0:T(1,128)}), f32[128,1,16]{2,1,0:T(1,128)S(1)}, u32[]{:S(2)}, u32[]{:S(2)}) %all-to-all-start) | async-done | bytes 8224 | tf_op jit(solution)/shard_map/all_to_all | solution.py:247
  199.1 0.7 reduce_sum.9
  (83 shorter events, 3.1 us)
Async XLA Ops:
  2.3 31.3 %copy-start.9 = (s32[1,1,8,2,256]{4,3,2,1,0:T(2,128)S(1)}, s32[1,1,8,2,256]{4,3,2,1,0:T(2,128)}, u32[]{:S(2)}) copy-start(s32[1,1,8,2,256]{4,3,2,1,0:T(2,128)} %param.9) | copy-start | bytes 49156
  2.3 74.9 %copy-start.8 = (s32[1,1,16,16,3]{3,2,4,1,0:T(8,128)S(1)}, s32[1,1,16,16,3]{3,2,4,1,0:T(8,128)}, u32[]{:S(2)}) copy-start(s32[1,1,16,16,3]{3,2,4,1,0:T(8,128)} %param.10) | copy-start | bytes 9220
  2.6 15.4 %collective-permute-start = (bf16[32,128,128]{2,1,0:T(8,128)(2,1)S(1)}, bf16[32,128,128]{2,1,0:T(8,128)(2,1)S(1)}, u32[]{:S(2)}, u32[]{:S(2)}) collective-permute-start(bf16[32,128,128]{2,1,0:T(8,128)(2,1)S(1)} %bitcast.43), channel_id=1, source_target_pairs={{0,1},{1,2},{2,3},{3,0},{8,11},{9,8},{10,9},{11,10},{4,5},{5,6},{6... | collective-permute-start | bytes 3145736 | tf_op jit(solution)/shard_map/ppermute | solution.py:32
  6.2 25.3 %collective-permute-start.6 = (bf16[32,128,128]{2,1,0:T(8,128)(2,1)S(1)}, bf16[32,128,128]{2,1,0:T(8,128)(2,1)}, u32[]{:S(2)}, u32[]{:S(2)}) collective-permute-start(bf16[32,128,128]{2,1,0:T(8,128)(2,1)S(1)} %bitcast.44), channel_id=1, source_target_pairs={{0,4},{4,0},{1,5},{5,1},{2,6},{6,2},{3,7},{7,3},{8,12},{12,8},{9,1... | collective-permute-start | bytes 3145736 | tf_op jit(solution)/shard_map/ppermute | solution.py:37
  8.1 23.5 %collective-permute-start.1 = (bf16[32,128,128]{2,1,0:T(8,128)(2,1)S(1)}, bf16[32,128,128]{2,1,0:T(8,128)(2,1)S(1)}, u32[]{:S(2)}, u32[]{:S(2)}) collective-permute-start(bf16[32,128,128]{2,1,0:T(8,128)(2,1)S(1)} %bitcast.46), channel_id=1, source_target_pairs={{0,1},{1,2},{2,3},{3,0},{8,11},{9,8},{10,9},{11,10},{4,5},{5,6},{6... | collective-permute-start | bytes 3145736 | tf_op jit(solution)/shard_map/ppermute | solution.py:32
  8.6 23.9 %collective-permute-start.15 = (bf16[32,128,128]{2,1,0:T(8,128)(2,1)}, bf16[32,128,128]{2,1,0:T(8,128)(2,1)S(1)}, u32[]{:S(2)}, u32[]{:S(2)}) collective-permute-start(bf16[32,128,128]{2,1,0:T(8,128)(2,1)} %bitcast.17.refs_14_), channel_id=1, source_target_pairs={{0,32},{32,64},{64,96},{96,0},{8,104},{40,8},{72,40},{104,72},{1,3... | collective-permute-start | bytes 3145736 | tf_op jit(solution)/shard_map/ppermute | solution.py:32
  11.1 26.4 %collective-permute-start.21 = (bf16[32,128,128]{2,1,0:T(8,128)(2,1)}, bf16[32,128,128]{2,1,0:T(8,128)(2,1)}, u32[]{:S(2)}, u32[]{:S(2)}) collective-permute-start(bf16[32,128,128]{2,1,0:T(8,128)(2,1)} %bitcast.17.refs_14_), channel_id=1, source_target_pairs={{0,20},{4,16},{16,4},{20,0},{1,21},{5,17},{17,5},{21,1},{2,22},{6,... | collective-permute-start | bytes 3145736 | tf_op jit(solution)/shard_map/ppermute | solution.py:37
  18.0 19.6 %collective-permute-start.14 = (bf16[32,128,128]{2,1,0:T(8,128)(2,1)}, bf16[32,128,128]{2,1,0:T(8,128)(2,1)}, u32[]{:S(2)}, u32[]{:S(2)}) collective-permute-start(bf16[32,128,128]{2,1,0:T(8,128)(2,1)} %bitcast.17.refs_14_), channel_id=1, source_target_pairs={{0,8},{8,0},{1,9},{9,1},{2,10},{10,2},{3,11},{11,3},{4,12},{12,4},... | collective-permute-start | bytes 3145736 | tf_op jit(solution)/shard_map/ppermute | solution.py:37
  31.5 14.0 %collective-permute-start.4 = (bf16[32,128,128]{2,1,0:T(8,128)(2,1)S(1)}, bf16[32,128,128]{2,1,0:T(8,128)(2,1)}, u32[]{:S(2)}, u32[]{:S(2)}) collective-permute-start(bf16[32,128,128]{2,1,0:T(8,128)(2,1)S(1)} %collective-permute-done.refs_5_), channel_id=1, source_target_pairs={{0,1},{1,2},{2,3},{3,0},{8,11},{9,8},{10,9},{11,10},{4,5},{5,6},{6... | collective-permute-start | bytes 3145736 | tf_op jit(solution)/shard_map/ppermute | solution.py:32
  31.6 1.0 copy-start.1
  31.6 16.5 %collective-permute-start.7 = (bf16[32,128,128]{2,1,0:T(8,128)(2,1)}, bf16[32,128,128]{2,1,0:T(8,128)(2,1)}, u32[]{:S(2)}, u32[]{:S(2)}) collective-permute-start(bf16[32,128,128]{2,1,0:T(8,128)(2,1)} %collective-permute-done.6.refs_11_), channel_id=1, source_target_pairs={{0,8},{8,0},{1,9},{9,1},{2,10},{10,2},{3,11},{11,3},{4,12},{12,4},... | collective-permute-start | bytes 3145736 | tf_op jit(solution)/shard_map/ppermute | solution.py:37
  32.5 1.0 copy-start.10
  33.5 15.8 %collective-permute-start.2 = (bf16[32,128,128]{2,1,0:T(8,128)(2,1)S(1)}, bf16[32,128,128]{2,1,0:T(8,128)(2,1)}, u32[]{:S(2)}, u32[]{:S(2)}) collective-permute-start(bf16[32,128,128]{2,1,0:T(8,128)(2,1)S(1)} %collective-permute-done.refs_5_), channel_id=1, source_target_pairs={{0,8},{8,0},{1,9},{9,1},{2,10},{10,2},{3,11},{11,3},{4,12},{12,4},... | collective-permute-start | bytes 3145736 | tf_op jit(solution)/shard_map/ppermute | solution.py:37
  37.5 19.2 %collective-permute-start.8 = (bf16[32,128,128]{2,1,0:T(8,128)(2,1)}, bf16[32,128,128]{2,1,0:T(8,128)(2,1)}, u32[]{:S(2)}, u32[]{:S(2)}) collective-permute-start(bf16[32,128,128]{2,1,0:T(8,128)(2,1)} %collective-permute-done.6.refs_11_), channel_id=1, source_target_pairs={{0,1},{1,2},{2,3},{3,0},{8,11},{9,8},{10,9},{11,10},{4,5},{5,6},{6... | collective-permute-start | bytes 3145736 | tf_op jit(solution)/shard_map/ppermute | solution.py:32
  37.5 37.8 %collective-permute-start.22 = (bf16[32,128,128]{2,1,0:T(8,128)(2,1)}, bf16[32,128,128]{2,1,0:T(8,128)(2,1)}, u32[]{:S(2)}, u32[]{:S(2)}) collective-permute-start(bf16[32,128,128]{2,1,0:T(8,128)(2,1)} %collective-permute-done.21.refs_22_), channel_id=1, source_target_pairs={{0,8},{8,0},{1,9},{9,1},{2,10},{10,2},{3,11},{11,3},{4,12},{12,4},... | collective-permute-start | bytes 3145736 | tf_op jit(solution)/shard_map/ppermute | solution.py:37
  45.5 31.6 %collective-permute-start.23 = (bf16[32,128,128]{2,1,0:T(8,128)(2,1)}, bf16[32,128,128]{2,1,0:T(8,128)(2,1)}, u32[]{:S(2)}, u32[]{:S(2)}) collective-permute-start(bf16[32,128,128]{2,1,0:T(8,128)(2,1)} %collective-permute-done.21.refs_22_), channel_id=1, source_target_pairs={{0,32},{32,64},{64,96},{96,0},{8,104},{40,8},{72,40},{104,72},{1,3... | collective-permute-start | bytes 3145736 | tf_op jit(solution)/shard_map/ppermute | solution.py:32
  48.0 3.8 %collective-permute-start.3 = (bf16[32,128,128]{2,1,0:T(8,128)(2,1)}, bf16[32,128,128]{2,1,0:T(8,128)(2,1)S(1)}, u32[]{:S(2)}, u32[]{:S(2)}) collective-permute-start(bf16[32,128,128]{2,1,0:T(8,128)(2,1)} %copy-done.1), channel_id=1, source_target_pairs={{0,8},{8,0},{1,9},{9,1},{2,10},{10,2},{3,11},{11,3},{4,12},{12,4},... | collective-permute-start | bytes 3145736 | tf_op jit(solution)/shard_map/ppermute | solution.py:37
  49.3 22.0 %collective-permute-start.19 = (bf16[32,128,128]{2,1,0:T(8,128)(2,1)}, bf16[32,128,128]{2,1,0:T(8,128)(2,1)}, u32[]{:S(2)}, u32[]{:S(2)}) collective-permute-start(bf16[32,128,128]{2,1,0:T(8,128)(2,1)} %copy-done.10), channel_id=1, source_target_pairs={{0,32},{32,64},{64,96},{96,0},{8,104},{40,8},{72,40},{104,72},{1,3... | collective-permute-start | bytes 3145736 | tf_op jit(solution)/shard_map/ppermute | solution.py:32
  51.8 1.0 copy-start.3
  52.8 33.5 %collective-permute-start.17 = (bf16[32,128,128]{2,1,0:T(8,128)(2,1)}, bf16[32,128,128]{2,1,0:T(8,128)(2,1)S(1)}, u32[]{:S(2)}, u32[]{:S(2)}) collective-permute-start(bf16[32,128,128]{2,1,0:T(8,128)(2,1)} %copy-done.10), channel_id=1, source_target_pairs={{0,8},{8,0},{1,9},{9,1},{2,10},{10,2},{3,11},{11,3},{4,12},{12,4},... | collective-permute-start | bytes 3145736 | tf_op jit(solution)/shard_map/ppermute | solution.py:37
  56.8 25.8 %collective-permute-start.16 = (bf16[32,128,128]{2,1,0:T(8,128)(2,1)}, bf16[32,128,128]{2,1,0:T(8,128)(2,1)S(1)}, u32[]{:S(2)}, u32[]{:S(2)}) collective-permute-start(bf16[32,128,128]{2,1,0:T(8,128)(2,1)} %collective-permute-done.14.refs_15_), channel_id=1, source_target_pairs={{0,32},{32,64},{64,96},{96,0},{8,104},{40,8},{72,40},{104,72},{1,3... | collective-permute-start | bytes 3145736 | tf_op jit(solution)/shard_map/ppermute | solution.py:32
  71.3 19.4 %collective-permute-start.5 = (bf16[32,128,128]{2,1,0:T(8,128)(2,1)}, bf16[32,128,128]{2,1,0:T(8,128)(2,1)S(1)}, u32[]{:S(2)}, u32[]{:S(2)}) collective-permute-start(bf16[32,128,128]{2,1,0:T(8,128)(2,1)} %collective-permute-done.4.refs_9_), channel_id=1, source_target_pairs={{0,8},{8,0},{1,9},{9,1},{2,10},{10,2},{3,11},{11,3},{4,12},{12,4},... | collective-permute-start | bytes 3145736 | tf_op jit(solution)/shard_map/ppermute | solution.py:37
  75.4 25.7 %collective-permute-start.12 = (bf16[32,128,128]{2,1,0:T(8,128)(2,1)}, bf16[32,128,128]{2,1,0:T(8,128)(2,1)}, u32[]{:S(2)}, u32[]{:S(2)}) collective-permute-start(bf16[32,128,128]{2,1,0:T(8,128)(2,1)} %collective-permute-done.4.refs_9_), channel_id=1, source_target_pairs={{0,4},{4,0},{1,5},{5,1},{2,6},{6,2},{3,7},{7,3},{8,12},{12,8},{9,1... | collective-permute-start | bytes 3145736 | tf_op jit(solution)/shard_map/ppermute | solution.py:37
  77.2 25.1 %collective-permute-start.9 = (bf16[32,128,128]{2,1,0:T(8,128)(2,1)}, bf16[32,128,128]{2,1,0:T(8,128)(2,1)}, u32[]{:S(2)}, u32[]{:S(2)}) collective-permute-start(bf16[32,128,128]{2,1,0:T(8,128)(2,1)} %collective-permute-done.7.refs_12_), channel_id=1, source_target_pairs={{0,1},{1,2},{2,3},{3,0},{8,11},{9,8},{10,9},{11,10},{4,5},{5,6},{6... | collective-permute-start | bytes 3145736 | tf_op jit(solution)/shard_map/ppermute | solution.py:32
  82.5 19.8 %copy-start.12 = (bf16[32,128,128]{2,1,0:T(8,128)(2,1)}, bf16[32,128,128]{2,1,0:T(8,128)(2,1)S(1)}, u32[]{:S(2)}) copy-start(bf16[32,128,128]{2,1,0:T(8,128)(2,1)S(1)} %collective-permute-done.16.refs_17_) | copy-start | bytes 3145732
  82.5 29.9 %collective-permute-start.27 = (bf16[32,128,128]{2,1,0:T(8,128)(2,1)}, bf16[32,128,128]{2,1,0:T(8,128)(2,1)}, u32[]{:S(2)}, u32[]{:S(2)}) collective-permute-start(bf16[32,128,128]{2,1,0:T(8,128)(2,1)} %collective-permute-done.19.refs_20_), channel_id=1, source_target_pairs={{0,20},{4,16},{16,4},{20,0},{1,21},{5,17},{17,5},{21,1},{2,22},{6,... | collective-permute-start | bytes 3145736 | tf_op jit(solution)/shard_map/ppermute | solution.py:37
  86.3 16.0 %copy-start.11 = (bf16[32,128,128]{2,1,0:T(8,128)(2,1)}, bf16[32,128,128]{2,1,0:T(8,128)(2,1)S(1)}, u32[]{:S(2)}) copy-start(bf16[32,128,128]{2,1,0:T(8,128)(2,1)S(1)} %collective-permute-done.17.refs_18_) | copy-start | bytes 3145732
  86.3 31.6 %collective-permute-start.20 = (bf16[32,128,128]{2,1,0:T(8,128)(2,1)}, bf16[32,128,128]{2,1,0:T(8,128)(2,1)}, u32[]{:S(2)}, u32[]{:S(2)}) collective-permute-start(bf16[32,128,128]{2,1,0:T(8,128)(2,1)} %collective-permute-done.19.refs_20_), channel_id=1, source_target_pairs={{0,8},{8,0},{1,9},{9,1},{2,10},{10,2},{3,11},{11,3},{4,12},{12,4},... | collective-permute-start | bytes 3145736 | tf_op jit(solution)/shard_map/ppermute | solution.py:37
  90.7 1.0 copy-start.5
  91.7 20.2 %collective-permute-start.10 = (bf16[32,128,128]{2,1,0:T(8,128)(2,1)}, bf16[32,128,128]{2,1,0:T(8,128)(2,1)}, u32[]{:S(2)}, u32[]{:S(2)}) collective-permute-start(bf16[32,128,128]{2,1,0:T(8,128)(2,1)} %collective-permute-done.8.refs_8_), channel_id=1, source_target_pairs={{0,8},{8,0},{1,9},{9,1},{2,10},{10,2},{3,11},{11,3},{4,12},{12,4},... | collective-permute-start | bytes 3145736 | tf_op jit(solution)/shard_map/ppermute | solution.py:37
  101.0 14.3 %collective-permute-start.24 = (bf16[32,128,128]{2,1,0:T(8,128)(2,1)}, bf16[32,128,128]{2,1,0:T(8,128)(2,1)}, u32[]{:S(2)}, u32[]{:S(2)}) collective-permute-start(bf16[32,128,128]{2,1,0:T(8,128)(2,1)} %collective-permute-done.22.refs_23_), channel_id=1, source_target_pairs={{0,32},{32,64},{64,96},{96,0},{8,104},{40,8},{72,40},{104,72},{1,3... | collective-permute-start | bytes 3145736 | tf_op jit(solution)/shard_map/ppermute | solution.py:32
  102.3 15.6 %collective-permute-start.25 = (bf16[32,128,128]{2,1,0:T(8,128)(2,1)}, bf16[32,128,128]{2,1,0:T(8,128)(2,1)}, u32[]{:S(2)}, u32[]{:S(2)}) collective-permute-start(bf16[32,128,128]{2,1,0:T(8,128)(2,1)} %collective-permute-done.23.refs_24_), channel_id=1, source_target_pairs={{0,8},{8,0},{1,9},{9,1},{2,10},{10,2},{3,11},{11,3},{4,12},{12,4},... | collective-permute-start | bytes 3145736 | tf_op jit(solution)/shard_map/ppermute | solution.py:37
  108.1 10.3 %copy-start = (bf16[16,8,128,128]{3,2,1,0:T(8,128)(2,1)S(1)}, bf16[16,8,128,128]{3,2,1,0:T(8,128)(2,1)}, u32[]{:S(2)}) copy-start(bf16[16,8,128,128]{3,2,1,0:T(8,128)(2,1)} %copy.9) | copy-start | bytes 12582916
  111.9 36.4 %collective-permute-start.18 = (bf16[32,128,128]{2,1,0:T(8,128)(2,1)}, bf16[32,128,128]{2,1,0:T(8,128)(2,1)S(1)}, u32[]{:S(2)}, u32[]{:S(2)}) collective-permute-start(bf16[32,128,128]{2,1,0:T(8,128)(2,1)} %copy-done.12), channel_id=1, source_target_pairs={{0,8},{8,0},{1,9},{9,1},{2,10},{10,2},{3,11},{11,3},{4,12},{12,4},... | collective-permute-start | bytes 3145736 | tf_op jit(solution)/shard_map/ppermute | solution.py:37
  112.4 35.9 %collective-permute-start.13 = (bf16[32,128,128]{2,1,0:T(8,128)(2,1)}, bf16[32,128,128]{2,1,0:T(8,128)(2,1)S(1)}, u32[]{:S(2)}, u32[]{:S(2)}) collective-permute-start(bf16[32,128,128]{2,1,0:T(8,128)(2,1)} %collective-permute-done.12.refs_12_), channel_id=1, source_target_pairs={{0,8},{8,0},{1,9},{9,1},{2,10},{10,2},{3,11},{11,3},{4,12},{12,4},... | collective-permute-start | bytes 3145736 | tf_op jit(solution)/shard_map/ppermute | solution.py:37
  115.3 33.0 %collective-permute-start.11 = (bf16[32,128,128]{2,1,0:T(8,128)(2,1)}, bf16[32,128,128]{2,1,0:T(8,128)(2,1)S(1)}, u32[]{:S(2)}, u32[]{:S(2)}) collective-permute-start(bf16[32,128,128]{2,1,0:T(8,128)(2,1)} %collective-permute-done.9.refs_9_), channel_id=1, source_target_pairs={{0,8},{8,0},{1,9},{9,1},{2,10},{10,2},{3,11},{11,3},{4,12},{12,4},... | collective-permute-start | bytes 3145736 | tf_op jit(solution)/shard_map/ppermute | solution.py:37
  117.9 30.4 %collective-permute-start.28 = (bf16[32,128,128]{2,1,0:T(8,128)(2,1)}, bf16[32,128,128]{2,1,0:T(8,128)(2,1)S(1)}, u32[]{:S(2)}, u32[]{:S(2)}) collective-permute-start(bf16[32,128,128]{2,1,0:T(8,128)(2,1)} %collective-permute-done.27.refs_28_), channel_id=1, source_target_pairs={{0,8},{8,0},{1,9},{9,1},{2,10},{10,2},{3,11},{11,3},{4,12},{12,4},... | collective-permute-start | bytes 3145736 | tf_op jit(solution)/shard_map/ppermute | solution.py:37
  117.9 30.4 %collective-permute-start.26 = (bf16[32,128,128]{2,1,0:T(8,128)(2,1)}, bf16[32,128,128]{2,1,0:T(8,128)(2,1)S(1)}, u32[]{:S(2)}, u32[]{:S(2)}) collective-permute-start(bf16[32,128,128]{2,1,0:T(8,128)(2,1)} %collective-permute-done.24.refs_25_), channel_id=1, source_target_pairs={{0,8},{8,0},{1,9},{9,1},{2,10},{10,2},{3,11},{11,3},{4,12},{12,4},... | collective-permute-start | bytes 3145736 | tf_op jit(solution)/shard_map/ppermute | solution.py:37
  118.4 1.2 copy-start.2
  119.7 1.2 copy-start.4
  120.9 1.2 copy-start.6
  146.3 2.0 %copy-start.7 = (f32[64,128,128]{2,1,0:T(8,128)}, f32[64,128,128]{2,1,0:T(8,128)S(1)}, u32[]{:S(2)}) copy-start(f32[64,128,128]{2,1,0:T(8,128)S(1)} %early_product.1.refs_6_) | copy-start | bytes 12582916
  148.3 1.0 copy-start.13
  148.3 1.4 copy-start.14
  148.3 1.7 copy-start.15
  148.3 2.0 copy-start.16
  184.2 14.9 %all-to-all-start = ((f32[128,1,16]{2,1,0:T(1,128)}), f32[128,1,16]{2,1,0:T(1,128)S(1)}, u32[]{:S(2)}, u32[]{:S(2)}) async-start(f32[128,1,16]{2,1,0:T(1,128)} %bitcast.18), calls=%async_computation | async-start | bytes 131072 | tf_op jit(solution)/shard_map/all_to_all | solution.py:247

commit v2 on v1

v2 whole, which is shorter than its diff:
```python
import jax
import jax.numpy as jnp
from jax import lax
from jax.experimental import pallas as pl
from jax.experimental.pallas import tpu as pltpu
from jax.sharding import Mesh
from jax.sharding import PartitionSpec as P

BS = 128
A_TILES = 128
B_TILES = 64
C_TILES = 64
KSTEP = 4
SLOT = 16
NBAS = 32
OWNERS = 16
HALF = 32
UNROLL = 16
TASKS = 8
ROWS = ("x", "zh", "core")
BLK = ("zl", "y")
MIB = 1 << 20
VMEM = 60 * MIB


def around(value, axis):
    pairs = []
    for core in range(2):
        for place in range(4):
            to = (place + 1) % 4 if core == 0 else (place + 3) % 4
            if axis == "x":
                pairs.append((place * 2 + core, to * 2 + core))
            else:
                pairs.append((core * 4 + place, core * 4 + to))
    return lax.ppermute(value, ("x", "core") if axis == "x" else ("core", axis), pairs)


def across(value, axes):
    count = 2 ** len(axes)
    return lax.ppermute(value, axes, [(i, count - 1 - i) for i in range(count)])


def swapped(value):
    return across(value, ("core",))


def half_of(share, core):
    return lax.dynamic_slice_in_dim(share, core * HALF, HALF, 0)


def gate(values, deps=()):
    count = len(values)
    return pl.pallas_call(
        lambda *refs: None,
        out_shape=tuple(jax.ShapeDtypeStruct(value.shape, value.dtype) for value in values),
        in_specs=[hbm()] * (count + len(deps)),
        out_specs=(hbm(),) * count,
        input_output_aliases={i: i for i in range(count)},
        compiler_params=pltpu.CompilerParams(vmem_limit_bytes=VMEM),
        name="gate",
    )(*values, *deps)


def slot_of(pair, hop, half, core):
    rel = half ^ core
    place = jnp.where(hop == ahead_of(core), 2 + rel, 5 - rel)
    return pair * 8 + jnp.where(hop == 0, rel, jnp.where(hop == 2, 6 + rel, place))


def ahead_of(core):
    return jnp.where(core == 0, 3, 1)


def tile_sum(c, share, a_ref, w_ref, left_ref, right_ref):
    total = None
    for k in range(0, KSTEP, 2):
        at = share * (C_TILES * KSTEP) + c * KSTEP + k
        lhs = jnp.concatenate([a_ref[left_ref[at]], a_ref[left_ref[at + 1]]], axis=1)
        rhs = jnp.concatenate([w_ref[right_ref[at]], w_ref[right_ref[at + 1]]], axis=0)
        term = jnp.dot(lhs, rhs, preferred_element_type=jnp.float32)
        total = term if total is None else total + term
    return total


def sums(sizes, count, first, refs, outs, last, square=None):
    left_ref, right_ref, a_hbm, pieces, acc_hbm, a_ref, w_ref, sum_ref, sems, others = refs
    tiles = pltpu.make_async_copy(a_hbm, a_ref.at[pl.ds(0, A_TILES)], sems.at[0])
    needs, at = [[] for _ in range(count)], 0
    for i, (size, piece) in enumerate(zip(sizes, pieces)):
        needs[at // B_TILES].append(pltpu.make_async_copy(piece, w_ref.at[pl.ds(at, size)], sems.at[2 + i]))
        at += size
    needs[0].append(tiles)
    if not first:
        needs[0].append(pltpu.make_async_copy(acc_hbm, sum_ref, sems.at[1]))
    for need in needs:
        for copy in need:
            copy.start()
    for copy in others:
        copy.start()
    a_ref[A_TILES] = jnp.zeros((BS, BS), jnp.bfloat16)
    if square is not None:
        needs[-1].append(square)
    for share in range(count):
        for copy in needs[share]:
            copy.wait()

        def some(g, carry, share=share):
            for u in range(UNROLL):
                c = g * UNROLL + u
                total = tile_sum(c, share, a_ref, w_ref, left_ref, right_ref)
                if share > 0 or not first:
                    total = total + sum_ref[c]
                if share < count - 1:
                    sum_ref[c] = total
                else:
                    outs(c, total)
            if share == count - 1:
                last(g)
            return carry

        lax.fori_loop(0, C_TILES // UNROLL, some, 0)


def product_kernel(sizes, count, first, left_ref, right_ref, a_hbm, *rest):
    pieces = rest[: len(sizes)]
    rest = list(rest[len(sizes) :])
    acc_hbm = None if first else rest.pop(0)
    out_hbm, out_ref, a_ref, w_ref, sum_ref, sems, out_sems = rest

    def put(part):
        span = pl.ds(part * UNROLL, UNROLL)
        return pltpu.make_async_copy(out_ref.at[span], out_hbm.at[span], out_sems.at[part])

    def outs(c, total):
        out_ref[c] = total

    refs = (left_ref, right_ref, a_hbm, pieces, acc_hbm, a_ref, w_ref, sum_ref, sems, [])
    sums(sizes, count, first, refs, outs, lambda g: put(g).start())
    for part in range(C_TILES // UNROLL):
        put(part).wait()


def final_kernel(sizes, count, slab_sizes, left_ref, right_ref, who_ref, tile_ref, row_ref, col_ref, a_hbm, *rest):
    pieces, rest = rest[: len(sizes)], rest[len(sizes) :]
    acc_hbm, sq_hbm = rest[:2]
    slabs, rest = rest[2 : 2 + len(slab_sizes)], rest[2 + len(slab_sizes) :]
    out_hbm, grid_ref, a_ref, w_ref, sum_ref, sq_ref, p_ref, b_ref, sems, out_sems, slab_sems = rest

    def bring(source, slot):
        return pltpu.make_async_copy(source, b_ref.at[pl.ds(slot * NBAS, NBAS)], slab_sems.at[slot])

    square = pltpu.make_async_copy(sq_hbm, sq_ref, out_sems.at[C_TILES // UNROLL])
    others, slot = [square], 0
    for size, slab in zip(slab_sizes, slabs):
        for part in range(size // NBAS):
            others.append(bring(slab.at[pl.ds(part * NBAS, NBAS)], slot))
            slot += 1

    def put(part):
        span = pl.ds(part * UNROLL, UNROLL)
        return pltpu.make_async_copy(p_ref.at[span], out_hbm.at[span], out_sems.at[part])

    def outs(c, total):
        p_ref[c] = (3.0 * sq_ref[c].astype(jnp.float32) - 2.0 * total).astype(jnp.bfloat16)

    p_ref[C_TILES] = jnp.zeros((BS, BS), jnp.bfloat16)
    refs = (left_ref, right_ref, a_hbm, pieces, acc_hbm, a_ref, w_ref, sum_ref, sems, others)
    sums(sizes, count, False, refs, outs, lambda g: put(g).start(), square)

    def one(slot, carry):
        s = who_ref[slot]
        live = jnp.int32(0)
        for t in range(SLOT):
            live = live + jnp.where(tile_ref[s * SLOT + t] < C_TILES, 1, 0)
        bring(slabs[0].at[pl.ds(0, NBAS)], slot).wait()

        def some(g, total):
            for t in range(TASKS):
                at = s * SLOT + g * TASKS + t
                spread = jnp.dot(p_ref[tile_ref[at]], b_ref[col_ref[at]], preferred_element_type=jnp.float32)
                total = total + b_ref[row_ref[at]].astype(jnp.float32) * spread
            return total

        total = lax.fori_loop(0, (live + TASKS - 1) // TASKS, some, jnp.zeros((BS, BS), jnp.float32))
        grid_ref[pl.ds(s, 1), :] = jnp.sum(total, axis=0, keepdims=True)
        return carry

    lax.fori_loop(0, OWNERS, one, 0)
    for part in range(C_TILES // UNROLL):
        put(part).wait()


def smem():
    return pl.BlockSpec(memory_space=pltpu.SMEM)


def hbm():
    return pl.BlockSpec(memory_space=pl.ANY)


def vmem():
    return pl.BlockSpec(memory_space=pltpu.VMEM)


def product(plan, a_tiles, pieces, acc=None):
    sizes = [piece.shape[0] for piece in pieces]
    count = sum(sizes) // B_TILES
    operands = [*plan, a_tiles, *pieces] + ([] if acc is None else [acc])
    return pl.pallas_call(
        lambda *refs: product_kernel(sizes, count, acc is None, *refs),
        out_shape=jax.ShapeDtypeStruct((C_TILES, BS, BS), jnp.float32),
        in_specs=[smem(), smem()] + [hbm()] * (len(operands) - 2),
        out_specs=hbm(),
        scratch_shapes=[
            pltpu.VMEM((C_TILES, BS, BS), jnp.float32),
            pltpu.VMEM((A_TILES + 1, BS, BS), jnp.bfloat16),
            pltpu.VMEM((sum(sizes), BS, BS), jnp.bfloat16),
            pltpu.VMEM((C_TILES, BS, BS), jnp.float32),
            pltpu.SemaphoreType.DMA((2 + len(pieces),)),
            pltpu.SemaphoreType.DMA((C_TILES // UNROLL,)),
        ],
        compiler_params=pltpu.CompilerParams(vmem_limit_bytes=VMEM),
        cost_estimate=pl.CostEstimate(
            flops=4 * count * C_TILES * KSTEP * BS**3, bytes_accessed=(12 + 2 * count) * MIB, transcendentals=0
        ),
        name="product",
    )(*operands)


def final(plan, who, tile, row, col, a_tiles, pieces, acc, square, slabs):
    sizes = [piece.shape[0] for piece in pieces]
    count = sum(sizes) // B_TILES
    slab_sizes = [slab.shape[0] for slab in slabs]
    return pl.pallas_call(
        lambda *refs: final_kernel(sizes, count, slab_sizes, *refs),
        out_shape=(
            jax.ShapeDtypeStruct((C_TILES, BS, BS), jnp.bfloat16),
            jax.ShapeDtypeStruct((OWNERS, BS), jnp.float32),
        ),
        in_specs=[smem()] * 6 + [hbm()] * (3 + len(pieces) + len(slabs)),
        out_specs=(hbm(), vmem()),
        scratch_shapes=[
            pltpu.VMEM((A_TILES + 1, BS, BS), jnp.bfloat16),
            pltpu.VMEM((sum(sizes), BS, BS), jnp.bfloat16),
            pltpu.VMEM((C_TILES, BS, BS), jnp.float32),
            pltpu.VMEM((C_TILES, BS, BS), jnp.bfloat16),
            pltpu.VMEM((C_TILES + 1, BS, BS), jnp.bfloat16),
            pltpu.VMEM((OWNERS * NBAS, BS, BS), jnp.bfloat16),
            pltpu.SemaphoreType.DMA((2 + len(pieces),)),
            pltpu.SemaphoreType.DMA((C_TILES // UNROLL + 1,)),
            pltpu.SemaphoreType.DMA((OWNERS,)),
        ],
        compiler_params=pltpu.CompilerParams(vmem_limit_bytes=VMEM),
        cost_estimate=pl.CostEstimate(
            flops=4 * (count * C_TILES * KSTEP + 512) * BS**3, bytes_accessed=40 * MIB, transcendentals=0
        ),
        name="final",
    )(*plan, who, tile, row, col, a_tiles, *pieces, acc, square, *slabs)


def plans(pairs, core, zl, y, shares):
    lefts, rights = [], []
    for at, (pair, hop, turned) in enumerate(shares):
        source = (zl ^ pair) * 4 + ((y + hop) & 3)
        step = ((zl * 4 + y) - source) & 7
        plan = lax.dynamic_index_in_dim(pairs, step, 0, keepdims=False)
        half = (plan[1] // HALF) ^ core ^ turned
        lefts.append(jnp.where(plan[0] < 0, A_TILES, plan[0]))
        rights.append(at * B_TILES + half * HALF + plan[1] % HALF)
    return jnp.concatenate(lefts), jnp.concatenate(rights)


def body(p2_tiles, window_tiles, square_tiles, pairs, tasks, basis):
    core = lax.axis_index("core")
    x, zh, zl, y = (lax.axis_index(name) for name in ("x", "zh", "zl", "y"))
    slab = basis[0]
    share = window_tiles[0]
    mine = half_of(share, core).reshape(HALF, BS, BS)
    other = half_of(share, 1 - core).reshape(HALF, BS, BS)
    a_tiles = p2_tiles[0, 0].reshape(A_TILES, BS, BS)
    square = square_tiles[0, 0].reshape(C_TILES, BS, BS)
    ahead = ahead_of(core)
    stages = (
        ((0, 0, 0), (0, ahead, 0), (0, 4 - ahead, 1), (0, 2, 0), (1, 0, 0)),
        ((1, ahead, 0),),
        ((1, 4 - ahead, 1), (1, 2, 0)),
    )
    plan = [plans(pairs[0, 0], core, zl, y, stage) for stage in stages]
    task = tasks[0, 0]
    owner = jnp.arange(OWNERS, dtype=jnp.int32)[:, None]
    place = slot_of((owner // 2 % 2) ^ zh, (owner // 4 - x) & 3, owner % 2, core) * NBAS
    tile = jnp.where(task[..., 0] < 0, C_TILES, task[..., 0]).reshape(-1)
    row = (place + jnp.clip(task[..., 1], 0, NBAS - 1)).reshape(-1)
    col = (place + jnp.clip(task[..., 2], 0, NBAS - 1)).reshape(-1)

    slots = jnp.arange(16, dtype=jnp.int32)[:, None]
    who = jnp.sum(jnp.where(place // NBAS == slots.T, owner, 0), axis=0)
    link, zz = ("zl",), ("zh", "zl")
    near_a, bnear_a = around(mine, "y"), around(slab, "x")
    pair, bpair = across(mine, link), across(slab, zz)
    bother = swapped(slab)
    near_b, bnear_b = around(other, "y"), around(bother, "x")
    work = [tile, row, col, who, *[index for both in plan for index in both], a_tiles]
    near_a, near_b, pair, bpair, bnear_a, bnear_b = gate([near_a, near_b, pair, bpair, bnear_a, bnear_b], work)
    far, bfar = around(near_a, "y"), around(bnear_a, "x")
    spair, sbpair = swapped(pair), swapped(bpair)
    snear_a, snear_b = swapped(near_a), swapped(near_b)
    both, bboth = jnp.concatenate([pair, spair]), jnp.concatenate([bpair, sbpair])
    both, bboth, far, bfar, bnear_a, bnear_b = gate(
        [both, bboth, far, bfar, bnear_a, bnear_b], [snear_a, snear_b, square]
    )
    pnear, bpnear = around(both, "y"), around(bboth, "x")
    pfar, bpfar = across(far, link), across(bfar, zz)
    sfar = swapped(far)
    acc = product(plan[0], a_tiles, [mine, other, near_a, near_b, snear_a, snear_b, far, sfar, both])
    sbnear_a, sbnear_b, sbfar = swapped(bnear_a), swapped(bnear_b), swapped(bfar)
    pnear, bpnear, pfar, bpfar = gate([pnear, bpnear, pfar, bpfar], [acc, sbnear_a, sbnear_b, sbfar])
    spnear, spfar, sbpfar, sbpnear = swapped(pnear), swapped(pfar), swapped(bpfar), swapped(bpnear)
    acc = product(plan[1], a_tiles, [pnear], acc)
    tables = [
        slab, bother, bnear_a, bnear_b, sbnear_a, sbnear_b, bfar, sbfar, bboth, bpnear, sbpnear, bpfar, sbpfar,
    ]
    pure, grid = final(plan[2], who, tile, row, col, a_tiles, [spnear, pfar, spfar], acc, square, tables)
    parts = lax.all_to_all(grid.reshape(128, 16), ROWS + BLK, split_axis=0, concat_axis=0, tiled=True)
    return pure.reshape(1, 1, C_TILES, BS * BS), jnp.sum(parts, axis=0)


def solution(mesh):
    split = Mesh(mesh.devices.reshape(4, 2, 2, 2, 4), ("x", "zh", "core", "zl", "y"))
    return jax.shard_map(
        body,
        mesh=split,
        in_specs=(
            P(ROWS, BLK, None, None),
            P(BLK, None, None),
            P(ROWS, BLK, None, None),
            P(ROWS, BLK, None, None, None),
            P(ROWS, BLK, None, None, None),
            P(ROWS, None, None, None),
        ),
        out_specs=(P(ROWS, BLK, None, None), P(ROWS + BLK)),
        check_vma=False,
    )
```

time: 200 us -> 144 us (0.72)
  waiting for transfers between devices: 65.6 us -> 27.4 us
  starting transfers between devices: 47.3 us -> 31.7 us
  other arithmetic: 0.86 us -> 10.4 us
  Pallas kernels: 57.3 us -> 50 us
  local copies, waits for them, and re-layouts: 27.8 us -> 22.8 us
    ppermute x10 -> x8, waiting for transfers between devices: 34.4 us -> 3.79 us  [around(): lax.ppermute(value, ('x', 'core') if axis == 'x' else ('core', axis), pairs)]
    ppermute x19 -> x17, starting transfers between devices: 27.8 us -> 13.7 us  [across(): return lax.ppermute(value, axes, [(i, count - 1 - i) for i in range(count)])]
    ppermute x19 -> x17, waiting for transfers between devices: 25.5 us -> 17.9 us  [across(): return lax.ppermute(value, axes, [(i, count - 1 - i) for i in range(count)])]
    pallas_call x2 -> x6, Pallas kernels: 57.3 us -> 50 us  [the longest x2 27.4 us: product(): pl.pallas_call(lambda *refs: product_kernel(sizes, count, acc is None, *r...]
    unnamed x39 -> x33, local copies, waits for them, and re-layouts: 22.6 us -> 16.9 us
    concatenate x0 -> x2, other arithmetic: none -> 5.47 us  [the longest x1 2.74 us: body(): jnp.concatenate([bpair, sbpair])]
    ppermute x10 -> x8, starting transfers between devices: 14.4 us -> 13.6 us  [around(): lax.ppermute(value, ('x', 'core') if axis == 'x' else ('core', axis), pairs)]
  transfers between devices with their start and end apart: 30 -> 26, of which waited for: 11 -> 13; matrix products, arithmetic and copies ran while one was open for 7% -> 19% of each run, Pallas kernels for 12% -> 19%
where the time goes in v2:
time: 144 us; the launch traced here: 143 us
  Pallas kernels  50 us (35%)
  starting transfers between devices  31.7 us (22%)
  waiting for transfers between devices  27.4 us (19%)
  local copies, waits for them, and re-layouts  22.8 us (16%)
  other arithmetic  10.4 us (7%)
    pallas_call x2, Pallas kernels, product(): pl.pallas_call(lambda *refs: product_kernel(sizes, count, acc is None, *r...  27.4 us
    pallas_call x1, Pallas kernels, final(): pl.pallas_call(lambda *refs: final_kernel(sizes, count, slab_sizes, *refs...  22.5 us
    ppermute x17, waiting for transfers between devices, across(): return lax.ppermute(value, axes, [(i, count - 1 - i) for i in range(count)])  17.9 us
    unnamed x33, local copies, waits for them, and re-layouts  16.9 us
    ppermute x17, starting transfers between devices, across(): return lax.ppermute(value, axes, [(i, count - 1 - i) for i in range(count)])  13.7 us
    ppermute x8, starting transfers between devices, around(): lax.ppermute(value, ('x', 'core') if axis == 'x' else ('core', axis), pairs)  13.6 us
    all_to_all x1, waiting for transfers between devices, body(): lax.all_to_all(grid.reshape(128, 16), ROWS + BLK, split_axis=0, concat_ax...  5.69 us
    all_to_all x1, starting transfers between devices, body(): lax.all_to_all(grid.reshape(128, 16), ROWS + BLK, split_axis=0, concat_ax...  4.35 us
  transfers between devices with their start and end apart: 26, of which 13 were waited for; matrix products, arithmetic and copies ran while one was open for 19% of the time, Pallas kernels for 19%

profile of v2, /device:TPU:1, one launch (start us, length us, event | category | flops | bytes accessed | tf_op | source)
XLA Modules:
  0.0 143.1 jit_solution(5973987108964058048)
XLA Ops:
  0.6 1.5 %collective-permute-start.5 = (bf16[32,128,128]{2,1,0:T(8,128)(2,1)}, bf16[32,128,128]{2,1,0:T(8,128)(2,1)}, u32[]{:S(2)}, u32[]{:S(2)}) collective-permute-start(bf16[32,128,128]{2,1,0:T(8,128)(2,1)} %bitcast.66), channel_id=1, source_target_pairs={{0,8},{8,0},{1,9},{9,1},{2,10},{10,2},{3,11},{11,3},{4,12},{12,4},... | collective-permute-start | bytes 3145736 | tf_op jit(solution)/shard_map/ppermute | solution.py:40
  2.1 2.6 %collective-permute-start.4 = (bf16[32,128,128]{2,1,0:T(8,128)(2,1)}, bf16[32,128,128]{2,1,0:T(8,128)(2,1)S(1)}, u32[]{:S(2)}, u32[]{:S(2)}) collective-permute-start(bf16[32,128,128]{2,1,0:T(8,128)(2,1)} %bitcast.67), channel_id=1, source_target_pairs={{0,32},{32,64},{64,96},{96,0},{8,104},{40,8},{72,40},{104,72},{1,3... | collective-permute-start | bytes 3145736 | tf_op jit(solution)/shard_map/ppermute | solution.py:35
  4.7 3.8 %collective-permute-start.3 = (bf16[32,128,128]{2,1,0:T(8,128)(2,1)}, bf16[32,128,128]{2,1,0:T(8,128)(2,1)}, u32[]{:S(2)}, u32[]{:S(2)}) collective-permute-start(bf16[32,128,128]{2,1,0:T(8,128)(2,1)} %bitcast.68), channel_id=1, source_target_pairs={{0,20},{4,16},{16,4},{20,0},{1,21},{5,17},{17,5},{21,1},{2,22},{6,... | collective-permute-start | bytes 3145736 | tf_op jit(solution)/shard_map/ppermute | solution.py:40
  8.5 1.7 %dynamic-slice_bitcast_fusion = (bf16[4,8,128,128]{3,1,2,0:T(8,128)(2,1)S(1)}, bf16[4,8,128,128]{3,1,2,0:T(8,128)(2,1)S(1)}) fusion(bf16[1,64,16384]{2,1,0:T(8,128)(2,1)} %param.7, s32[]{:T(128)S(6)} %select_n.242, s32[]{:T(128)S(6)} %select_n.241), kind=kLoop, calls=%fused_computation.2 | loop fusion | bytes 4194312
  10.2 1.2 copy.27
  11.4 2.7 %collective-permute-start = (bf16[32,128,128]{2,1,0:T(8,128)(2,1)}, bf16[32,128,128]{2,1,0:T(8,128)(2,1)S(1)}, u32[]{:S(2)}, u32[]{:S(2)}) collective-permute-start(bf16[32,128,128]{2,1,0:T(8,128)(2,1)} %bitcast.28.refs_3_), channel_id=1, source_target_pairs={{0,1},{1,2},{2,3},{3,0},{8,11},{9,8},{10,9},{11,10},{4,5},{5,6},{6... | collective-permute-start | bytes 3145736 | tf_op jit(solution)/shard_map/ppermute | solution.py:35
  14.3 0.6 fusion.1
  14.9 0.6 pad_add_fusion.1.refs_15_.refs_1_
  15.6 1.2 copy.28
  16.8 0.6 compare_select_fusion.6
  17.4 0.6 pad_add_fusion.refs_14_.refs_0_
  18.5 1.6 %collective-permute-start.6 = (bf16[32,128,128]{2,1,0:T(8,128)(2,1)}, bf16[32,128,128]{2,1,0:T(8,128)(2,1)S(1)}, u32[]{:S(2)}, u32[]{:S(2)}) collective-permute-start(bf16[32,128,128]{2,1,0:T(8,128)(2,1)} %collective-permute-done.5.refs_13_), channel_id=1, source_target_pairs={{0,32},{32,64},{64,96},{96,0},{8,104},{40,8},{72,40},{104,72},{1,3... | collective-permute-start | bytes 3145736 | tf_op jit(solution)/shard_map/ppermute | solution.py:35
  20.5 5.4 %copy.26 = bf16[16,8,128,128]{3,2,1,0:T(8,128)(2,1)} copy(bf16[16,8,128,128]{3,1,2,0:T(8,128)(2,1)} %bitcast.47) | data formatting | bytes 8388608
  25.9 0.6 select_reduce_fusion.refs_9_.refs_2_
  26.5 0.6 constant_dynamic-update-slice_fusion
  27.1 0.6 fusion.17
  27.7 4.1 %collective-permute-done.3.refs_3_ = bf16[32,128,128]{2,1,0:T(8,128)(2,1)} collective-permute-done((bf16[32,128,128]{2,1,0:T(8,128)(2,1)}, bf16[32,128,128]{2,1,0:T(8,128)(2,1)}, u32[]{:S(2)}, u32[]{:S(2)}) %collective-permute-start.3) | collective-permute-done | bytes 1048608 | tf_op jit(solution)/shard_map/ppermute | solution.py:40
  31.8 4.9 %collective-permute-done.2.refs_2_ = bf16[32,128,128]{2,1,0:T(8,128)(2,1)} collective-permute-done((bf16[32,128,128]{2,1,0:T(8,128)(2,1)}, bf16[32,128,128]{2,1,0:T(8,128)(2,1)}, u32[]{:S(2)}, u32[]{:S(2)}) %collective-permute-start.2) | collective-permute-done | bytes 1048608 | tf_op jit(solution)/shard_map/ppermute | solution.py:40
  36.7 0.7 collective-permute-done.1.refs_1_
  37.7 0.7 copy-done.2
  38.4 0.9 collective-permute-start.7
  39.3 1.5 %collective-permute-start.10 = (bf16[32,128,128]{2,1,0:T(8,128)(2,1)}, bf16[32,128,128]{2,1,0:T(8,128)(2,1)S(1)}, u32[]{:S(2)}, u32[]{:S(2)}) collective-permute-start(bf16[32,128,128]{2,1,0:T(8,128)(2,1)} %get-tuple-element.23.refs_4_), channel_id=1, source_target_pairs={{0,32},{32,64},{64,96},{96,0},{8,104},{40,8},{72,40},{104,72},{1,3... | collective-permute-start | bytes 3145736 | tf_op jit(solution)/shard_map/ppermute | solution.py:35
  40.8 0.5 collective-permute-start.12
  41.8 2.6 %collective-permute-start.9 = (bf16[32,128,128]{2,1,0:T(8,128)(2,1)}, bf16[32,128,128]{2,1,0:T(8,128)(2,1)}, u32[]{:S(2)}, u32[]{:S(2)}) collective-permute-start(bf16[32,128,128]{2,1,0:T(8,128)(2,1)} %get-tuple-element.22.refs_5_), channel_id=1, source_target_pairs={{0,1},{1,2},{2,3},{3,0},{8,11},{9,8},{10,9},{11,10},{4,5},{5,6},{6... | collective-permute-start | bytes 3145736 | tf_op jit(solution)/shard_map/ppermute | solution.py:35
  44.4 3.5 %copy.29 = bf16[8,8,128,128]{3,2,1,0:T(8,128)(2,1)} copy(bf16[8,8,128,128]{3,1,2,0:T(8,128)(2,1)} %bitcast.48) | data formatting | bytes 4194304
  47.9 2.7 %pad_maximum_fusion.refs_0_ = bf16[64,128,128]{2,1,0:T(8,128)(2,1)} fusion(bf16[32,128,128]{2,1,0:T(8,128)(2,1)S(1)} %collective-permute-done.7, bf16[32,128,128]{2,1,0:T(8,128)(2,1)} %get-tuple-element.20), kind=kLoop, calls=%fused_computation | loop fusion | flops 1048576 | bytes 4194304 | tf_op jit(solution)/shard_map/concatenate | solution.py:308
  50.6 2.7 %pad_maximum_fusion.1.refs_1_ = bf16[64,128,128]{2,1,0:T(8,128)(2,1)} fusion(bf16[32,128,128]{2,1,0:T(8,128)(2,1)S(1)} %collective-permute-done.8, bf16[32,128,128]{2,1,0:T(8,128)(2,1)} %get-tuple-element.21), kind=kLoop, calls=%fused_computation.1 | loop fusion | flops 1048576 | bytes 4194304 | tf_op jit(solution)/shard_map/concatenate | solution.py:308
  53.6 2.9 %collective-permute-done.9.refs_2_ = bf16[32,128,128]{2,1,0:T(8,128)(2,1)} collective-permute-done((bf16[32,128,128]{2,1,0:T(8,128)(2,1)}, bf16[32,128,128]{2,1,0:T(8,128)(2,1)}, u32[]{:S(2)}, u32[]{:S(2)}) %collective-permute-start.9) | collective-permute-done | bytes 1048608 | tf_op jit(solution)/shard_map/ppermute | solution.py:35
  56.5 2.2 %collective-permute-start.18 = (bf16[32,128,128]{2,1,0:T(8,128)(2,1)}, bf16[32,128,128]{2,1,0:T(8,128)(2,1)S(1)}, u32[]{:S(2)}, u32[]{:S(2)}) collective-permute-start(bf16[32,128,128]{2,1,0:T(8,128)(2,1)} %get-tuple-element.30.refs_14_), channel_id=1, source_target_pairs={{0,8},{8,0},{1,9},{9,1},{2,10},{10,2},{3,11},{11,3},{4,12},{12,4},... | collective-permute-start | bytes 3145736 | tf_op jit(solution)/shard_map/ppermute | solution.py:40
  59.1 1.3 collective-permute-start.13
  60.5 0.8 collective-permute-start.14
  61.7 1.7 %collective-permute-start.15 = (bf16[32,128,128]{2,1,0:T(8,128)(2,1)}, bf16[32,128,128]{2,1,0:T(8,128)(2,1)}, u32[]{:S(2)}, u32[]{:S(2)}) collective-permute-start(bf16[32,128,128]{2,1,0:T(8,128)(2,1)} %get-tuple-element.28.refs_9_), channel_id=1, source_target_pairs={{0,4},{4,0},{1,5},{5,1},{2,6},{6,2},{3,7},{7,3},{8,12},{12,8},{9,1... | collective-permute-start | bytes 3145736 | tf_op jit(solution)/shard_map/ppermute | solution.py:40
  63.5 0.7 collective-permute-start.20
  64.5 18.8 %product.2.refs_4_ = f32[64,128,128]{2,1,0:T(8,128)} custom-call(s32[1280]{0:T(1024)} %copy-done.11, s32[1280]{0:T(1024)} %copy-done.10, bf16[128,128,128]{2,1,0:T(8,128)(2,1)} %bitcast.42, bf16[32,128,128]{2,1,0:T(8,128)(2,1)} %bitcast.28.refs_3_, bf16[32,128,128]{2,1,0:T(8,128)(2,1)} %bitcast.31.refs_4_, bf16[32,128,128]{2,1,0:T(8,128)(2,1)} %get-tuple-element.22.refs_5_, ...), custom_call_target="tpu_custom_call" | custom-call | flops 10737418240 | bytes 23068672 | tf_op jit(solution)/shard_map/product/pallas_call | solution.py:209
  83.3 3.7 %collective-permute-done.15.refs_2_ = bf16[32,128,128]{2,1,0:T(8,128)(2,1)} collective-permute-done((bf16[32,128,128]{2,1,0:T(8,128)(2,1)}, bf16[32,128,128]{2,1,0:T(8,128)(2,1)}, u32[]{:S(2)}, u32[]{:S(2)}) %collective-permute-start.15) | collective-permute-done | bytes 1048608 | tf_op jit(solution)/shard_map/ppermute | solution.py:40
  87.0 3.2 %collective-permute-done.16.refs_3_ = bf16[32,128,128]{2,1,0:T(8,128)(2,1)} collective-permute-done((bf16[32,128,128]{2,1,0:T(8,128)(2,1)}, bf16[32,128,128]{2,1,0:T(8,128)(2,1)}, u32[]{:S(2)}, u32[]{:S(2)}) %collective-permute-start.16) | collective-permute-done | bytes 1048608 | tf_op jit(solution)/shard_map/ppermute | solution.py:40
  90.2 1.3 copy-done
  91.5 1.2 collective-permute-start.21
  93.2 8.6 %product.3.refs_10_ = f32[64,128,128]{2,1,0:T(8,128)} custom-call(s32[256]{0:T(256)} %get-tuple-element.68.refs_12_.refs_0_, s32[256]{0:T(256)} %get-tuple-element.66.refs_13_.refs_1_, bf16[128,128,128]{2,1,0:T(8,128)(2,1)} %bitcast.43, bf16[64,128,128]{2,1,0:T(8,128)(2,1)} %get-tuple-element.32.refs_3_, f32[64,128,128]{2,1,0:T(8,128)} %product.2.refs_4_), custom_call_target="tpu_custom_call" | custom-call | flops 2147483648 | bytes 14680064 | tf_op jit(solution)/shard_map/product/pallas_call | solution.py:209
  101.9 0.8 collective-permute-done.22.refs_9_
  102.8 0.8 copy-done.13
  103.6 0.7 copy-done.12
  104.3 22.5 %final.1 = (bf16[64,128,128]{2,1,0:T(8,128)(2,1)}, f32[16,128]{1,0:T(8,128)}) custom-call(s32[512]{0:T(512)} %pad_add_fusion.refs_14_.refs_0_, s32[512]{0:T(512)} %pad_add_fusion.1.refs_15_.refs_1_, s32[16]{0:T(128)} %select_reduce_fusion.refs_9_.refs_2_, s32[256]{0:T(256)} %get-tuple-element.69.refs_6_.refs_3_, s32[256]{0:T(256)} %get-tuple-element.62.refs_7_.refs_4_, ...), custom_call_target="tpu_custom_call" | custom-call | flops 8589934592 | bytes 41943040 | tf_op jit(solution)/shard_map/final/pallas_call | solution.py:234
  126.8 1.4 all_to_all.6
  128.2 4.4 %all-to-all-start = ((f32[128,1,16]{2,1,0:T(1,128)}), f32[128,1,16]{2,1,0:T(1,128)S(1)}, u32[]{:S(2)}, u32[]{:S(2)}) async-start(f32[128,1,16]{2,1,0:T(1,128)} %bitcast.18), calls=%async_computation | async-start | bytes 131072 | tf_op jit(solution)/shard_map/all_to_all | solution.py:324
  132.6 4.2 %reshape.250 = bf16[1,1,64,16384]{3,2,1,0:T(8,128)(2,1)} reshape(bf16[64,128,128]{2,1,0:T(8,128)(2,1)} %get-tuple-element.36) | data formatting | bytes 4194304 | tf_op jit(solution)/shard_map/reshape | solution.py:325
  136.8 5.7 %all-to-all-done = f32[128,1,16]{2,1,0:T(1,128)S(1)} async-done(((f32[128,1,16]{2,1,0:T(1,128)}), f32[128,1,16]{2,1,0:T(1,128)S(1)}, u32[]{:S(2)}, u32[]{:S(2)}) %all-to-all-start) | async-done | bytes 8224 | tf_op jit(solution)/shard_map/all_to_all | solution.py:324
  142.4 0.7 reduce_sum.19
  (75 shorter events, 4.2 us)
Async XLA Ops:
  0.6 17.4 %collective-permute-start.5 = (bf16[32,128,128]{2,1,0:T(8,128)(2,1)}, bf16[32,128,128]{2,1,0:T(8,128)(2,1)}, u32[]{:S(2)}, u32[]{:S(2)}) collective-permute-start(bf16[32,128,128]{2,1,0:T(8,128)(2,1)} %bitcast.66), channel_id=1, source_target_pairs={{0,8},{8,0},{1,9},{9,1},{2,10},{10,2},{3,11},{11,3},{4,12},{12,4},... | collective-permute-start | bytes 3145736 | tf_op jit(solution)/shard_map/ppermute | solution.py:40
  2.1 16.4 %collective-permute-start.4 = (bf16[32,128,128]{2,1,0:T(8,128)(2,1)}, bf16[32,128,128]{2,1,0:T(8,128)(2,1)S(1)}, u32[]{:S(2)}, u32[]{:S(2)}) collective-permute-start(bf16[32,128,128]{2,1,0:T(8,128)(2,1)} %bitcast.67), channel_id=1, source_target_pairs={{0,32},{32,64},{64,96},{96,0},{8,104},{40,8},{72,40},{104,72},{1,3... | collective-permute-start | bytes 3145736 | tf_op jit(solution)/shard_map/ppermute | solution.py:35
  4.7 27.1 %collective-permute-start.3 = (bf16[32,128,128]{2,1,0:T(8,128)(2,1)}, bf16[32,128,128]{2,1,0:T(8,128)(2,1)}, u32[]{:S(2)}, u32[]{:S(2)}) collective-permute-start(bf16[32,128,128]{2,1,0:T(8,128)(2,1)} %bitcast.68), channel_id=1, source_target_pairs={{0,20},{4,16},{16,4},{20,0},{1,21},{5,17},{17,5},{21,1},{2,22},{6,... | collective-permute-start | bytes 3145736 | tf_op jit(solution)/shard_map/ppermute | solution.py:40
  10.1 4.0 %copy-start.8 = (s32[1,1,16,16,3]{3,2,4,1,0:T(8,128)S(1)}, s32[1,1,16,16,3]{3,2,4,1,0:T(8,128)}, u32[]{:S(2)}) copy-start(s32[1,1,16,16,3]{3,2,4,1,0:T(8,128)} %param.10) | copy-start | bytes 9220
  10.2 4.0 %copy-start.9 = (s32[1,1,8,2,256]{4,3,2,1,0:T(2,128)S(1)}, s32[1,1,8,2,256]{4,3,2,1,0:T(2,128)}, u32[]{:S(2)}) copy-start(s32[1,1,8,2,256]{4,3,2,1,0:T(2,128)} %param.9) | copy-start | bytes 49156
  11.4 25.3 %collective-permute-start.2 = (bf16[32,128,128]{2,1,0:T(8,128)(2,1)}, bf16[32,128,128]{2,1,0:T(8,128)(2,1)}, u32[]{:S(2)}, u32[]{:S(2)}) collective-permute-start(bf16[32,128,128]{2,1,0:T(8,128)(2,1)} %bitcast.28.refs_3_), channel_id=1, source_target_pairs={{0,4},{4,0},{1,5},{5,1},{2,6},{6,2},{3,7},{7,3},{8,12},{12,8},{9,1... | collective-permute-start | bytes 3145736 | tf_op jit(solution)/shard_map/ppermute | solution.py:40
  11.4 25.3 %collective-permute-start = (bf16[32,128,128]{2,1,0:T(8,128)(2,1)}, bf16[32,128,128]{2,1,0:T(8,128)(2,1)S(1)}, u32[]{:S(2)}, u32[]{:S(2)}) collective-permute-start(bf16[32,128,128]{2,1,0:T(8,128)(2,1)} %bitcast.28.refs_3_), channel_id=1, source_target_pairs={{0,1},{1,2},{2,3},{3,0},{8,11},{9,8},{10,9},{11,10},{4,5},{5,6},{6... | collective-permute-start | bytes 3145736 | tf_op jit(solution)/shard_map/ppermute | solution.py:35
  14.9 11.0 %copy-start.10 = (s32[1280]{0:T(1024)}, s32[1280]{0:T(1024)S(1)}, u32[]{:S(2)}) copy-start(s32[1280]{0:T(1024)S(1)} %get-tuple-element.63.refs_11_.refs_1_) | copy-start | bytes 15364
  18.0 19.4 %collective-permute-start.1 = (bf16[32,128,128]{2,1,0:T(8,128)(2,1)}, bf16[32,128,128]{2,1,0:T(8,128)(2,1)}, u32[]{:S(2)}, u32[]{:S(2)}) collective-permute-start(bf16[32,128,128]{2,1,0:T(8,128)(2,1)} %bitcast.31.refs_4_), channel_id=1, source_target_pairs={{0,1},{1,2},{2,3},{3,0},{8,11},{9,8},{10,9},{11,10},{4,5},{5,6},{6... | collective-permute-start | bytes 3145736 | tf_op jit(solution)/shard_map/ppermute | solution.py:35
  18.5 7.4 %copy-start.1 = (bf16[32,128,128]{2,1,0:T(8,128)(2,1)}, bf16[32,128,128]{2,1,0:T(8,128)(2,1)S(1)}, u32[]{:S(2)}) copy-start(bf16[32,128,128]{2,1,0:T(8,128)(2,1)S(1)} %collective-permute-done.4.refs_4_) | copy-start | bytes 3145732
  18.5 18.9 %collective-permute-start.6 = (bf16[32,128,128]{2,1,0:T(8,128)(2,1)}, bf16[32,128,128]{2,1,0:T(8,128)(2,1)S(1)}, u32[]{:S(2)}, u32[]{:S(2)}) collective-permute-start(bf16[32,128,128]{2,1,0:T(8,128)(2,1)} %collective-permute-done.5.refs_13_), channel_id=1, source_target_pairs={{0,32},{32,64},{64,96},{96,0},{8,104},{40,8},{72,40},{104,72},{1,3... | collective-permute-start | bytes 3145736 | tf_op jit(solution)/shard_map/ppermute | solution.py:35
  27.1 10.3 %copy-start.11 = (s32[1280]{0:T(1024)}, s32[1280]{0:T(1024)S(1)}, u32[]{:S(2)}) copy-start(s32[1280]{0:T(1024)S(1)} %get-tuple-element.67.refs_10_.refs_0_) | copy-start | bytes 15364
  36.7 1.0 copy-start.3
  37.4 1.0 copy-start.2
  38.4 3.4 %collective-permute-start.7 = (bf16[32,128,128]{2,1,0:T(8,128)(2,1)}, bf16[32,128,128]{2,1,0:T(8,128)(2,1)S(1)}, u32[]{:S(2)}, u32[]{:S(2)}) collective-permute-start(bf16[32,128,128]{2,1,0:T(8,128)(2,1)} %get-tuple-element.20), channel_id=1, source_target_pairs={{0,8},{8,0},{1,9},{9,1},{2,10},{10,2},{3,11},{11,3},{4,12},{12,4},... | collective-permute-start | bytes 3145736 | tf_op jit(solution)/shard_map/ppermute | solution.py:40
  39.3 11.3 %collective-permute-start.8 = (bf16[32,128,128]{2,1,0:T(8,128)(2,1)}, bf16[32,128,128]{2,1,0:T(8,128)(2,1)S(1)}, u32[]{:S(2)}, u32[]{:S(2)}) collective-permute-start(bf16[32,128,128]{2,1,0:T(8,128)(2,1)} %get-tuple-element.21), channel_id=1, source_target_pairs={{0,8},{8,0},{1,9},{9,1},{2,10},{10,2},{3,11},{11,3},{4,12},{12,4},... | collective-permute-start | bytes 3145736 | tf_op jit(solution)/shard_map/ppermute | solution.py:40
  39.3 14.3 %collective-permute-start.10 = (bf16[32,128,128]{2,1,0:T(8,128)(2,1)}, bf16[32,128,128]{2,1,0:T(8,128)(2,1)S(1)}, u32[]{:S(2)}, u32[]{:S(2)}) collective-permute-start(bf16[32,128,128]{2,1,0:T(8,128)(2,1)} %get-tuple-element.23.refs_4_), channel_id=1, source_target_pairs={{0,32},{32,64},{64,96},{96,0},{8,104},{40,8},{72,40},{104,72},{1,3... | collective-permute-start | bytes 3145736 | tf_op jit(solution)/shard_map/ppermute | solution.py:35
  40.8 12.8 %collective-permute-start.12 = (bf16[32,128,128]{2,1,0:T(8,128)(2,1)}, bf16[32,128,128]{2,1,0:T(8,128)(2,1)S(1)}, u32[]{:S(2)}, u32[]{:S(2)}) collective-permute-start(bf16[32,128,128]{2,1,0:T(8,128)(2,1)} %get-tuple-element.25.refs_6_), channel_id=1, source_target_pairs={{0,8},{8,0},{1,9},{9,1},{2,10},{10,2},{3,11},{11,3},{4,12},{12,4},... | collective-permute-start | bytes 3145736 | tf_op jit(solution)/shard_map/ppermute | solution.py:40
  41.3 12.3 %collective-permute-start.11 = (bf16[32,128,128]{2,1,0:T(8,128)(2,1)}, bf16[32,128,128]{2,1,0:T(8,128)(2,1)S(1)}, u32[]{:S(2)}, u32[]{:S(2)}) collective-permute-start(bf16[32,128,128]{2,1,0:T(8,128)(2,1)} %get-tuple-element.22.refs_5_), channel_id=1, source_target_pairs={{0,8},{8,0},{1,9},{9,1},{2,10},{10,2},{3,11},{11,3},{4,12},{12,4},... | collective-permute-start | bytes 3145736 | tf_op jit(solution)/shard_map/ppermute | solution.py:40
  41.8 14.6 %collective-permute-start.9 = (bf16[32,128,128]{2,1,0:T(8,128)(2,1)}, bf16[32,128,128]{2,1,0:T(8,128)(2,1)}, u32[]{:S(2)}, u32[]{:S(2)}) collective-permute-start(bf16[32,128,128]{2,1,0:T(8,128)(2,1)} %get-tuple-element.22.refs_5_), channel_id=1, source_target_pairs={{0,1},{1,2},{2,3},{3,0},{8,11},{9,8},{10,9},{11,10},{4,5},{5,6},{6... | collective-permute-start | bytes 3145736 | tf_op jit(solution)/shard_map/ppermute | solution.py:35
  53.6 2.9 %copy-start.6 = (bf16[32,128,128]{2,1,0:T(8,128)(2,1)}, bf16[32,128,128]{2,1,0:T(8,128)(2,1)S(1)}, u32[]{:S(2)}) copy-start(bf16[32,128,128]{2,1,0:T(8,128)(2,1)S(1)} %collective-permute-done.10.refs_3_) | copy-start | bytes 3145732
  53.6 2.9 %copy-start.4 = (bf16[32,128,128]{2,1,0:T(8,128)(2,1)}, bf16[32,128,128]{2,1,0:T(8,128)(2,1)S(1)}, u32[]{:S(2)}) copy-start(bf16[32,128,128]{2,1,0:T(8,128)(2,1)S(1)} %collective-permute-done.12.refs_7_.refs_8_) | copy-start | bytes 3145732
  53.6 2.9 %copy-start.5 = (bf16[32,128,128]{2,1,0:T(8,128)(2,1)}, bf16[32,128,128]{2,1,0:T(8,128)(2,1)S(1)}, u32[]{:S(2)}) copy-start(bf16[32,128,128]{2,1,0:T(8,128)(2,1)S(1)} %collective-permute-done.11.refs_6_.refs_7_) | copy-start | bytes 3145732
  56.5 5.2 %collective-permute-start.18 = (bf16[32,128,128]{2,1,0:T(8,128)(2,1)}, bf16[32,128,128]{2,1,0:T(8,128)(2,1)S(1)}, u32[]{:S(2)}, u32[]{:S(2)}) collective-permute-start(bf16[32,128,128]{2,1,0:T(8,128)(2,1)} %get-tuple-element.30.refs_14_), channel_id=1, source_target_pairs={{0,8},{8,0},{1,9},{9,1},{2,10},{10,2},{3,11},{11,3},{4,12},{12,4},... | collective-permute-start | bytes 3145736 | tf_op jit(solution)/shard_map/ppermute | solution.py:40
  58.6 4.8 %collective-permute-start.19 = (bf16[32,128,128]{2,1,0:T(8,128)(2,1)}, bf16[32,128,128]{2,1,0:T(8,128)(2,1)}, u32[]{:S(2)}, u32[]{:S(2)}) collective-permute-start(bf16[32,128,128]{2,1,0:T(8,128)(2,1)} %get-tuple-element.31.refs_15_), channel_id=1, source_target_pairs={{0,8},{8,0},{1,9},{9,1},{2,10},{10,2},{3,11},{11,3},{4,12},{12,4},... | collective-permute-start | bytes 3145736 | tf_op jit(solution)/shard_map/ppermute | solution.py:40
  58.7 5.5 %collective-permute-start.17 = (bf16[32,128,128]{2,1,0:T(8,128)(2,1)}, bf16[32,128,128]{2,1,0:T(8,128)(2,1)}, u32[]{:S(2)}, u32[]{:S(2)}) collective-permute-start(bf16[32,128,128]{2,1,0:T(8,128)(2,1)} %get-tuple-element.28.refs_9_), channel_id=1, source_target_pairs={{0,8},{8,0},{1,9},{9,1},{2,10},{10,2},{3,11},{11,3},{4,12},{12,4},... | collective-permute-start | bytes 3145736 | tf_op jit(solution)/shard_map/ppermute | solution.py:40
  59.1 31.0 %collective-permute-start.13 = (bf16[64,128,128]{2,1,0:T(8,128)(2,1)}, bf16[64,128,128]{2,1,0:T(8,128)(2,1)S(1)}, u32[]{:S(2)}, u32[]{:S(2)}) collective-permute-start(bf16[64,128,128]{2,1,0:T(8,128)(2,1)} %get-tuple-element.26.refs_11_), channel_id=1, source_target_pairs={{0,1},{1,2},{2,3},{3,0},{8,11},{9,8},{10,9},{11,10},{4,5},{5,6},{6... | collective-permute-start | bytes 6291464 | tf_op jit(solution)/shard_map/ppermute | solution.py:35
  60.5 29.7 %collective-permute-start.14 = (bf16[64,128,128]{2,1,0:T(8,128)(2,1)}, bf16[64,128,128]{2,1,0:T(8,128)(2,1)}, u32[]{:S(2)}, u32[]{:S(2)}) collective-permute-start(bf16[64,128,128]{2,1,0:T(8,128)(2,1)} %get-tuple-element.27.refs_20_), channel_id=1, source_target_pairs={{0,32},{32,64},{64,96},{96,0},{8,104},{40,8},{72,40},{104,72},{1,3... | collective-permute-start | bytes 6291464 | tf_op jit(solution)/shard_map/ppermute | solution.py:35
  61.7 21.6 %copy-start.7 = (bf16[32,128,128]{2,1,0:T(8,128)(2,1)}, bf16[32,128,128]{2,1,0:T(8,128)(2,1)S(1)}, u32[]{:S(2)}) copy-start(bf16[32,128,128]{2,1,0:T(8,128)(2,1)S(1)} %collective-permute-done.18.refs_5_.refs_16_) | copy-start | bytes 3145732
  61.7 25.3 %collective-permute-start.15 = (bf16[32,128,128]{2,1,0:T(8,128)(2,1)}, bf16[32,128,128]{2,1,0:T(8,128)(2,1)}, u32[]{:S(2)}, u32[]{:S(2)}) collective-permute-start(bf16[32,128,128]{2,1,0:T(8,128)(2,1)} %get-tuple-element.28.refs_9_), channel_id=1, source_target_pairs={{0,4},{4,0},{1,5},{5,1},{2,6},{6,2},{3,7},{7,3},{8,12},{12,8},{9,1... | collective-permute-start | bytes 3145736 | tf_op jit(solution)/shard_map/ppermute | solution.py:40
  63.5 23.5 %collective-permute-start.20 = (bf16[32,128,128]{2,1,0:T(8,128)(2,1)}, bf16[32,128,128]{2,1,0:T(8,128)(2,1)}, u32[]{:S(2)}, u32[]{:S(2)}) collective-permute-start(bf16[32,128,128]{2,1,0:T(8,128)(2,1)} %get-tuple-element.29.refs_18_), channel_id=1, source_target_pairs={{0,8},{8,0},{1,9},{9,1},{2,10},{10,2},{3,11},{11,3},{4,12},{12,4},... | collective-permute-start | bytes 3145736 | tf_op jit(solution)/shard_map/ppermute | solution.py:40
  64.3 25.9 %collective-permute-start.16 = (bf16[32,128,128]{2,1,0:T(8,128)(2,1)}, bf16[32,128,128]{2,1,0:T(8,128)(2,1)}, u32[]{:S(2)}, u32[]{:S(2)}) collective-permute-start(bf16[32,128,128]{2,1,0:T(8,128)(2,1)} %get-tuple-element.29.refs_18_), channel_id=1, source_target_pairs={{0,20},{4,16},{16,4},{20,0},{1,21},{5,17},{17,5},{21,1},{2,22},{6,... | collective-permute-start | bytes 3145736 | tf_op jit(solution)/shard_map/ppermute | solution.py:40
  90.2 1.3 copy-start
  91.5 11.3 %collective-permute-start.21 = (bf16[64,128,128]{2,1,0:T(8,128)(2,1)}, bf16[64,128,128]{2,1,0:T(8,128)(2,1)S(1)}, u32[]{:S(2)}, u32[]{:S(2)}) collective-permute-start(bf16[64,128,128]{2,1,0:T(8,128)(2,1)} %get-tuple-element.32.refs_3_), channel_id=1, source_target_pairs={{0,8},{8,0},{1,9},{9,1},{2,10},{10,2},{3,11},{11,3},{4,12},{12,4},... | collective-permute-start | bytes 6291464 | tf_op jit(solution)/shard_map/ppermute | solution.py:40
  92.7 10.1 %collective-permute-start.23 = (bf16[64,128,128]{2,1,0:T(8,128)(2,1)}, bf16[64,128,128]{2,1,0:T(8,128)(2,1)}, u32[]{:S(2)}, u32[]{:S(2)}) collective-permute-start(bf16[64,128,128]{2,1,0:T(8,128)(2,1)} %get-tuple-element.34.refs_21_), channel_id=1, source_target_pairs={{0,8},{8,0},{1,9},{9,1},{2,10},{10,2},{3,11},{11,3},{4,12},{12,4},... | collective-permute-start | bytes 6291464 | tf_op jit(solution)/shard_map/ppermute | solution.py:40
  92.7 10.0 %collective-permute-start.22 = (bf16[32,128,128]{2,1,0:T(8,128)(2,1)}, bf16[32,128,128]{2,1,0:T(8,128)(2,1)S(1)}, u32[]{:S(2)}, u32[]{:S(2)}) collective-permute-start(bf16[32,128,128]{2,1,0:T(8,128)(2,1)} %get-tuple-element.33.refs_8_), channel_id=1, source_target_pairs={{0,8},{8,0},{1,9},{9,1},{2,10},{10,2},{3,11},{11,3},{4,12},{12,4},... | collective-permute-start | bytes 3145736 | tf_op jit(solution)/shard_map/ppermute | solution.py:40
  93.2 9.6 %collective-permute-start.24 = (bf16[32,128,128]{2,1,0:T(8,128)(2,1)}, bf16[32,128,128]{2,1,0:T(8,128)(2,1)}, u32[]{:S(2)}, u32[]{:S(2)}) collective-permute-start(bf16[32,128,128]{2,1,0:T(8,128)(2,1)} %get-tuple-element.35.refs_23_), channel_id=1, source_target_pairs={{0,8},{8,0},{1,9},{9,1},{2,10},{10,2},{3,11},{11,3},{4,12},{12,4},... | collective-permute-start | bytes 3145736 | tf_op jit(solution)/shard_map/ppermute | solution.py:40
  102.7 1.0 copy-start.13
  102.8 1.5 %copy-start.12 = (bf16[64,128,128]{2,1,0:T(8,128)(2,1)}, bf16[64,128,128]{2,1,0:T(8,128)(2,1)S(1)}, u32[]{:S(2)}) copy-start(bf16[64,128,128]{2,1,0:T(8,128)(2,1)S(1)} %collective-permute-done.21.refs_7_) | copy-start | bytes 6291460
  128.2 14.2 %all-to-all-start = ((f32[128,1,16]{2,1,0:T(1,128)}), f32[128,1,16]{2,1,0:T(1,128)S(1)}, u32[]{:S(2)}, u32[]{:S(2)}) async-start(f32[128,1,16]{2,1,0:T(1,128)} %bitcast.18), calls=%async_computation | async-start | bytes 131072 | tf_op jit(solution)/shard_map/all_to_all | solution.py:324

commit v3 on v2

v3 whole, which is shorter than its diff:
```python
import jax
import jax.numpy as jnp
from jax import lax
from jax.experimental import pallas as pl
from jax.experimental.pallas import tpu as pltpu
from jax.sharding import Mesh
from jax.sharding import PartitionSpec as P

BS = 128
A_TILES = 128
B_TILES = 64
C_TILES = 64
KSTEP = 4
SLOT = 16
NBAS = 32
OWNERS = 16
HALF = 32
UNROLL = 16
ROWS = ("x", "zh", "core")
BLK = ("zl", "y")
MIB = 1 << 20


def around(value, axis):
    pairs = []
    for core in range(2):
        for place in range(4):
            to = (place + 1) % 4 if core == 0 else (place + 3) % 4
            if axis == "x":
                pairs.append((place * 2 + core, to * 2 + core))
            else:
                pairs.append((core * 4 + place, core * 4 + to))
    return lax.ppermute(value, ("x", "core") if axis == "x" else ("core", axis), pairs)


def across(value, axes):
    count = 2 ** len(axes)
    return lax.ppermute(value, axes, [(i, count - 1 - i) for i in range(count)])


def swapped(value):
    return across(value, ("core",))


def half_of(share, core):
    return lax.dynamic_slice_in_dim(share, core * HALF, HALF, 0)


def matrices(flat):
    return flat.reshape(flat.shape[0], BS, BS)


def gate(values, deps=()):
    count = len(values)
    return pl.pallas_call(
        lambda *refs: None,
        out_shape=tuple(jax.ShapeDtypeStruct(value.shape, value.dtype) for value in values),
        in_specs=[hbm()] * (count + len(deps)),
        out_specs=(hbm(),) * count,
        input_output_aliases={i: i for i in range(count)},
        compiler_params=pltpu.CompilerParams(vmem_limit_bytes=MIB),
        name="gate",
    )(*values, *deps)


def slot_of(pair, hop, half, core):
    rel = half ^ core
    place = jnp.where(hop == ahead_of(core), 2 + rel, 5 - rel)
    return pair * 8 + jnp.where(hop == 0, rel, jnp.where(hop == 2, 6 + rel, place))


def ahead_of(core):
    return jnp.where(core == 0, 3, 1)


def tile_sum(c, share, a_ref, w_ref, left_ref, right_ref):
    total = None
    for k in range(0, KSTEP, 2):
        at = share * (C_TILES * KSTEP) + c * KSTEP + k
        lhs = jnp.concatenate([a_ref[left_ref[at]], a_ref[left_ref[at + 1]]], axis=1)
        rhs = jnp.concatenate([w_ref[right_ref[at]], w_ref[right_ref[at + 1]]], axis=0)
        term = jnp.dot(lhs, rhs, preferred_element_type=jnp.float32)
        total = term if total is None else total + term
    return total


def sums(sizes, count, refs, start, outs):
    left_ref, right_ref, a_ref, pieces, w_ref, sum_ref, sems = refs
    needs, at = [[] for _ in range(count)], 0
    for i, (size, piece) in enumerate(zip(sizes, pieces)):
        needs[at // B_TILES].append(pltpu.make_async_copy(piece, w_ref.at[pl.ds(at, size)], sems.at[i]))
        at += size
    for need in needs:
        for copy in need:
            copy.start()
    w_ref[count * B_TILES] = jnp.zeros((BS, BS), jnp.bfloat16)
    for share in range(count):
        for copy in needs[share]:
            copy.wait()

        def some(g, carry, share=share):
            for u in range(UNROLL):
                c = g * UNROLL + u
                total = tile_sum(c, share, a_ref, w_ref, left_ref, right_ref)
                before = sum_ref[c] if share > 0 else start(c)
                if before is not None:
                    total = total + before
                if share < count - 1:
                    sum_ref[c] = total
                else:
                    outs(g, u, total)
            return carry

        lax.fori_loop(0, C_TILES // UNROLL, some, 0)


def product_kernel(sizes, count, first, left_ref, right_ref, a_ref, *rest):
    pieces = rest[: len(sizes)]
    rest = list(rest[len(sizes) :])
    acc_ref = None if first else rest.pop(0)
    out_ref, w_ref, sems = rest

    def outs(g, u, total):
        out_ref[g * UNROLL + u] = total

    refs = (left_ref, right_ref, a_ref, pieces, w_ref, out_ref, sems)
    sums(sizes, count, refs, lambda c: None if first else acc_ref[c], outs)


def final_kernel(sizes, count, slab_sizes, left_ref, right_ref, who_ref, tile_ref, row_ref, col_ref, a_ref, *rest):
    pieces, rest = rest[: len(sizes)], rest[len(sizes) :]
    acc_ref, sq_ref = rest[:2]
    slabs, rest = rest[2 : 2 + len(slab_sizes)], rest[2 + len(slab_sizes) :]
    out_hbm, grid_ref, w_ref, sum_ref, p_ref, sems, out_sems = rest

    def put(part):
        span = pl.ds(part * UNROLL, UNROLL)
        return pltpu.make_async_copy(p_ref.at[span], out_hbm.at[span], out_sems.at[part])

    def outs(g, u, total):
        c = g * UNROLL + u
        p_ref[c] = (3.0 * sq_ref[c].astype(jnp.float32) - 2.0 * total).astype(jnp.bfloat16)
        if u == UNROLL - 1:
            put(g).start()

    p_ref[C_TILES] = jnp.zeros((BS, BS), jnp.bfloat16)
    refs = (left_ref, right_ref, a_ref, pieces, w_ref, sum_ref, sems)
    sums(sizes, count, refs, lambda c: acc_ref[c], outs)

    slot = 0
    for size, slab in zip(slab_sizes, slabs):
        base = slot * NBAS
        for _ in range(size // NBAS):
            s = who_ref[slot]
            total = None
            for t in range(SLOT):
                at = s * SLOT + t
                spread = jnp.dot(p_ref[tile_ref[at]], slab[col_ref[at] - base], preferred_element_type=jnp.float32)
                term = slab[row_ref[at] - base].astype(jnp.float32) * spread
                total = term if total is None else total + term
            grid_ref[pl.ds(s, 1), :] = jnp.sum(total, axis=0, keepdims=True)
            slot += 1
    for part in range(C_TILES // UNROLL):
        put(part).wait()


def smem():
    return pl.BlockSpec(memory_space=pltpu.SMEM)


def hbm():
    return pl.BlockSpec(memory_space=pl.ANY)


def vmem():
    return pl.BlockSpec(memory_space=pltpu.VMEM)


def product(plan, a_tiles, pieces, acc=None):
    sizes = [piece.shape[0] for piece in pieces]
    count = sum(sizes) // B_TILES
    operands = [*plan, a_tiles, *pieces] + ([] if acc is None else [acc])
    specs = [smem(), smem(), vmem()] + [hbm()] * len(pieces) + ([] if acc is None else [vmem()])
    return pl.pallas_call(
        lambda *refs: product_kernel(sizes, count, acc is None, *refs),
        out_shape=jax.ShapeDtypeStruct((C_TILES, BS, BS), jnp.float32),
        in_specs=specs,
        out_specs=vmem(),
        scratch_shapes=[
            pltpu.VMEM((sum(sizes) + 1, BS, BS), jnp.bfloat16),
            pltpu.SemaphoreType.DMA((len(pieces),)),
        ],
        compiler_params=pltpu.CompilerParams(vmem_limit_bytes=(2 * count + 3) * MIB),
        cost_estimate=pl.CostEstimate(
            flops=4 * count * C_TILES * KSTEP * BS**3, bytes_accessed=(12 + 2 * count) * MIB, transcendentals=0
        ),
        name="product",
    )(*operands)


def final(plan, who, tile, row, col, a_tiles, pieces, acc, square, slabs):
    sizes = [piece.shape[0] for piece in pieces]
    count = sum(sizes) // B_TILES
    slab_sizes = [slab.shape[0] for slab in slabs]
    return pl.pallas_call(
        lambda *refs: final_kernel(sizes, count, slab_sizes, *refs),
        out_shape=(
            jax.ShapeDtypeStruct((C_TILES, BS, BS), jnp.bfloat16),
            jax.ShapeDtypeStruct((OWNERS, BS), jnp.float32),
        ),
        in_specs=[smem()] * 6 + [vmem()] + [hbm()] * len(pieces) + [vmem()] * (2 + len(slabs)),
        out_specs=(pl.BlockSpec(memory_space=pltpu.HBM), vmem()),
        scratch_shapes=[
            pltpu.VMEM((sum(sizes) + 1, BS, BS), jnp.bfloat16),
            pltpu.VMEM((C_TILES, BS, BS), jnp.float32),
            pltpu.VMEM((C_TILES + 1, BS, BS), jnp.bfloat16),
            pltpu.SemaphoreType.DMA((len(pieces),)),
            pltpu.SemaphoreType.DMA((C_TILES // UNROLL,)),
        ],
        compiler_params=pltpu.CompilerParams(vmem_limit_bytes=18 * MIB),
        cost_estimate=pl.CostEstimate(
            flops=4 * (count * C_TILES * KSTEP + 512) * BS**3, bytes_accessed=40 * MIB, transcendentals=0
        ),
        name="final",
    )(*plan, who, tile, row, col, a_tiles, *pieces, acc, square, *slabs)


def plans(pairs, core, zl, y, shares):
    lefts, rights = [], []
    for at, (pair, hop, turned) in enumerate(shares):
        source = (zl ^ pair) * 4 + ((y + hop) & 3)
        step = ((zl * 4 + y) - source) & 7
        plan = lax.dynamic_index_in_dim(pairs, step, 0, keepdims=False)
        half = (plan[1] // HALF) ^ core ^ turned
        lefts.append(jnp.maximum(plan[0], 0))
        rights.append(jnp.where(plan[0] < 0, len(shares) * B_TILES, at * B_TILES + half * HALF + plan[1] % HALF))
    return jnp.concatenate(lefts), jnp.concatenate(rights)


def body(p2_tiles, window_tiles, square_tiles, pairs, tasks, basis):
    core = lax.axis_index("core")
    x, zh, zl, y = (lax.axis_index(name) for name in ("x", "zh", "zl", "y"))
    slab = basis[0]
    share = window_tiles[0]
    raw_mine, raw_other, slab = gate([half_of(share, core), half_of(share, 1 - core), slab])
    mine, other = matrices(raw_mine), matrices(raw_other)
    a_tiles = p2_tiles[0, 0].reshape(A_TILES, BS, BS)
    square = square_tiles[0, 0].reshape(C_TILES, BS, BS)
    ahead = ahead_of(core)
    stages = (
        ((0, 0, 0), (0, ahead, 0), (0, 4 - ahead, 1), (0, 2, 0), (1, 0, 0)),
        ((1, ahead, 0),),
        ((1, 4 - ahead, 1), (1, 2, 0)),
    )
    plan = [plans(pairs[0, 0], core, zl, y, stage) for stage in stages]
    task = tasks[0, 0]
    owner = jnp.arange(OWNERS, dtype=jnp.int32)[:, None]
    place = slot_of((owner // 2 % 2) ^ zh, (owner // 4 - x) & 3, owner % 2, core) * NBAS
    tile = jnp.where(task[..., 0] < 0, C_TILES, task[..., 0]).reshape(-1)
    row = (place + jnp.clip(task[..., 1], 0, NBAS - 1)).reshape(-1)
    col = (place + jnp.clip(task[..., 2], 0, NBAS - 1)).reshape(-1)

    slots = jnp.arange(16, dtype=jnp.int32)[:, None]
    who = jnp.sum(jnp.where(place // NBAS == slots.T, owner, 0), axis=0)
    link, zz = ("zl",), ("zh", "zl")
    raw_near, bnear_a = around(raw_mine, "y"), around(slab, "x")
    pair, bpair = across(mine, link), across(slab, zz)
    bother = swapped(slab)
    near_b, bnear_b = around(other, "y"), around(bother, "x")
    near_a = matrices(raw_near)
    sbnear_a = swapped(bnear_a)
    work = [tile, row, col, who, *[index for both in plan for index in both], a_tiles, sbnear_a]
    raw_near, near_a, near_b, pair, bpair, bnear_a, bnear_b = gate(
        [raw_near, near_a, near_b, pair, bpair, bnear_a, bnear_b], work
    )
    far, bfar = around(raw_near, "y"), around(bnear_a, "x")
    spair, sbpair = swapped(pair), swapped(bpair)
    snear_a, snear_b = swapped(near_a), swapped(near_b)
    both, bboth = jnp.concatenate([pair, spair]), jnp.concatenate([bpair, sbpair])
    both, bboth, far, bfar, bnear_b = gate([both, bboth, far, bfar, bnear_b], [snear_a, snear_b, square])
    far = matrices(far)
    pnear, bpnear = around(both, "y"), around(bboth, "x")
    pfar, bpfar = across(far, link), across(bfar, zz)
    sfar = swapped(far)
    acc = product(plan[0], a_tiles, [mine, other, near_a, near_b, snear_a, snear_b, far, sfar, both])
    (bnear_b,) = gate([bnear_b], [acc])
    sbnear_b, sbfar = swapped(bnear_b), swapped(bfar)
    pnear, bpnear, pfar, bpfar = gate([pnear, bpnear, pfar, bpfar], [acc, sbnear_b, sbfar])
    spnear, spfar, sbpfar, sbpnear = swapped(pnear), swapped(pfar), swapped(bpfar), swapped(bpnear)
    acc = product(plan[1], a_tiles, [pnear], acc)
    tables = [
        slab, bother, bnear_a, bnear_b, sbnear_a, sbnear_b, bfar, sbfar, bboth, bpnear, sbpnear, bpfar, sbpfar,
    ]
    pure, grid = final(plan[2], who, tile, row, col, a_tiles, [spnear, pfar, spfar], acc, square, tables)
    parts = lax.all_to_all(grid.reshape(128, 16), ROWS + BLK, split_axis=0, concat_axis=0, tiled=True)
    return pure.reshape(1, 1, C_TILES, BS * BS), jnp.sum(parts, axis=0)


def solution(mesh):
    split = Mesh(mesh.devices.reshape(4, 2, 2, 2, 4), ("x", "zh", "core", "zl", "y"))
    return jax.shard_map(
        body,
        mesh=split,
        in_specs=(
            P(ROWS, BLK, None, None),
            P(BLK, None, None),
            P(ROWS, BLK, None, None),
            P(ROWS, BLK, None, None, None),
            P(ROWS, BLK, None, None, None),
            P(ROWS, None, None, None),
        ),
        out_specs=(P(ROWS, BLK, None, None), P(ROWS + BLK)),
        check_vma=False,
    )
```

time: 144 us -> 131 us (0.910)
  waiting for transfers between devices: 27.4 us -> 50 us
  Pallas kernels: 50 us -> 31.2 us
  local copies, waits for them, and re-layouts: 22.8 us -> 14.3 us
  other arithmetic: 10.4 us -> 3.82 us
  starting transfers between devices: 31.7 us -> 29.9 us
    ppermute x8, waiting for transfers between devices: 3.79 us -> 22.7 us  [around(): lax.ppermute(value, ('x', 'core') if axis == 'x' else ('core', axis), pairs)]
    pallas_call x1, Pallas kernels: 22.5 us -> 11.3 us  [final(): pl.pallas_call(lambda *refs: final_kernel(sizes, count, slab_sizes, *refs...]
    pallas_call x2, Pallas kernels: 27.4 us -> 19.8 us  [product(): pl.pallas_call(lambda *refs: product_kernel(sizes, count, acc is None, *r...]
    unnamed x33 -> x17, local copies, waits for them, and re-layouts: 16.9 us -> 9.27 us
    ppermute x17, starting transfers between devices: 13.7 us -> 10.6 us  [across(): return lax.ppermute(value, axes, [(i, count - 1 - i) for i in range(count)])]
    all_to_all x1, waiting for transfers between devices: 5.69 us -> 7.57 us  [body(): lax.all_to_all(grid.reshape(128, 16), ROWS + BLK, split_axis=0, concat_ax...]
    reshape x1, local copies, waits for them, and re-layouts: 4.16 us -> 2.29 us  [body(): return (pure.reshape(1, 1, C_TILES, BS * BS), jnp.sum(parts, axis=0))]
    ppermute x17, waiting for transfers between devices: 17.9 us -> 19.8 us  [across(): return lax.ppermute(value, axes, [(i, count - 1 - i) for i in range(count)])]
  transfers between devices with their start and end apart: 26 -> 26, of which waited for: 13 -> 12; matrix products, arithmetic and copies ran while one was open for 19% -> 10% of each run, Pallas kernels for 19% -> 15%
where the time goes in v3:
time: 131 us; the launch traced here: 130 us
  waiting for transfers between devices  50 us (38%)
  Pallas kernels  31.2 us (24%)
  starting transfers between devices  29.9 us (23%)
  local copies, waits for them, and re-layouts  14.3 us (11%)
  other arithmetic  3.82 us (3%)
    ppermute x8, waiting for transfers between devices, around(): lax.ppermute(value, ('x', 'core') if axis == 'x' else ('core', axis), pairs)  22.7 us
    pallas_call x2, Pallas kernels, product(): pl.pallas_call(lambda *refs: product_kernel(sizes, count, acc is None, *r...  19.8 us
    ppermute x17, waiting for transfers between devices, across(): return lax.ppermute(value, axes, [(i, count - 1 - i) for i in range(count)])  19.8 us
    ppermute x8, starting transfers between devices, around(): lax.ppermute(value, ('x', 'core') if axis == 'x' else ('core', axis), pairs)  13.8 us
    pallas_call x1, Pallas kernels, final(): pl.pallas_call(lambda *refs: final_kernel(sizes, count, slab_sizes, *refs...  11.3 us
    ppermute x17, starting transfers between devices, across(): return lax.ppermute(value, axes, [(i, count - 1 - i) for i in range(count)])  10.6 us
    unnamed x17, local copies, waits for them, and re-layouts  9.27 us
    all_to_all x1, waiting for transfers between devices, body(): lax.all_to_all(grid.reshape(128, 16), ROWS + BLK, split_axis=0, concat_ax...  7.57 us
  transfers between devices with their start and end apart: 26, of which 12 were waited for; matrix products, arithmetic and copies ran while one was open for 10% of the time, Pallas kernels for 15%

profile of v3, /device:TPU:1, one launch (start us, length us, event | category | flops | bytes accessed | tf_op | source)
XLA Modules:
  0.0 130.2 jit_solution(2010330440656244980)
XLA Ops:
  0.6 2.3 %copy.67 = bf16[1,32,128,128]{3,2,1,0:T(8,128)(2,1)} copy(bf16[1,32,128,128]{3,2,1,0:T(8,128)(2,1)} %param.11) | data formatting | bytes 2097152
  2.9 1.7 %dynamic-slice_bitcast_fusion = (bf16[32,16384]{1,0:T(8,128)(2,1)S(1)}, bf16[32,16384]{1,0:T(8,128)(2,1)S(1)}) fusion(bf16[1,64,16384]{2,1,0:T(8,128)(2,1)} %param.7, s32[]{:T(128)S(6)} %select_n.242, s32[]{:T(128)S(6)} %select_n.241), kind=kLoop, calls=%fused_computation.2 | loop fusion | bytes 4194312 | tf_op jit(solution)/shard_map/dynamic_slice | solution.py:46
  4.6 1.5 %collective-permute-start.5 = (bf16[32,128,128]{2,1,0:T(8,128)(2,1)}, bf16[32,128,128]{2,1,0:T(8,128)(2,1)}, u32[]{:S(2)}, u32[]{:S(2)}) collective-permute-start(bf16[32,128,128]{2,1,0:T(8,128)(2,1)} %get-tuple-element.25.refs_12_), channel_id=1, source_target_pairs={{0,8},{8,0},{1,9},{9,1},{2,10},{10,2},{3,11},{11,3},{4,12},{12,4},... | collective-permute-start | bytes 3145736 | tf_op jit(solution)/shard_map/ppermute | solution.py:38
  6.1 2.6 %collective-permute-start.4 = (bf16[32,128,128]{2,1,0:T(8,128)(2,1)}, bf16[32,128,128]{2,1,0:T(8,128)(2,1)}, u32[]{:S(2)}, u32[]{:S(2)}) collective-permute-start(bf16[32,128,128]{2,1,0:T(8,128)(2,1)} %get-tuple-element.25.refs_12_), channel_id=1, source_target_pairs={{0,32},{32,64},{64,96},{96,0},{8,104},{40,8},{72,40},{104,72},{1,3... | collective-permute-start | bytes 3145736 | tf_op jit(solution)/shard_map/ppermute | solution.py:33
  8.7 3.8 %collective-permute-start.3 = (bf16[32,128,128]{2,1,0:T(8,128)(2,1)}, bf16[32,128,128]{2,1,0:T(8,128)(2,1)}, u32[]{:S(2)}, u32[]{:S(2)}) collective-permute-start(bf16[32,128,128]{2,1,0:T(8,128)(2,1)} %get-tuple-element.25.refs_12_), channel_id=1, source_target_pairs={{0,20},{4,16},{16,4},{20,0},{1,21},{5,17},{17,5},{21,1},{2,22},{6,... | collective-permute-start | bytes 3145736 | tf_op jit(solution)/shard_map/ppermute | solution.py:38
  12.5 2.7 %collective-permute-start = (bf16[32,16384]{1,0:T(8,128)(2,1)S(1)}, bf16[32,16384]{1,0:T(8,128)(2,1)S(1)}, u32[]{:S(2)}, u32[]{:S(2)}) collective-permute-start(bf16[32,16384]{1,0:T(8,128)(2,1)S(1)} %get-tuple-element.23), channel_id=1, source_target_pairs={{0,1},{1,2},{2,3},{3,0},{8,11},{9,8},{10,9},{11,10},{4,5},{5,6},{6... | collective-permute-start | bytes 3145736 | tf_op jit(solution)/shard_map/ppermute | solution.py:33
  15.2 1.2 copy.33
  16.6 1.2 copy.32
  18.0 9.0 %collective-permute-done.refs_0_ = bf16[32,16384]{1,0:T(8,128)(2,1)S(1)} collective-permute-done((bf16[32,16384]{1,0:T(8,128)(2,1)S(1)}, bf16[32,16384]{1,0:T(8,128)(2,1)S(1)}, u32[]{:S(2)}, u32[]{:S(2)}) %collective-permute-start) | collective-permute-done | bytes 1048608 | tf_op jit(solution)/shard_map/ppermute | solution.py:33
  26.9 3.5 %collective-permute-start.1 = (bf16[32,128,128]{2,1,0:T(8,128)(2,1)}, bf16[32,128,128]{2,1,0:T(8,128)(2,1)}, u32[]{:S(2)}, u32[]{:S(2)}) collective-permute-start(bf16[32,128,128]{2,1,0:T(8,128)(2,1)} %bitcast.31.refs_4_), channel_id=1, source_target_pairs={{0,1},{1,2},{2,3},{3,0},{8,11},{9,8},{10,9},{11,10},{4,5},{5,6},{6... | collective-permute-start | bytes 3145736 | tf_op jit(solution)/shard_map/ppermute | solution.py:33
  30.5 0.5 collective-permute-start.6
  31.4 3.4 %copy.30 = bf16[16,8,128,128]{3,2,1,0:T(8,128)(2,1)S(1)} copy(bf16[16,8,128,128]{3,1,2,0:T(8,128)(2,1)} %bitcast.61) | data formatting | bytes 8388608
  35.0 0.2 copy.31
  35.3 5.3 %collective-permute-done.2.refs_3_ = bf16[32,128,128]{2,1,0:T(8,128)(2,1)} collective-permute-done((bf16[32,128,128]{2,1,0:T(8,128)(2,1)}, bf16[32,128,128]{2,1,0:T(8,128)(2,1)}, u32[]{:S(2)}, u32[]{:S(2)}) %collective-permute-start.2) | collective-permute-done | bytes 1048608 | tf_op jit(solution)/shard_map/ppermute | solution.py:38
  40.6 1.9 %collective-permute-done.1.refs_2_ = bf16[32,128,128]{2,1,0:T(8,128)(2,1)} collective-permute-done((bf16[32,128,128]{2,1,0:T(8,128)(2,1)}, bf16[32,128,128]{2,1,0:T(8,128)(2,1)}, u32[]{:S(2)}, u32[]{:S(2)}) %collective-permute-start.1) | collective-permute-done | bytes 1048608 | tf_op jit(solution)/shard_map/ppermute | solution.py:33
  42.5 1.8 %collective-permute-done.6.refs_6_ = bf16[32,128,128]{2,1,0:T(8,128)(2,1)S(1)} collective-permute-done((bf16[32,128,128]{2,1,0:T(8,128)(2,1)}, bf16[32,128,128]{2,1,0:T(8,128)(2,1)S(1)}, u32[]{:S(2)}, u32[]{:S(2)}) %collective-permute-start.6) | collective-permute-done | bytes 1048608 | tf_op jit(solution)/shard_map/ppermute | solution.py:33
  44.3 0.1 collective-permute-start.8
  44.4 0.4 collective-permute-start.9
  44.8 2.3 %collective-permute-start.10 = (bf16[32,16384]{1,0:T(8,128)(2,1)S(1)}, bf16[32,16384]{1,0:T(8,128)(2,1)S(1)}, u32[]{:S(2)}, u32[]{:S(2)}) collective-permute-start(bf16[32,16384]{1,0:T(8,128)(2,1)S(1)} %get-tuple-element.28), channel_id=1, source_target_pairs={{0,1},{1,2},{2,3},{3,0},{8,11},{9,8},{10,9},{11,10},{4,5},{5,6},{6... | collective-permute-start | bytes 3145736 | tf_op jit(solution)/shard_map/ppermute | solution.py:33
  47.1 0.3 collective-permute-start.11
  47.4 0.5 collective-permute-start.13
  47.9 0.6 copy.34
  48.5 1.4 %pad_maximum_fusion.refs_0_ = bf16[64,128,128]{2,1,0:T(8,128)(2,1)S(1)} fusion(bf16[32,128,128]{2,1,0:T(8,128)(2,1)S(1)} %collective-permute-done.8, bf16[32,128,128]{2,1,0:T(8,128)(2,1)} %get-tuple-element.26), kind=kLoop, calls=%fused_computation | loop fusion | flops 1048576 | bytes 4194304 | tf_op jit(solution)/shard_map/concatenate | solution.py:279
  49.9 1.4 %pad_maximum_fusion.1.refs_1_ = bf16[64,128,128]{2,1,0:T(8,128)(2,1)S(1)} fusion(bf16[32,128,128]{2,1,0:T(8,128)(2,1)S(1)} %collective-permute-done.9, bf16[32,128,128]{2,1,0:T(8,128)(2,1)} %get-tuple-element.27), kind=kLoop, calls=%fused_computation.1 | loop fusion | flops 1048576 | bytes 4194304 | tf_op jit(solution)/shard_map/concatenate | solution.py:279
  51.3 7.6 %collective-permute-done.10.refs_2_ = bf16[32,16384]{1,0:T(8,128)(2,1)S(1)} collective-permute-done((bf16[32,16384]{1,0:T(8,128)(2,1)S(1)}, bf16[32,16384]{1,0:T(8,128)(2,1)S(1)}, u32[]{:S(2)}, u32[]{:S(2)}) %collective-permute-start.10) | collective-permute-done | bytes 1048608 | tf_op jit(solution)/shard_map/ppermute | solution.py:33
  58.9 2.4 %collective-permute-done.11.refs_3_ = bf16[32,128,128]{2,1,0:T(8,128)(2,1)S(1)} collective-permute-done((bf16[32,128,128]{2,1,0:T(8,128)(2,1)}, bf16[32,128,128]{2,1,0:T(8,128)(2,1)S(1)}, u32[]{:S(2)}, u32[]{:S(2)}) %collective-permute-start.11) | collective-permute-done | bytes 1048608 | tf_op jit(solution)/shard_map/ppermute | solution.py:33
  61.3 0.2 copy.35
  61.5 1.6 %collective-permute-start.18 = (bf16[32,128,128]{2,1,0:T(8,128)(2,1)S(1)}, bf16[32,128,128]{2,1,0:T(8,128)(2,1)S(1)}, u32[]{:S(2)}, u32[]{:S(2)}) collective-permute-start(bf16[32,128,128]{2,1,0:T(8,128)(2,1)S(1)} %bitcast.56), channel_id=1, source_target_pairs={{0,8},{8,0},{1,9},{9,1},{2,10},{10,2},{3,11},{11,3},{4,12},{12,4},... | collective-permute-start | bytes 3145736 | tf_op jit(solution)/shard_map/ppermute | solution.py:38
  63.1 1.4 %collective-permute-start.14 = (bf16[64,128,128]{2,1,0:T(8,128)(2,1)S(1)}, bf16[64,128,128]{2,1,0:T(8,128)(2,1)S(1)}, u32[]{:S(2)}, u32[]{:S(2)}) collective-permute-start(bf16[64,128,128]{2,1,0:T(8,128)(2,1)S(1)} %get-tuple-element.33.refs_11_), channel_id=1, source_target_pairs={{0,1},{1,2},{2,3},{3,0},{8,11},{9,8},{10,9},{11,10},{4,5},{5,6},{6... | collective-permute-start | bytes 6291464 | tf_op jit(solution)/shard_map/ppermute | solution.py:33
  64.5 0.5 collective-permute-start.15
  65.0 0.4 collective-permute-done.18.refs_10_
  65.4 16.3 %product.2.refs_1_.refs_4_ = f32[64,128,128]{2,1,0:T(8,128)S(1)} custom-call(s32[1280]{0:T(1024)S(1)} %get-tuple-element.81.refs_11_.refs_0_, s32[1280]{0:T(1024)S(1)} %get-tuple-element.77.refs_12_.refs_1_, bf16[128,128,128]{2,1,0:T(8,128)(2,1)S(1)} %bitcast.46, bf16[32,128,128]{2,1,0:T(8,128)(2,1)} %bitcast.33.refs_3_, ...), custom_call_target="tpu_custom_call" | custom-call | flops 10737418240 | bytes 23068672 | tf_op jit(solution)/shard_map/product/pallas_call | solution.py:184
  81.7 6.1 %collective-permute-done.16.refs_2_ = bf16[32,128,128]{2,1,0:T(8,128)(2,1)S(1)} collective-permute-done((bf16[32,128,128]{2,1,0:T(8,128)(2,1)S(1)}, bf16[32,128,128]{2,1,0:T(8,128)(2,1)S(1)}, u32[]{:S(2)}, u32[]{:S(2)}) %collective-permute-start.16) | collective-permute-done | bytes 1048608 | tf_op jit(solution)/shard_map/ppermute | solution.py:38
  87.8 0.9 collective-permute-start.19
  88.7 2.3 %collective-permute-done.17.refs_3_ = bf16[32,128,128]{2,1,0:T(8,128)(2,1)S(1)} collective-permute-done((bf16[32,128,128]{2,1,0:T(8,128)(2,1)S(1)}, bf16[32,128,128]{2,1,0:T(8,128)(2,1)S(1)}, u32[]{:S(2)}, u32[]{:S(2)}) %collective-permute-start.17) | collective-permute-done | bytes 1048608 | tf_op jit(solution)/shard_map/ppermute | solution.py:38
  91.0 1.3 collective-permute-start.21
  92.3 0.1 collective-permute-start.23
  92.4 0.4 collective-permute-start.22
  92.8 0.1 collective-permute-start.24
  92.9 3.5 %product.3.refs_10_ = f32[64,128,128]{2,1,0:T(8,128)S(1)} custom-call(s32[256]{0:T(256)S(1)} %bitcast.60, s32[256]{0:T(256)S(1)} %get-tuple-element.80.refs_14_.refs_1_, bf16[128,128,128]{2,1,0:T(8,128)(2,1)S(1)} %bitcast.47, bf16[64,128,128]{2,1,0:T(8,128)(2,1)S(1)} %get-tuple-element.38.refs_3_, f32[64,128,128]{2,1,0:T(8,128)S(1)} %product.2.refs_1_.refs_4_), custom_call_target="tpu_custom_call" | custom-call | flops 2147483648 | bytes 14680064 | tf_op jit(solution)/shard_map/product/pallas_call | solution.py:184
  96.4 4.2 %collective-permute-done.22.refs_9_ = bf16[32,128,128]{2,1,0:T(8,128)(2,1)S(1)} collective-permute-done((bf16[32,128,128]{2,1,0:T(8,128)(2,1)S(1)}, bf16[32,128,128]{2,1,0:T(8,128)(2,1)S(1)}, u32[]{:S(2)}, u32[]{:S(2)}) %collective-permute-start.22) | collective-permute-done | bytes 1048608 | tf_op jit(solution)/shard_map/ppermute | solution.py:38
  100.6 1.5 %collective-permute-done.24.refs_24_ = bf16[32,128,128]{2,1,0:T(8,128)(2,1)S(1)} collective-permute-done((bf16[32,128,128]{2,1,0:T(8,128)(2,1)S(1)}, bf16[32,128,128]{2,1,0:T(8,128)(2,1)S(1)}, u32[]{:S(2)}, u32[]{:S(2)}) %collective-permute-start.24) | collective-permute-done | bytes 1048608 | tf_op jit(solution)/shard_map/ppermute | solution.py:38
  102.1 11.3 %final.1 = (bf16[64,128,128]{2,1,0:T(8,128)(2,1)S(1)}, f32[16,128]{1,0:T(8,128)S(1)}) custom-call(s32[512]{0:T(512)S(1)} %pad_add_fusion.refs_15_.refs_0_, s32[512]{0:T(512)S(1)} %pad_add_fusion.1.refs_16_.refs_1_, s32[16]{0:T(128)S(1)} %select_reduce_fusion.refs_10_.refs_2_, s32[256]{0:T(256)S(1)} %get-tuple-element.82.refs_7_.refs_3_, ...), custom_call_target="tpu_custom_call" | custom-call | flops 8589934592 | bytes 41943040 | tf_op jit(solution)/shard_map/final/pallas_call | solution.py:205
  113.4 0.7 all_to_all.6
  114.1 5.5 %all-to-all-start = ((f32[128,1,16]{2,1,0:T(1,128)}), f32[128,1,16]{2,1,0:T(1,128)S(1)}, u32[]{:S(2)}, u32[]{:S(2)}) async-start(f32[128,1,16]{2,1,0:T(1,128)} %bitcast.20), calls=%async_computation | async-start | bytes 131072 | tf_op jit(solution)/shard_map/all_to_all | solution.py:295
  119.6 2.3 %reshape.288 = bf16[1,1,64,16384]{3,2,1,0:T(8,128)(2,1)} reshape(bf16[64,128,128]{2,1,0:T(8,128)(2,1)S(1)} %get-tuple-element.42) | data formatting | bytes 4194304 | tf_op jit(solution)/shard_map/reshape | solution.py:296
  121.9 7.6 %all-to-all-done = f32[128,1,16]{2,1,0:T(1,128)S(1)} async-done(((f32[128,1,16]{2,1,0:T(1,128)}), f32[128,1,16]{2,1,0:T(1,128)S(1)}, u32[]{:S(2)}, u32[]{:S(2)}) %all-to-all-start) | async-done | bytes 8224 | tf_op jit(solution)/shard_map/all_to_all | solution.py:295
  129.5 0.7 reduce_sum.19
  (57 shorter events, 0.8 us)
Async XLA Ops:
  4.6 11.8 %copy-start.1 = (s32[1,1,8,2,256]{4,3,2,1,0:T(2,128)S(1)}, s32[1,1,8,2,256]{4,3,2,1,0:T(2,128)}, u32[]{:S(2)}) copy-start(s32[1,1,8,2,256]{4,3,2,1,0:T(2,128)} %param.9) | copy-start | bytes 49156
  4.6 25.8 %collective-permute-start.5 = (bf16[32,128,128]{2,1,0:T(8,128)(2,1)}, bf16[32,128,128]{2,1,0:T(8,128)(2,1)}, u32[]{:S(2)}, u32[]{:S(2)}) collective-permute-start(bf16[32,128,128]{2,1,0:T(8,128)(2,1)} %get-tuple-element.25.refs_12_), channel_id=1, source_target_pairs={{0,8},{8,0},{1,9},{9,1},{2,10},{10,2},{3,11},{11,3},{4,12},{12,4},... | collective-permute-start | bytes 3145736 | tf_op jit(solution)/shard_map/ppermute | solution.py:38
  6.1 24.9 %collective-permute-start.4 = (bf16[32,128,128]{2,1,0:T(8,128)(2,1)}, bf16[32,128,128]{2,1,0:T(8,128)(2,1)}, u32[]{:S(2)}, u32[]{:S(2)}) collective-permute-start(bf16[32,128,128]{2,1,0:T(8,128)(2,1)} %get-tuple-element.25.refs_12_), channel_id=1, source_target_pairs={{0,32},{32,64},{64,96},{96,0},{8,104},{40,8},{72,40},{104,72},{1,3... | collective-permute-start | bytes 3145736 | tf_op jit(solution)/shard_map/ppermute | solution.py:33
  8.7 33.8 %collective-permute-start.3 = (bf16[32,128,128]{2,1,0:T(8,128)(2,1)}, bf16[32,128,128]{2,1,0:T(8,128)(2,1)}, u32[]{:S(2)}, u32[]{:S(2)}) collective-permute-start(bf16[32,128,128]{2,1,0:T(8,128)(2,1)} %get-tuple-element.25.refs_12_), channel_id=1, source_target_pairs={{0,20},{4,16},{16,4},{20,0},{1,21},{5,17},{17,5},{21,1},{2,22},{6,... | collective-permute-start | bytes 3145736 | tf_op jit(solution)/shard_map/ppermute | solution.py:38
  12.5 14.5 %collective-permute-start = (bf16[32,16384]{1,0:T(8,128)(2,1)S(1)}, bf16[32,16384]{1,0:T(8,128)(2,1)S(1)}, u32[]{:S(2)}, u32[]{:S(2)}) collective-permute-start(bf16[32,16384]{1,0:T(8,128)(2,1)S(1)} %get-tuple-element.23), channel_id=1, source_target_pairs={{0,1},{1,2},{2,3},{3,0},{8,11},{9,8},{10,9},{11,10},{4,5},{5,6},{6... | collective-permute-start | bytes 3145736 | tf_op jit(solution)/shard_map/ppermute | solution.py:33
  15.2 2.7 %copy-start.2 = (s32[1,1,16,16,3]{3,2,4,1,0:T(8,128)S(1)}, s32[1,1,16,16,3]{3,2,4,1,0:T(8,128)}, u32[]{:S(2)}) copy-start(s32[1,1,16,16,3]{3,2,4,1,0:T(8,128)} %param.10) | copy-start | bytes 9220
  16.4 24.2 %collective-permute-start.2 = (bf16[32,128,128]{2,1,0:T(8,128)(2,1)}, bf16[32,128,128]{2,1,0:T(8,128)(2,1)}, u32[]{:S(2)}, u32[]{:S(2)}) collective-permute-start(bf16[32,128,128]{2,1,0:T(8,128)(2,1)} %bitcast.33.refs_3_), channel_id=1, source_target_pairs={{0,4},{4,0},{1,5},{5,1},{2,6},{6,2},{3,7},{7,3},{8,12},{12,8},{9,1... | collective-permute-start | bytes 3145736 | tf_op jit(solution)/shard_map/ppermute | solution.py:38
  26.9 15.6 %collective-permute-start.1 = (bf16[32,128,128]{2,1,0:T(8,128)(2,1)}, bf16[32,128,128]{2,1,0:T(8,128)(2,1)}, u32[]{:S(2)}, u32[]{:S(2)}) collective-permute-start(bf16[32,128,128]{2,1,0:T(8,128)(2,1)} %bitcast.31.refs_4_), channel_id=1, source_target_pairs={{0,1},{1,2},{2,3},{3,0},{8,11},{9,8},{10,9},{11,10},{4,5},{5,6},{6... | collective-permute-start | bytes 3145736 | tf_op jit(solution)/shard_map/ppermute | solution.py:33
  30.5 13.9 %collective-permute-start.6 = (bf16[32,128,128]{2,1,0:T(8,128)(2,1)}, bf16[32,128,128]{2,1,0:T(8,128)(2,1)S(1)}, u32[]{:S(2)}, u32[]{:S(2)}) collective-permute-start(bf16[32,128,128]{2,1,0:T(8,128)(2,1)} %collective-permute-done.5.refs_13_), channel_id=1, source_target_pairs={{0,32},{32,64},{64,96},{96,0},{8,104},{40,8},{72,40},{104,72},{1,3... | collective-permute-start | bytes 3145736 | tf_op jit(solution)/shard_map/ppermute | solution.py:33
  31.0 13.3 %collective-permute-start.7 = (bf16[32,128,128]{2,1,0:T(8,128)(2,1)}, bf16[32,128,128]{2,1,0:T(8,128)(2,1)}, u32[]{:S(2)}, u32[]{:S(2)}) collective-permute-start(bf16[32,128,128]{2,1,0:T(8,128)(2,1)} %collective-permute-done.4.refs_5_), channel_id=1, source_target_pairs={{0,8},{8,0},{1,9},{9,1},{2,10},{10,2},{3,11},{11,3},{4,12},{12,4},... | collective-permute-start | bytes 3145736 | tf_op jit(solution)/shard_map/ppermute | solution.py:38
  44.3 3.6 %copy-start = (bf16[1,1,64,16384]{3,2,1,0:T(8,128)(2,1)S(1)}, bf16[1,1,64,16384]{3,2,1,0:T(8,128)(2,1)}, u32[]{:S(2)}) copy-start(bf16[1,1,64,16384]{3,2,1,0:T(8,128)(2,1)} %param.8) | copy-start | bytes 6291460
  44.3 3.1 %collective-permute-start.8 = (bf16[32,128,128]{2,1,0:T(8,128)(2,1)}, bf16[32,128,128]{2,1,0:T(8,128)(2,1)S(1)}, u32[]{:S(2)}, u32[]{:S(2)}) collective-permute-start(bf16[32,128,128]{2,1,0:T(8,128)(2,1)} %get-tuple-element.26), channel_id=1, source_target_pairs={{0,8},{8,0},{1,9},{9,1},{2,10},{10,2},{3,11},{11,3},{4,12},{12,4},... | collective-permute-start | bytes 3145736 | tf_op jit(solution)/shard_map/ppermute | solution.py:38
  44.4 5.4 %collective-permute-start.9 = (bf16[32,128,128]{2,1,0:T(8,128)(2,1)}, bf16[32,128,128]{2,1,0:T(8,128)(2,1)S(1)}, u32[]{:S(2)}, u32[]{:S(2)}) collective-permute-start(bf16[32,128,128]{2,1,0:T(8,128)(2,1)} %get-tuple-element.27), channel_id=1, source_target_pairs={{0,8},{8,0},{1,9},{9,1},{2,10},{10,2},{3,11},{11,3},{4,12},{12,4},... | collective-permute-start | bytes 3145736 | tf_op jit(solution)/shard_map/ppermute | solution.py:38
  44.8 14.0 %collective-permute-start.10 = (bf16[32,16384]{1,0:T(8,128)(2,1)S(1)}, bf16[32,16384]{1,0:T(8,128)(2,1)S(1)}, u32[]{:S(2)}, u32[]{:S(2)}) collective-permute-start(bf16[32,16384]{1,0:T(8,128)(2,1)S(1)} %get-tuple-element.28), channel_id=1, source_target_pairs={{0,1},{1,2},{2,3},{3,0},{8,11},{9,8},{10,9},{11,10},{4,5},{5,6},{6... | collective-permute-start | bytes 3145736 | tf_op jit(solution)/shard_map/ppermute | solution.py:33
  47.1 14.2 %collective-permute-start.11 = (bf16[32,128,128]{2,1,0:T(8,128)(2,1)}, bf16[32,128,128]{2,1,0:T(8,128)(2,1)S(1)}, u32[]{:S(2)}, u32[]{:S(2)}) collective-permute-start(bf16[32,128,128]{2,1,0:T(8,128)(2,1)} %get-tuple-element.29.refs_14_), channel_id=1, source_target_pairs={{0,32},{32,64},{64,96},{96,0},{8,104},{40,8},{72,40},{104,72},{1,3... | collective-permute-start | bytes 3145736 | tf_op jit(solution)/shard_map/ppermute | solution.py:33
  47.4 13.9 %collective-permute-start.12 = (bf16[32,128,128]{2,1,0:T(8,128)(2,1)S(1)}, bf16[32,128,128]{2,1,0:T(8,128)(2,1)S(1)}, u32[]{:S(2)}, u32[]{:S(2)}) collective-permute-start(bf16[32,128,128]{2,1,0:T(8,128)(2,1)S(1)} %get-tuple-element.31.refs_5_), channel_id=1, source_target_pairs={{0,8},{8,0},{1,9},{9,1},{2,10},{10,2},{3,11},{11,3},{4,12},{12,4},... | collective-permute-start | bytes 3145736 | tf_op jit(solution)/shard_map/ppermute | solution.py:38
  47.4 13.9 %collective-permute-start.13 = (bf16[32,128,128]{2,1,0:T(8,128)(2,1)}, bf16[32,128,128]{2,1,0:T(8,128)(2,1)S(1)}, u32[]{:S(2)}, u32[]{:S(2)}) collective-permute-start(bf16[32,128,128]{2,1,0:T(8,128)(2,1)} %get-tuple-element.32.refs_6_), channel_id=1, source_target_pairs={{0,8},{8,0},{1,9},{9,1},{2,10},{10,2},{3,11},{11,3},{4,12},{12,4},... | collective-permute-start | bytes 3145736 | tf_op jit(solution)/shard_map/ppermute | solution.py:38
  61.5 3.8 %collective-permute-start.18 = (bf16[32,128,128]{2,1,0:T(8,128)(2,1)S(1)}, bf16[32,128,128]{2,1,0:T(8,128)(2,1)S(1)}, u32[]{:S(2)}, u32[]{:S(2)}) collective-permute-start(bf16[32,128,128]{2,1,0:T(8,128)(2,1)S(1)} %bitcast.56), channel_id=1, source_target_pairs={{0,8},{8,0},{1,9},{9,1},{2,10},{10,2},{3,11},{11,3},{4,12},{12,4},... | collective-permute-start | bytes 3145736 | tf_op jit(solution)/shard_map/ppermute | solution.py:38
  63.1 24.7 %collective-permute-start.16 = (bf16[32,128,128]{2,1,0:T(8,128)(2,1)S(1)}, bf16[32,128,128]{2,1,0:T(8,128)(2,1)S(1)}, u32[]{:S(2)}, u32[]{:S(2)}) collective-permute-start(bf16[32,128,128]{2,1,0:T(8,128)(2,1)S(1)} %bitcast.57), channel_id=1, source_target_pairs={{0,4},{4,0},{1,5},{5,1},{2,6},{6,2},{3,7},{7,3},{8,12},{12,8},{9,1... | collective-permute-start | bytes 3145736 | tf_op jit(solution)/shard_map/ppermute | solution.py:38
  63.1 27.9 %collective-permute-start.14 = (bf16[64,128,128]{2,1,0:T(8,128)(2,1)S(1)}, bf16[64,128,128]{2,1,0:T(8,128)(2,1)S(1)}, u32[]{:S(2)}, u32[]{:S(2)}) collective-permute-start(bf16[64,128,128]{2,1,0:T(8,128)(2,1)S(1)} %get-tuple-element.33.refs_11_), channel_id=1, source_target_pairs={{0,1},{1,2},{2,3},{3,0},{8,11},{9,8},{10,9},{11,10},{4,5},{5,6},{6... | collective-permute-start | bytes 6291464 | tf_op jit(solution)/shard_map/ppermute | solution.py:33
  64.5 26.5 %collective-permute-start.15 = (bf16[64,128,128]{2,1,0:T(8,128)(2,1)S(1)}, bf16[64,128,128]{2,1,0:T(8,128)(2,1)S(1)}, u32[]{:S(2)}, u32[]{:S(2)}) collective-permute-start(bf16[64,128,128]{2,1,0:T(8,128)(2,1)S(1)} %get-tuple-element.34.refs_20_), channel_id=1, source_target_pairs={{0,32},{32,64},{64,96},{96,0},{8,104},{40,8},{72,40},{104,72},{1,3... | collective-permute-start | bytes 6291464 | tf_op jit(solution)/shard_map/ppermute | solution.py:33
  65.0 23.7 %collective-permute-start.20 = (bf16[32,128,128]{2,1,0:T(8,128)(2,1)S(1)}, bf16[32,128,128]{2,1,0:T(8,128)(2,1)S(1)}, u32[]{:S(2)}, u32[]{:S(2)}) collective-permute-start(bf16[32,128,128]{2,1,0:T(8,128)(2,1)S(1)} %get-tuple-element.36.refs_18_), channel_id=1, source_target_pairs={{0,8},{8,0},{1,9},{9,1},{2,10},{10,2},{3,11},{11,3},{4,12},{12,4},... | collective-permute-start | bytes 3145736 | tf_op jit(solution)/shard_map/ppermute | solution.py:38
  65.4 25.6 %collective-permute-start.17 = (bf16[32,128,128]{2,1,0:T(8,128)(2,1)S(1)}, bf16[32,128,128]{2,1,0:T(8,128)(2,1)S(1)}, u32[]{:S(2)}, u32[]{:S(2)}) collective-permute-start(bf16[32,128,128]{2,1,0:T(8,128)(2,1)S(1)} %get-tuple-element.36.refs_18_), channel_id=1, source_target_pairs={{0,20},{4,16},{16,4},{20,0},{1,21},{5,17},{17,5},{21,1},{2,22},{6,... | collective-permute-start | bytes 3145736 | tf_op jit(solution)/shard_map/ppermute | solution.py:38
  87.8 3.2 %collective-permute-start.19 = (bf16[32,128,128]{2,1,0:T(8,128)(2,1)S(1)}, bf16[32,128,128]{2,1,0:T(8,128)(2,1)S(1)}, u32[]{:S(2)}, u32[]{:S(2)}) collective-permute-start(bf16[32,128,128]{2,1,0:T(8,128)(2,1)S(1)} %gate.8.refs_15_), channel_id=1, source_target_pairs={{0,8},{8,0},{1,9},{9,1},{2,10},{10,2},{3,11},{11,3},{4,12},{12,4},... | collective-permute-start | bytes 3145736 | tf_op jit(solution)/shard_map/ppermute | solution.py:38
  91.0 11.1 %collective-permute-start.21 = (bf16[64,128,128]{2,1,0:T(8,128)(2,1)S(1)}, bf16[64,128,128]{2,1,0:T(8,128)(2,1)S(1)}, u32[]{:S(2)}, u32[]{:S(2)}) collective-permute-start(bf16[64,128,128]{2,1,0:T(8,128)(2,1)S(1)} %get-tuple-element.38.refs_3_), channel_id=1, source_target_pairs={{0,8},{8,0},{1,9},{9,1},{2,10},{10,2},{3,11},{11,3},{4,12},{12,4},... | collective-permute-start | bytes 6291464 | tf_op jit(solution)/shard_map/ppermute | solution.py:38
  92.3 9.8 %collective-permute-start.23 = (bf16[64,128,128]{2,1,0:T(8,128)(2,1)S(1)}, bf16[64,128,128]{2,1,0:T(8,128)(2,1)S(1)}, u32[]{:S(2)}, u32[]{:S(2)}) collective-permute-start(bf16[64,128,128]{2,1,0:T(8,128)(2,1)S(1)} %get-tuple-element.40.refs_21_), channel_id=1, source_target_pairs={{0,8},{8,0},{1,9},{9,1},{2,10},{10,2},{3,11},{11,3},{4,12},{12,4},... | collective-permute-start | bytes 6291464 | tf_op jit(solution)/shard_map/ppermute | solution.py:38
  92.4 8.2 %collective-permute-start.22 = (bf16[32,128,128]{2,1,0:T(8,128)(2,1)S(1)}, bf16[32,128,128]{2,1,0:T(8,128)(2,1)S(1)}, u32[]{:S(2)}, u32[]{:S(2)}) collective-permute-start(bf16[32,128,128]{2,1,0:T(8,128)(2,1)S(1)} %get-tuple-element.39.refs_8_), channel_id=1, source_target_pairs={{0,8},{8,0},{1,9},{9,1},{2,10},{10,2},{3,11},{11,3},{4,12},{12,4},... | collective-permute-start | bytes 3145736 | tf_op jit(solution)/shard_map/ppermute | solution.py:38
  92.8 9.3 %collective-permute-start.24 = (bf16[32,128,128]{2,1,0:T(8,128)(2,1)S(1)}, bf16[32,128,128]{2,1,0:T(8,128)(2,1)S(1)}, u32[]{:S(2)}, u32[]{:S(2)}) collective-permute-start(bf16[32,128,128]{2,1,0:T(8,128)(2,1)S(1)} %get-tuple-element.41.refs_23_), channel_id=1, source_target_pairs={{0,8},{8,0},{1,9},{9,1},{2,10},{10,2},{3,11},{11,3},{4,12},{12,4},... | collective-permute-start | bytes 3145736 | tf_op jit(solution)/shard_map/ppermute | solution.py:38
  114.1 15.4 %all-to-all-start = ((f32[128,1,16]{2,1,0:T(1,128)}), f32[128,1,16]{2,1,0:T(1,128)S(1)}, u32[]{:S(2)}, u32[]{:S(2)}) async-start(f32[128,1,16]{2,1,0:T(1,128)} %bitcast.20), calls=%async_computation | async-start | bytes 131072 | tf_op jit(solution)/shard_map/all_to_all | solution.py:295

commit v4 on v3

--- a/solution.py
+++ b/solution.py
@@ -242,14 +242,13 @@
     x, zh, zl, y = (lax.axis_index(name) for name in ("x", "zh", "zl", "y"))
     slab = basis[0]
     share = window_tiles[0]
-    raw_mine, raw_other, slab = gate([half_of(share, core), half_of(share, 1 - core), slab])
-    mine, other = matrices(raw_mine), matrices(raw_other)
+    raw_share, share = share, matrices(share)
     a_tiles = p2_tiles[0, 0].reshape(A_TILES, BS, BS)
     square = square_tiles[0, 0].reshape(C_TILES, BS, BS)
     ahead = ahead_of(core)
     stages = (
-        ((0, 0, 0), (0, ahead, 0), (0, 4 - ahead, 1), (0, 2, 0), (1, 0, 0)),
-        ((1, ahead, 0),),
+        ((0, 0, core), (0, ahead, core), (0, 4 - ahead, core), (1, 0, 0)),
+        ((1, ahead, 0), (0, 2, 0)),
         ((1, 4 - ahead, 1), (1, 2, 0)),
     )
     plan = [plans(pairs[0, 0], core, zl, y, stage) for stage in stages]
@@ -263,31 +262,27 @@
     slots = jnp.arange(16, dtype=jnp.int32)[:, None]
     who = jnp.sum(jnp.where(place // NBAS == slots.T, owner, 0), axis=0)
     link, zz = ("zl",), ("zh", "zl")
-    raw_near, bnear_a = around(raw_mine, "y"), around(slab, "x")
-    pair, bpair = across(mine, link), across(slab, zz)
+    near, bnear_a = around(raw_share, "y"), around(slab, "x")
+    pair, bpair = across(half_of(raw_share, core), link), across(slab, zz)
     bother = swapped(slab)
-    near_b, bnear_b = around(other, "y"), around(bother, "x")
-    near_a = matrices(raw_near)
+    bnear_b = around(bother, "x")
     sbnear_a = swapped(bnear_a)
-    work = [tile, row, col, who, *[index for both in plan for index in both], a_tiles, sbnear_a]
-    raw_near, near_a, near_b, pair, bpair, bnear_a, bnear_b = gate(
-        [raw_near, near_a, near_b, pair, bpair, bnear_a, bnear_b], work
-    )
-    far, bfar = around(raw_near, "y"), around(bnear_a, "x")
-    spair, sbpair = swapped(pair), swapped(bpair)
-    snear_a, snear_b = swapped(near_a), swapped(near_b)
+    work = [tile, row, col, who, *[index for both in plan for index in both], a_tiles, share, sbnear_a]
+    near, pair, bpair, bnear_a, bnear_b = gate([near, pair, bpair, bnear_a, bnear_b], work)
+    far, bfar = around(half_of(near, core), "y"), around(bnear_a, "x")
+    near, pair = matrices(near), matrices(pair)
+    spair, sbpair, snear = swapped(pair), swapped(bpair), swapped(near)
     both, bboth = jnp.concatenate([pair, spair]), jnp.concatenate([bpair, sbpair])
-    both, bboth, far, bfar, bnear_b = gate([both, bboth, far, bfar, bnear_b], [snear_a, snear_b, square])
+    both, bboth, far, bfar, bnear_b = gate([both, bboth, far, bfar, bnear_b], [snear, square])
     far = matrices(far)
     pnear, bpnear = around(both, "y"), around(bboth, "x")
     pfar, bpfar = across(far, link), across(bfar, zz)
-    sfar = swapped(far)
-    acc = product(plan[0], a_tiles, [mine, other, near_a, near_b, snear_a, snear_b, far, sfar, both])
-    (bnear_b,) = gate([bnear_b], [acc])
-    sbnear_b, sbfar = swapped(bnear_b), swapped(bfar)
-    pnear, bpnear, pfar, bpfar = gate([pnear, bpnear, pfar, bpfar], [acc, sbnear_b, sbfar])
+    acc = product(plan[0], a_tiles, [share, near, snear, both])
+    bnear_b, far = gate([bnear_b, far], [acc])
+    sbnear_b, sbfar, sfar = swapped(bnear_b), swapped(bfar), swapped(far)
+    pnear, bpnear, pfar, bpfar = gate([pnear, bpnear, pfar, bpfar], [acc, sfar, sbnear_b, sbfar])
     spnear, spfar, sbpfar, sbpnear = swapped(pnear), swapped(pfar), swapped(bpfar), swapped(bpnear)
-    acc = product(plan[1], a_tiles, [pnear], acc)
+    acc = product(plan[1], a_tiles, [pnear, far, sfar], acc)
     tables = [
         slab, bother, bnear_a, bnear_b, sbnear_a, sbnear_b, bfar, sbfar, bboth, bpnear, sbpnear, bpfar, sbpfar,
     ]

time: 131 us -> 125 us (0.954)
  local copies, waits for them, and re-layouts: 14.3 us -> 12.6 us
    ppermute x8 -> x7, waiting for transfers between devices: 22.7 us -> 14.1 us  [around(): lax.ppermute(value, ('x', 'core') if axis == 'x' else ('core', axis), pairs)]
    ppermute x17 -> x16, waiting for transfers between devices: 19.8 us -> 27 us  [across(): return lax.ppermute(value, axes, [(i, count - 1 - i) for i in range(count)])]
    ppermute x17 -> x16, starting transfers between devices: 10.6 us -> 13.4 us  [across(): return lax.ppermute(value, axes, [(i, count - 1 - i) for i in range(count)])]
    unnamed x17 -> x20, local copies, waits for them, and re-layouts: 9.27 us -> 6.92 us
    ppermute x8 -> x7, starting transfers between devices: 13.8 us -> 11.8 us  [around(): lax.ppermute(value, ('x', 'core') if axis == 'x' else ('core', axis), pairs)]
  transfers between devices with their start and end apart: 26 -> 24, of which waited for: 12 -> 11; matrix products, arithmetic and copies ran while one was open for 10% -> 9% of each run, Pallas kernels for 15% -> 15%
where the time goes in v4:
time: 125 us
  waiting for transfers between devices  48.7 us (39%)
  Pallas kernels  30.4 us (24%)
  starting transfers between devices  29.6 us (24%)
  local copies, waits for them, and re-layouts  12.6 us (10%)
  other arithmetic  2.56 us (2%)
    ppermute x16, waiting for transfers between devices, across(): return lax.ppermute(value, axes, [(i, count - 1 - i) for i in range(count)])  27 us
    pallas_call x2, Pallas kernels, product(): pl.pallas_call(lambda *refs: product_kernel(sizes, count, acc is None, *r...  19.4 us
    ppermute x7, waiting for transfers between devices, around(): lax.ppermute(value, ('x', 'core') if axis == 'x' else ('core', axis), pairs)  14.1 us
    ppermute x16, starting transfers between devices, across(): return lax.ppermute(value, axes, [(i, count - 1 - i) for i in range(count)])  13.4 us
    ppermute x7, starting transfers between devices, around(): lax.ppermute(value, ('x', 'core') if axis == 'x' else ('core', axis), pairs)  11.8 us
    pallas_call x1, Pallas kernels, final(): pl.pallas_call(lambda *refs: final_kernel(sizes, count, slab_sizes, *refs...  11.1 us
    all_to_all x1, waiting for transfers between devices, body(): lax.all_to_all(grid.reshape(128, 16), ROWS + BLK, split_axis=0, concat_ax...  7.55 us
    unnamed x20, local copies, waits for them, and re-layouts  6.92 us
  transfers between devices with their start and end apart: 24, of which 11 were waited for; matrix products, arithmetic and copies ran while one was open for 9% of the time, Pallas kernels for 15%

profile of v4, /device:TPU:1, one launch (start us, length us, event | category | flops | bytes accessed | tf_op | source)
XLA Modules:
  0.0 124.9 jit_solution(4927401497284010773)
XLA Ops:
  0.6 1.5 %collective-permute-start.4 = (bf16[32,128,128]{2,1,0:T(8,128)(2,1)}, bf16[32,128,128]{2,1,0:T(8,128)(2,1)}, u32[]{:S(2)}, u32[]{:S(2)}) collective-permute-start(bf16[32,128,128]{2,1,0:T(8,128)(2,1)} %bitcast.59), channel_id=1, source_target_pairs={{0,8},{8,0},{1,9},{9,1},{2,10},{10,2},{3,11},{11,3},{4,12},{12,4},... | collective-permute-start | bytes 3145736 | tf_op jit(solution)/shard_map/ppermute | solution.py:38
  2.2 2.6 %collective-permute-start.3 = (bf16[32,128,128]{2,1,0:T(8,128)(2,1)}, bf16[32,128,128]{2,1,0:T(8,128)(2,1)}, u32[]{:S(2)}, u32[]{:S(2)}) collective-permute-start(bf16[32,128,128]{2,1,0:T(8,128)(2,1)} %bitcast.60), channel_id=1, source_target_pairs={{0,32},{32,64},{64,96},{96,0},{8,104},{40,8},{72,40},{104,72},{1,3... | collective-permute-start | bytes 3145736 | tf_op jit(solution)/shard_map/ppermute | solution.py:33
  4.7 3.8 %collective-permute-start.2 = (bf16[32,128,128]{2,1,0:T(8,128)(2,1)}, bf16[32,128,128]{2,1,0:T(8,128)(2,1)}, u32[]{:S(2)}, u32[]{:S(2)}) collective-permute-start(bf16[32,128,128]{2,1,0:T(8,128)(2,1)} %bitcast.61), channel_id=1, source_target_pairs={{0,20},{4,16},{16,4},{20,0},{1,21},{5,17},{17,5},{21,1},{2,22},{6,... | collective-permute-start | bytes 3145736 | tf_op jit(solution)/shard_map/ppermute | solution.py:38
  8.5 2.3 %dynamic-slice_bitcast_fusion = bf16[32,16384]{1,0:T(8,128)(2,1)} fusion(bf16[1,64,16384]{2,1,0:T(8,128)(2,1)} %param.7, s32[]{:T(128)S(6)} %select_n.239), kind=kLoop, calls=%fused_computation.2 | loop fusion | bytes 2097156 | tf_op jit(solution)/shard_map/dynamic_slice | solution.py:46
  10.7 2.7 %collective-permute-start = (bf16[64,16384]{1,0:T(8,128)(2,1)}, bf16[64,16384]{1,0:T(8,128)(2,1)S(1)}, u32[]{:S(2)}, u32[]{:S(2)}) collective-permute-start(bf16[64,16384]{1,0:T(8,128)(2,1)} %bitcast.5), channel_id=1, source_target_pairs={{0,1},{1,2},{2,3},{3,0},{8,11},{9,8},{10,9},{11,10},{4,5},{5,6},{6... | collective-permute-start | bytes 6291464 | tf_op jit(solution)/shard_map/ppermute | solution.py:33
  13.7 0.6 collective-permute-start.5
  14.3 2.5 %collective-permute-done.3.refs_3_ = bf16[32,128,128]{2,1,0:T(8,128)(2,1)} collective-permute-done((bf16[32,128,128]{2,1,0:T(8,128)(2,1)}, bf16[32,128,128]{2,1,0:T(8,128)(2,1)}, u32[]{:S(2)}, u32[]{:S(2)}) %collective-permute-start.3) | collective-permute-done | bytes 1048608 | tf_op jit(solution)/shard_map/ppermute | solution.py:33
  16.8 1.8 %collective-permute-start.6 = (bf16[32,128,128]{2,1,0:T(8,128)(2,1)}, bf16[32,128,128]{2,1,0:T(8,128)(2,1)}, u32[]{:S(2)}, u32[]{:S(2)}) collective-permute-start(bf16[32,128,128]{2,1,0:T(8,128)(2,1)} %collective-permute-done.3.refs_3_), channel_id=1, source_target_pairs={{0,8},{8,0},{1,9},{9,1},{2,10},{10,2},{3,11},{11,3},{4,12},{12,4},... | collective-permute-start | bytes 3145736 | tf_op jit(solution)/shard_map/ppermute | solution.py:38
  19.0 2.3 %copy.27 = bf16[8,8,128,128]{3,2,1,0:T(8,128)(2,1)S(1)} copy(bf16[8,8,128,128]{3,1,2,0:T(8,128)(2,1)} %bitcast.29) | data formatting | bytes 4194304
  21.3 0.5 copy-done.3
  21.8 1.2 copy.26
  23.2 12.7 %collective-permute-done.1.refs_1_ = bf16[32,16384]{1,0:T(8,128)(2,1)} collective-permute-done((bf16[32,16384]{1,0:T(8,128)(2,1)}, bf16[32,16384]{1,0:T(8,128)(2,1)}, u32[]{:S(2)}, u32[]{:S(2)}) %collective-permute-start.1) | collective-permute-done | bytes 1048608 | tf_op jit(solution)/shard_map/ppermute | solution.py:38
  36.0 0.8 collective-permute-done.refs_0_
  36.8 1.5 %copy.28 = bf16[4,8,128,128]{3,2,1,0:T(8,128)(2,1)S(1)} copy(bf16[4,8,128,128]{3,1,2,0:T(8,128)(2,1)} %bitcast.31) | data formatting | bytes 2097152
  38.2 0.9 collective-permute-start.7
  39.1 0.1 collective-permute-start.8
  39.2 0.6 copy.29
  39.8 0.5 collective-permute-start.11
  40.4 2.4 %collective-permute-start.9 = (bf16[32,16384]{1,0:T(8,128)(2,1)S(1)}, bf16[32,16384]{1,0:T(8,128)(2,1)S(1)}, u32[]{:S(2)}, u32[]{:S(2)}) collective-permute-start(bf16[32,16384]{1,0:T(8,128)(2,1)S(1)} %constant_dynamic-slice_fusion.8), channel_id=1, source_target_pairs={{0,1},{1,2},{2,3},{3,0},{8,11},{9,8},{10,9},{11,10},{4,5},{5,6},{6... | collective-permute-start | bytes 3145736 | tf_op jit(solution)/shard_map/ppermute | solution.py:33
  42.7 0.7 collective-permute-start.10
  43.4 0.6 copy.30
  44.0 0.2 pad_maximum_fusion.refs_0_
  44.2 0.3 collective-permute-done.8
  44.5 1.4 %pad_maximum_fusion.1.refs_1_ = bf16[64,128,128]{2,1,0:T(8,128)(2,1)S(1)} fusion(bf16[32,128,128]{2,1,0:T(8,128)(2,1)S(1)} %collective-permute-done.8, bf16[32,128,128]{2,1,0:T(8,128)(2,1)} %get-tuple-element.21), kind=kLoop, calls=%fused_computation.1 | loop fusion | flops 1048576 | bytes 4194304 | tf_op jit(solution)/shard_map/concatenate | solution.py:275
  45.9 8.6 %collective-permute-done.9.refs_2_ = bf16[32,16384]{1,0:T(8,128)(2,1)S(1)} collective-permute-done((bf16[32,16384]{1,0:T(8,128)(2,1)S(1)}, bf16[32,16384]{1,0:T(8,128)(2,1)S(1)}, u32[]{:S(2)}, u32[]{:S(2)}) %collective-permute-start.9) | collective-permute-done | bytes 1048608 | tf_op jit(solution)/shard_map/ppermute | solution.py:33
  54.5 2.3 %collective-permute-done.10.refs_3_ = bf16[32,128,128]{2,1,0:T(8,128)(2,1)S(1)} collective-permute-done((bf16[32,128,128]{2,1,0:T(8,128)(2,1)}, bf16[32,128,128]{2,1,0:T(8,128)(2,1)S(1)}, u32[]{:S(2)}, u32[]{:S(2)}) %collective-permute-start.10) | collective-permute-done | bytes 1048608 | tf_op jit(solution)/shard_map/ppermute | solution.py:33
  56.8 0.2 copy.31
  57.0 1.7 %collective-permute-start.14 = (bf16[32,128,128]{2,1,0:T(8,128)(2,1)S(1)}, bf16[32,128,128]{2,1,0:T(8,128)(2,1)S(1)}, u32[]{:S(2)}, u32[]{:S(2)}) collective-permute-start(bf16[32,128,128]{2,1,0:T(8,128)(2,1)S(1)} %bitcast.50), channel_id=1, source_target_pairs={{0,4},{4,0},{1,5},{5,1},{2,6},{6,2},{3,7},{7,3},{8,12},{12,8},{9,1... | collective-permute-start | bytes 3145736 | tf_op jit(solution)/shard_map/ppermute | solution.py:38
  58.7 0.8 collective-permute-start.18
  59.5 2.6 %collective-permute-start.12 = (bf16[64,128,128]{2,1,0:T(8,128)(2,1)S(1)}, bf16[64,128,128]{2,1,0:T(8,128)(2,1)S(1)}, u32[]{:S(2)}, u32[]{:S(2)}) collective-permute-start(bf16[64,128,128]{2,1,0:T(8,128)(2,1)S(1)} %get-tuple-element.25.refs_6_), channel_id=1, source_target_pairs={{0,1},{1,2},{2,3},{3,0},{8,11},{9,8},{10,9},{11,10},{4,5},{5,6},{6... | collective-permute-start | bytes 6291464 | tf_op jit(solution)/shard_map/ppermute | solution.py:33
  62.1 0.3 collective-permute-start.13
  62.3 12.7 %product.2.refs_2_.refs_4_.refs_6_ = f32[64,128,128]{2,1,0:T(8,128)S(1)} custom-call(s32[1024]{0:T(1024)S(1)} %pad_add_fusion.refs_9_.refs_0_, s32[1024]{0:T(1024)S(1)} %pad_add_fusion.1.refs_10_.refs_1_, bf16[128,128,128]{2,1,0:T(8,128)(2,1)S(1)} %bitcast.46, bf16[64,128,128]{2,1,0:T(8,128)(2,1)S(1)} %bitcast.55, bf16[64,128,128]{2,1,0:T(8,128)(2,1)S(1)} %bitcast.58, ...), custom_call_target="tpu_custom_call" | custom-call | flops 8589934592 | bytes 20971520 | tf_op jit(solution)/shard_map/product/pallas_call | solution.py:184
  75.0 6.7 %collective-permute-done.14.refs_2_ = bf16[32,128,128]{2,1,0:T(8,128)(2,1)S(1)} collective-permute-done((bf16[32,128,128]{2,1,0:T(8,128)(2,1)S(1)}, bf16[32,128,128]{2,1,0:T(8,128)(2,1)S(1)}, u32[]{:S(2)}, u32[]{:S(2)}) %collective-permute-start.14) | collective-permute-done | bytes 1048608 | tf_op jit(solution)/shard_map/ppermute | solution.py:38
  81.7 1.1 collective-permute-start.16
  82.9 5.0 %collective-permute-done.15.refs_3_ = bf16[32,128,128]{2,1,0:T(8,128)(2,1)S(1)} collective-permute-done((bf16[32,128,128]{2,1,0:T(8,128)(2,1)S(1)}, bf16[32,128,128]{2,1,0:T(8,128)(2,1)S(1)}, u32[]{:S(2)}, u32[]{:S(2)}) %collective-permute-start.15) | collective-permute-done | bytes 1048608 | tf_op jit(solution)/shard_map/ppermute | solution.py:38
  87.9 0.4 collective-permute-start.19
  88.4 0.3 collective-permute-start.21
  88.7 0.2 collective-permute-start.20
  88.9 0.3 collective-permute-start.22
  89.2 6.7 %product.3.refs_10_ = f32[64,128,128]{2,1,0:T(8,128)S(1)} custom-call(s32[512]{0:T(512)S(1)} %get-tuple-element.78.refs_11_.refs_0_, s32[512]{0:T(512)S(1)} %pad_add_fusion.5.refs_12_.refs_1_, bf16[128,128,128]{2,1,0:T(8,128)(2,1)S(1)} %bitcast.47, bf16[64,128,128]{2,1,0:T(8,128)(2,1)S(1)} %get-tuple-element.32.refs_3_, ...), custom_call_target="tpu_custom_call" | custom-call | flops 4294967296 | bytes 16777216 | tf_op jit(solution)/shard_map/product/pallas_call | solution.py:184
  95.8 0.8 collective-permute-done.20.refs_9_
  96.7 1.5 %collective-permute-done.22.refs_24_ = bf16[32,128,128]{2,1,0:T(8,128)(2,1)S(1)} collective-permute-done((bf16[32,128,128]{2,1,0:T(8,128)(2,1)S(1)}, bf16[32,128,128]{2,1,0:T(8,128)(2,1)S(1)}, u32[]{:S(2)}, u32[]{:S(2)}) %collective-permute-start.22) | collective-permute-done | bytes 1048608 | tf_op jit(solution)/shard_map/ppermute | solution.py:38
  98.2 11.1 %final.1 = (bf16[64,128,128]{2,1,0:T(8,128)(2,1)S(1)}, f32[16,128]{1,0:T(8,128)S(1)}) custom-call(s32[512]{0:T(512)S(1)} %get-tuple-element.77.refs_13_.refs_0_, s32[512]{0:T(512)S(1)} %pad_add_fusion.3.refs_14_.refs_1_, s32[16]{0:T(128)S(1)} %select_reduce_fusion.refs_8_.refs_2_, s32[256]{0:T(256)S(1)} %get-tuple-element.79.refs_5_.refs_3_, ...), custom_call_target="tpu_custom_call" | custom-call | flops 8589934592 | bytes 41943040 | tf_op jit(solution)/shard_map/final/pallas_call | solution.py:205
  109.3 0.7 all_to_all.6
  110.0 4.4 %all-to-all-start = ((f32[128,1,16]{2,1,0:T(1,128)}), f32[128,1,16]{2,1,0:T(1,128)S(1)}, u32[]{:S(2)}, u32[]{:S(2)}) async-start(f32[128,1,16]{2,1,0:T(1,128)} %bitcast.20), calls=%async_computation | async-start | bytes 131072 | tf_op jit(solution)/shard_map/all_to_all | solution.py:290
  114.4 2.3 %reshape.283 = bf16[1,1,64,16384]{3,2,1,0:T(8,128)(2,1)} reshape(bf16[64,128,128]{2,1,0:T(8,128)(2,1)S(1)} %get-tuple-element.36) | data formatting | bytes 4194304 | tf_op jit(solution)/shard_map/reshape | solution.py:291
  116.7 7.5 %all-to-all-done = f32[128,1,16]{2,1,0:T(1,128)S(1)} async-done(((f32[128,1,16]{2,1,0:T(1,128)}), f32[128,1,16]{2,1,0:T(1,128)S(1)}, u32[]{:S(2)}, u32[]{:S(2)}) %all-to-all-start) | async-done | bytes 8224 | tf_op jit(solution)/shard_map/all_to_all | solution.py:290
  124.2 0.7 reduce_sum.19
  (54 shorter events, 0.9 us)
Async XLA Ops:
  0.6 12.8 %copy-start.5 = (s32[1,1,8,2,256]{4,3,2,1,0:T(2,128)S(1)}, s32[1,1,8,2,256]{4,3,2,1,0:T(2,128)}, u32[]{:S(2)}) copy-start(s32[1,1,8,2,256]{4,3,2,1,0:T(2,128)} %param.9) | copy-start | bytes 49156
  0.6 13.0 %copy-start.6 = (s32[1,1,16,16,3]{3,2,4,1,0:T(8,128)S(1)}, s32[1,1,16,16,3]{3,2,4,1,0:T(8,128)}, u32[]{:S(2)}) copy-start(s32[1,1,16,16,3]{3,2,4,1,0:T(8,128)} %param.10) | copy-start | bytes 9220
  0.6 13.0 %collective-permute-start.4 = (bf16[32,128,128]{2,1,0:T(8,128)(2,1)}, bf16[32,128,128]{2,1,0:T(8,128)(2,1)}, u32[]{:S(2)}, u32[]{:S(2)}) collective-permute-start(bf16[32,128,128]{2,1,0:T(8,128)(2,1)} %bitcast.59), channel_id=1, source_target_pairs={{0,8},{8,0},{1,9},{9,1},{2,10},{10,2},{3,11},{11,3},{4,12},{12,4},... | collective-permute-start | bytes 3145736 | tf_op jit(solution)/shard_map/ppermute | solution.py:38
  2.2 14.6 %collective-permute-start.3 = (bf16[32,128,128]{2,1,0:T(8,128)(2,1)}, bf16[32,128,128]{2,1,0:T(8,128)(2,1)}, u32[]{:S(2)}, u32[]{:S(2)}) collective-permute-start(bf16[32,128,128]{2,1,0:T(8,128)(2,1)} %bitcast.60), channel_id=1, source_target_pairs={{0,32},{32,64},{64,96},{96,0},{8,104},{40,8},{72,40},{104,72},{1,3... | collective-permute-start | bytes 3145736 | tf_op jit(solution)/shard_map/ppermute | solution.py:33
  4.7 31.3 %collective-permute-start.2 = (bf16[32,128,128]{2,1,0:T(8,128)(2,1)}, bf16[32,128,128]{2,1,0:T(8,128)(2,1)}, u32[]{:S(2)}, u32[]{:S(2)}) collective-permute-start(bf16[32,128,128]{2,1,0:T(8,128)(2,1)} %bitcast.61), channel_id=1, source_target_pairs={{0,20},{4,16},{16,4},{20,0},{1,21},{5,17},{17,5},{21,1},{2,22},{6,... | collective-permute-start | bytes 3145736 | tf_op jit(solution)/shard_map/ppermute | solution.py:38
  10.7 25.2 %collective-permute-start.1 = (bf16[32,16384]{1,0:T(8,128)(2,1)}, bf16[32,16384]{1,0:T(8,128)(2,1)}, u32[]{:S(2)}, u32[]{:S(2)}) collective-permute-start(bf16[32,16384]{1,0:T(8,128)(2,1)} %dynamic-slice_bitcast_fusion), channel_id=1, source_target_pairs={{0,4},{4,0},{1,5},{5,1},{2,6},{6,2},{3,7},{7,3},{8,12},{12,8},{9,1... | collective-permute-start | bytes 3145736 | tf_op jit(solution)/shard_map/ppermute | solution.py:38
  10.7 26.0 %collective-permute-start = (bf16[64,16384]{1,0:T(8,128)(2,1)}, bf16[64,16384]{1,0:T(8,128)(2,1)S(1)}, u32[]{:S(2)}, u32[]{:S(2)}) collective-permute-start(bf16[64,16384]{1,0:T(8,128)(2,1)} %bitcast.5), channel_id=1, source_target_pairs={{0,1},{1,2},{2,3},{3,0},{8,11},{9,8},{10,9},{11,10},{4,5},{5,6},{6... | collective-permute-start | bytes 6291464 | tf_op jit(solution)/shard_map/ppermute | solution.py:33
  13.7 22.3 %collective-permute-start.5 = (bf16[32,128,128]{2,1,0:T(8,128)(2,1)}, bf16[32,128,128]{2,1,0:T(8,128)(2,1)S(1)}, u32[]{:S(2)}, u32[]{:S(2)}) collective-permute-start(bf16[32,128,128]{2,1,0:T(8,128)(2,1)} %collective-permute-done.4.refs_13_), channel_id=1, source_target_pairs={{0,32},{32,64},{64,96},{96,0},{8,104},{40,8},{72,40},{104,72},{1,3... | collective-permute-start | bytes 3145736 | tf_op jit(solution)/shard_map/ppermute | solution.py:33
  16.8 19.2 %collective-permute-start.6 = (bf16[32,128,128]{2,1,0:T(8,128)(2,1)}, bf16[32,128,128]{2,1,0:T(8,128)(2,1)}, u32[]{:S(2)}, u32[]{:S(2)}) collective-permute-start(bf16[32,128,128]{2,1,0:T(8,128)(2,1)} %collective-permute-done.3.refs_3_), channel_id=1, source_target_pairs={{0,8},{8,0},{1,9},{9,1},{2,10},{10,2},{3,11},{11,3},{4,12},{12,4},... | collective-permute-start | bytes 3145736 | tf_op jit(solution)/shard_map/ppermute | solution.py:38
  19.0 2.8 %copy-start.3 = (bf16[1,1,128,16384]{3,2,1,0:T(8,128)(2,1)S(1)}, bf16[1,1,128,16384]{3,2,1,0:T(8,128)(2,1)}, u32[]{:S(2)}) copy-start(bf16[1,1,128,16384]{3,2,1,0:T(8,128)(2,1)} %param.6) | copy-start | bytes 12582916
  38.2 5.8 %collective-permute-start.7 = (bf16[32,128,128]{2,1,0:T(8,128)(2,1)S(1)}, bf16[32,128,128]{2,1,0:T(8,128)(2,1)S(1)}, u32[]{:S(2)}, u32[]{:S(2)}) collective-permute-start(bf16[32,128,128]{2,1,0:T(8,128)(2,1)S(1)} %bitcast.64), channel_id=1, source_target_pairs={{0,8},{8,0},{1,9},{9,1},{2,10},{10,2},{3,11},{11,3},{4,12},{12,4},... | collective-permute-start | bytes 3145736 | tf_op jit(solution)/shard_map/ppermute | solution.py:38
  39.1 5.4 %collective-permute-start.8 = (bf16[32,128,128]{2,1,0:T(8,128)(2,1)}, bf16[32,128,128]{2,1,0:T(8,128)(2,1)S(1)}, u32[]{:S(2)}, u32[]{:S(2)}) collective-permute-start(bf16[32,128,128]{2,1,0:T(8,128)(2,1)} %get-tuple-element.21), channel_id=1, source_target_pairs={{0,8},{8,0},{1,9},{9,1},{2,10},{10,2},{3,11},{11,3},{4,12},{12,4},... | collective-permute-start | bytes 3145736 | tf_op jit(solution)/shard_map/ppermute | solution.py:38
  39.8 3.6 %copy-start.4 = (bf16[1,1,64,16384]{3,2,1,0:T(8,128)(2,1)S(1)}, bf16[1,1,64,16384]{3,2,1,0:T(8,128)(2,1)}, u32[]{:S(2)}) copy-start(bf16[1,1,64,16384]{3,2,1,0:T(8,128)(2,1)} %param.8) | copy-start | bytes 6291460
  39.8 17.0 %collective-permute-start.11 = (bf16[64,128,128]{2,1,0:T(8,128)(2,1)S(1)}, bf16[64,128,128]{2,1,0:T(8,128)(2,1)S(1)}, u32[]{:S(2)}, u32[]{:S(2)}) collective-permute-start(bf16[64,128,128]{2,1,0:T(8,128)(2,1)S(1)} %bitcast.57), channel_id=1, source_target_pairs={{0,8},{8,0},{1,9},{9,1},{2,10},{10,2},{3,11},{11,3},{4,12},{12,4},... | collective-permute-start | bytes 6291464 | tf_op jit(solution)/shard_map/ppermute | solution.py:38
  40.4 14.1 %collective-permute-start.9 = (bf16[32,16384]{1,0:T(8,128)(2,1)S(1)}, bf16[32,16384]{1,0:T(8,128)(2,1)S(1)}, u32[]{:S(2)}, u32[]{:S(2)}) collective-permute-start(bf16[32,16384]{1,0:T(8,128)(2,1)S(1)} %constant_dynamic-slice_fusion.8), channel_id=1, source_target_pairs={{0,1},{1,2},{2,3},{3,0},{8,11},{9,8},{10,9},{11,10},{4,5},{5,6},{6... | collective-permute-start | bytes 3145736 | tf_op jit(solution)/shard_map/ppermute | solution.py:33
  42.7 14.0 %collective-permute-start.10 = (bf16[32,128,128]{2,1,0:T(8,128)(2,1)}, bf16[32,128,128]{2,1,0:T(8,128)(2,1)S(1)}, u32[]{:S(2)}, u32[]{:S(2)}) collective-permute-start(bf16[32,128,128]{2,1,0:T(8,128)(2,1)} %get-tuple-element.23.refs_14_), channel_id=1, source_target_pairs={{0,32},{32,64},{64,96},{96,0},{8,104},{40,8},{72,40},{104,72},{1,3... | collective-permute-start | bytes 3145736 | tf_op jit(solution)/shard_map/ppermute | solution.py:33
  56.8 18.2 %copy-start = (bf16[32,128,128]{2,1,0:T(8,128)(2,1)}, bf16[32,128,128]{2,1,0:T(8,128)(2,1)S(1)}, u32[]{:S(2)}) copy-start(bf16[32,128,128]{2,1,0:T(8,128)(2,1)S(1)} %get-tuple-element.28.refs_18_) | copy-start | bytes 3145732
  57.0 24.7 %collective-permute-start.14 = (bf16[32,128,128]{2,1,0:T(8,128)(2,1)S(1)}, bf16[32,128,128]{2,1,0:T(8,128)(2,1)S(1)}, u32[]{:S(2)}, u32[]{:S(2)}) collective-permute-start(bf16[32,128,128]{2,1,0:T(8,128)(2,1)S(1)} %bitcast.50), channel_id=1, source_target_pairs={{0,4},{4,0},{1,5},{5,1},{2,6},{6,2},{3,7},{7,3},{8,12},{12,8},{9,1... | collective-permute-start | bytes 3145736 | tf_op jit(solution)/shard_map/ppermute | solution.py:38
  58.7 24.1 %collective-permute-start.18 = (bf16[32,128,128]{2,1,0:T(8,128)(2,1)S(1)}, bf16[32,128,128]{2,1,0:T(8,128)(2,1)S(1)}, u32[]{:S(2)}, u32[]{:S(2)}) collective-permute-start(bf16[32,128,128]{2,1,0:T(8,128)(2,1)S(1)} %get-tuple-element.28.refs_18_), channel_id=1, source_target_pairs={{0,8},{8,0},{1,9},{9,1},{2,10},{10,2},{3,11},{11,3},{4,12},{12,4},... | collective-permute-start | bytes 3145736 | tf_op jit(solution)/shard_map/ppermute | solution.py:38
  59.5 28.4 %collective-permute-start.12 = (bf16[64,128,128]{2,1,0:T(8,128)(2,1)S(1)}, bf16[64,128,128]{2,1,0:T(8,128)(2,1)S(1)}, u32[]{:S(2)}, u32[]{:S(2)}) collective-permute-start(bf16[64,128,128]{2,1,0:T(8,128)(2,1)S(1)} %get-tuple-element.25.refs_6_), channel_id=1, source_target_pairs={{0,1},{1,2},{2,3},{3,0},{8,11},{9,8},{10,9},{11,10},{4,5},{5,6},{6... | collective-permute-start | bytes 6291464 | tf_op jit(solution)/shard_map/ppermute | solution.py:33
  62.1 25.8 %collective-permute-start.13 = (bf16[64,128,128]{2,1,0:T(8,128)(2,1)S(1)}, bf16[64,128,128]{2,1,0:T(8,128)(2,1)S(1)}, u32[]{:S(2)}, u32[]{:S(2)}) collective-permute-start(bf16[64,128,128]{2,1,0:T(8,128)(2,1)S(1)} %get-tuple-element.26.refs_20_), channel_id=1, source_target_pairs={{0,32},{32,64},{64,96},{96,0},{8,104},{40,8},{72,40},{104,72},{1,3... | collective-permute-start | bytes 6291464 | tf_op jit(solution)/shard_map/ppermute | solution.py:33
  62.3 25.6 %collective-permute-start.15 = (bf16[32,128,128]{2,1,0:T(8,128)(2,1)S(1)}, bf16[32,128,128]{2,1,0:T(8,128)(2,1)S(1)}, u32[]{:S(2)}, u32[]{:S(2)}) collective-permute-start(bf16[32,128,128]{2,1,0:T(8,128)(2,1)S(1)} %get-tuple-element.28.refs_18_), channel_id=1, source_target_pairs={{0,20},{4,16},{16,4},{20,0},{1,21},{5,17},{17,5},{21,1},{2,22},{6,... | collective-permute-start | bytes 3145736 | tf_op jit(solution)/shard_map/ppermute | solution.py:38
  81.7 6.2 %collective-permute-start.16 = (bf16[32,128,128]{2,1,0:T(8,128)(2,1)S(1)}, bf16[32,128,128]{2,1,0:T(8,128)(2,1)S(1)}, u32[]{:S(2)}, u32[]{:S(2)}) collective-permute-start(bf16[32,128,128]{2,1,0:T(8,128)(2,1)S(1)} %get-tuple-element.30.refs_4_), channel_id=1, source_target_pairs={{0,8},{8,0},{1,9},{9,1},{2,10},{10,2},{3,11},{11,3},{4,12},{12,4},... | collective-permute-start | bytes 3145736 | tf_op jit(solution)/shard_map/ppermute | solution.py:38
  82.8 5.1 %collective-permute-start.17 = (bf16[32,128,128]{2,1,0:T(8,128)(2,1)S(1)}, bf16[32,128,128]{2,1,0:T(8,128)(2,1)S(1)}, u32[]{:S(2)}, u32[]{:S(2)}) collective-permute-start(bf16[32,128,128]{2,1,0:T(8,128)(2,1)S(1)} %get-tuple-element.31.refs_15_), channel_id=1, source_target_pairs={{0,8},{8,0},{1,9},{9,1},{2,10},{10,2},{3,11},{11,3},{4,12},{12,4},... | collective-permute-start | bytes 3145736 | tf_op jit(solution)/shard_map/ppermute | solution.py:38
  87.9 10.2 %collective-permute-start.19 = (bf16[64,128,128]{2,1,0:T(8,128)(2,1)S(1)}, bf16[64,128,128]{2,1,0:T(8,128)(2,1)S(1)}, u32[]{:S(2)}, u32[]{:S(2)}) collective-permute-start(bf16[64,128,128]{2,1,0:T(8,128)(2,1)S(1)} %get-tuple-element.32.refs_3_), channel_id=1, source_target_pairs={{0,8},{8,0},{1,9},{9,1},{2,10},{10,2},{3,11},{11,3},{4,12},{12,4},... | collective-permute-start | bytes 6291464 | tf_op jit(solution)/shard_map/ppermute | solution.py:38
  88.4 9.8 %collective-permute-start.21 = (bf16[64,128,128]{2,1,0:T(8,128)(2,1)S(1)}, bf16[64,128,128]{2,1,0:T(8,128)(2,1)S(1)}, u32[]{:S(2)}, u32[]{:S(2)}) collective-permute-start(bf16[64,128,128]{2,1,0:T(8,128)(2,1)S(1)} %get-tuple-element.34.refs_21_), channel_id=1, source_target_pairs={{0,8},{8,0},{1,9},{9,1},{2,10},{10,2},{3,11},{11,3},{4,12},{12,4},... | collective-permute-start | bytes 6291464 | tf_op jit(solution)/shard_map/ppermute | solution.py:38
  88.7 8.0 %collective-permute-start.20 = (bf16[32,128,128]{2,1,0:T(8,128)(2,1)S(1)}, bf16[32,128,128]{2,1,0:T(8,128)(2,1)S(1)}, u32[]{:S(2)}, u32[]{:S(2)}) collective-permute-start(bf16[32,128,128]{2,1,0:T(8,128)(2,1)S(1)} %get-tuple-element.33.refs_8_), channel_id=1, source_target_pairs={{0,8},{8,0},{1,9},{9,1},{2,10},{10,2},{3,11},{11,3},{4,12},{12,4},... | collective-permute-start | bytes 3145736 | tf_op jit(solution)/shard_map/ppermute | solution.py:38
  88.9 9.3 %copy-start.1 = (bf16[32,128,128]{2,1,0:T(8,128)(2,1)S(1)}, bf16[32,128,128]{2,1,0:T(8,128)(2,1)}, u32[]{:S(2)}) copy-start(bf16[32,128,128]{2,1,0:T(8,128)(2,1)} %copy-done) | copy-start | bytes 3145732
  88.9 9.3 %copy-start.2 = (bf16[1,32,128,128]{3,2,1,0:T(8,128)(2,1)S(1)}, bf16[1,32,128,128]{3,2,1,0:T(8,128)(2,1)}, u32[]{:S(2)}) copy-start(bf16[1,32,128,128]{3,2,1,0:T(8,128)(2,1)} %param.11) | copy-start | bytes 3145732
  88.9 9.3 %collective-permute-start.22 = (bf16[32,128,128]{2,1,0:T(8,128)(2,1)S(1)}, bf16[32,128,128]{2,1,0:T(8,128)(2,1)S(1)}, u32[]{:S(2)}, u32[]{:S(2)}) collective-permute-start(bf16[32,128,128]{2,1,0:T(8,128)(2,1)S(1)} %get-tuple-element.35.refs_23_), channel_id=1, source_target_pairs={{0,8},{8,0},{1,9},{9,1},{2,10},{10,2},{3,11},{11,3},{4,12},{12,4},... | collective-permute-start | bytes 3145736 | tf_op jit(solution)/shard_map/ppermute | solution.py:38
  110.0 14.3 %all-to-all-start = ((f32[128,1,16]{2,1,0:T(1,128)}), f32[128,1,16]{2,1,0:T(1,128)S(1)}, u32[]{:S(2)}, u32[]{:S(2)}) async-start(f32[128,1,16]{2,1,0:T(1,128)} %bitcast.20), calls=%async_computation | async-start | bytes 131072 | tf_op jit(solution)/shard_map/all_to_all | solution.py:290

commit v5 on v4

--- a/solution.py
+++ b/solution.py
@@ -270,10 +270,10 @@
     work = [tile, row, col, who, *[index for both in plan for index in both], a_tiles, share, sbnear_a]
     near, pair, bpair, bnear_a, bnear_b = gate([near, pair, bpair, bnear_a, bnear_b], work)
     far, bfar = around(half_of(near, core), "y"), around(bnear_a, "x")
-    near, pair = matrices(near), matrices(pair)
     spair, sbpair, snear = swapped(pair), swapped(bpair), swapped(near)
-    both, bboth = jnp.concatenate([pair, spair]), jnp.concatenate([bpair, sbpair])
-    both, bboth, far, bfar, bnear_b = gate([both, bboth, far, bfar, bnear_b], [snear, square])
+    both, bboth = matrices(jnp.concatenate([pair, spair])), jnp.concatenate([bpair, sbpair])
+    near, snear = matrices(near), matrices(snear)
+    both, bboth, far, bfar, bnear_b = gate([both, bboth, far, bfar, bnear_b], [near, snear, square])
     far = matrices(far)
     pnear, bpnear = around(both, "y"), around(bboth, "x")
     pfar, bpfar = across(far, link), across(bfar, zz)

time: 125 us -> 123 us (0.984)
  waiting for transfers between devices: 48.7 us -> 45.6 us
    ppermute x7, waiting for transfers between devices: 14.1 us -> 11.5 us  [around(): lax.ppermute(value, ('x', 'core') if axis == 'x' else ('core', axis), pairs)]
    unnamed x0 -> x1, other arithmetic: none -> 1.38 us
    unnamed x20 -> x25, local copies, waits for them, and re-layouts: 6.92 us -> 6.61 us
  transfers between devices with their start and end apart: 24 -> 24, of which waited for: 11 -> 10; matrix products, arithmetic and copies ran while one was open for 9% -> 11% of each run, Pallas kernels for 15% -> 16%
where the time goes in v5:
time: 123 us
  waiting for transfers between devices  45.6 us (37%)
  Pallas kernels  30.4 us (25%)
  starting transfers between devices  29.6 us (24%)
  local copies, waits for them, and re-layouts  12.3 us (10%)
  other arithmetic  3.76 us (3%)
    ppermute x16, waiting for transfers between devices, across(): return lax.ppermute(value, axes, [(i, count - 1 - i) for i in range(count)])  26.5 us
    pallas_call x2, Pallas kernels, product(): pl.pallas_call(lambda *refs: product_kernel(sizes, count, acc is None, *r...  19.4 us
    ppermute x16, starting transfers between devices, across(): return lax.ppermute(value, axes, [(i, count - 1 - i) for i in range(count)])  13.4 us
    ppermute x7, starting transfers between devices, around(): lax.ppermute(value, ('x', 'core') if axis == 'x' else ('core', axis), pairs)  11.8 us
    ppermute x7, waiting for transfers between devices, around(): lax.ppermute(value, ('x', 'core') if axis == 'x' else ('core', axis), pairs)  11.5 us
    pallas_call x1, Pallas kernels, final(): pl.pallas_call(lambda *refs: final_kernel(sizes, count, slab_sizes, *refs...  11.1 us
    all_to_all x1, waiting for transfers between devices, body(): lax.all_to_all(grid.reshape(128, 16), ROWS + BLK, split_axis=0, concat_ax...  7.57 us
    unnamed x25, local copies, waits for them, and re-layouts  6.61 us
  transfers between devices with their start and end apart: 24, of which 10 were waited for; matrix products, arithmetic and copies ran while one was open for 11% of the time, Pallas kernels for 16%

profile of v5, /device:TPU:1, one launch (start us, length us, event | category | flops | bytes accessed | tf_op | source)
XLA Modules:
  0.0 122.7 jit_solution(1638961212986738301)
XLA Ops:
  0.6 1.5 %collective-permute-start.4 = (bf16[32,128,128]{2,1,0:T(8,128)(2,1)}, bf16[32,128,128]{2,1,0:T(8,128)(2,1)}, u32[]{:S(2)}, u32[]{:S(2)}) collective-permute-start(bf16[32,128,128]{2,1,0:T(8,128)(2,1)} %bitcast.65), channel_id=1, source_target_pairs={{0,8},{8,0},{1,9},{9,1},{2,10},{10,2},{3,11},{11,3},{4,12},{12,4},... | collective-permute-start | bytes 3145736 | tf_op jit(solution)/shard_map/ppermute | solution.py:38
  2.2 2.6 %collective-permute-start.3 = (bf16[32,128,128]{2,1,0:T(8,128)(2,1)}, bf16[32,128,128]{2,1,0:T(8,128)(2,1)}, u32[]{:S(2)}, u32[]{:S(2)}) collective-permute-start(bf16[32,128,128]{2,1,0:T(8,128)(2,1)} %bitcast.66), channel_id=1, source_target_pairs={{0,32},{32,64},{64,96},{96,0},{8,104},{40,8},{72,40},{104,72},{1,3... | collective-permute-start | bytes 3145736 | tf_op jit(solution)/shard_map/ppermute | solution.py:33
  4.7 3.8 %collective-permute-start.2 = (bf16[32,128,128]{2,1,0:T(8,128)(2,1)}, bf16[32,128,128]{2,1,0:T(8,128)(2,1)}, u32[]{:S(2)}, u32[]{:S(2)}) collective-permute-start(bf16[32,128,128]{2,1,0:T(8,128)(2,1)} %bitcast.67), channel_id=1, source_target_pairs={{0,20},{4,16},{16,4},{20,0},{1,21},{5,17},{17,5},{21,1},{2,22},{6,... | collective-permute-start | bytes 3145736 | tf_op jit(solution)/shard_map/ppermute | solution.py:38
  8.5 2.3 %dynamic-slice_bitcast_fusion = bf16[32,16384]{1,0:T(8,128)(2,1)} fusion(bf16[1,64,16384]{2,1,0:T(8,128)(2,1)} %param.7, s32[]{:T(128)S(6)} %select_n.239), kind=kLoop, calls=%fused_computation.2 | loop fusion | bytes 2097156 | tf_op jit(solution)/shard_map/dynamic_slice | solution.py:46
  10.7 2.7 %collective-permute-start = (bf16[64,16384]{1,0:T(8,128)(2,1)}, bf16[64,16384]{1,0:T(8,128)(2,1)S(1)}, u32[]{:S(2)}, u32[]{:S(2)}) collective-permute-start(bf16[64,16384]{1,0:T(8,128)(2,1)} %bitcast.5), channel_id=1, source_target_pairs={{0,1},{1,2},{2,3},{3,0},{8,11},{9,8},{10,9},{11,10},{4,5},{5,6},{6... | collective-permute-start | bytes 6291464 | tf_op jit(solution)/shard_map/ppermute | solution.py:33
  13.7 0.6 collective-permute-start.5
  14.3 2.5 %collective-permute-done.3.refs_3_ = bf16[32,128,128]{2,1,0:T(8,128)(2,1)} collective-permute-done((bf16[32,128,128]{2,1,0:T(8,128)(2,1)}, bf16[32,128,128]{2,1,0:T(8,128)(2,1)}, u32[]{:S(2)}, u32[]{:S(2)}) %collective-permute-start.3) | collective-permute-done | bytes 1048608 | tf_op jit(solution)/shard_map/ppermute | solution.py:33
  16.8 1.8 %collective-permute-start.6 = (bf16[32,128,128]{2,1,0:T(8,128)(2,1)}, bf16[32,128,128]{2,1,0:T(8,128)(2,1)}, u32[]{:S(2)}, u32[]{:S(2)}) collective-permute-start(bf16[32,128,128]{2,1,0:T(8,128)(2,1)} %collective-permute-done.3.refs_3_), channel_id=1, source_target_pairs={{0,8},{8,0},{1,9},{9,1},{2,10},{10,2},{3,11},{11,3},{4,12},{12,4},... | collective-permute-start | bytes 3145736 | tf_op jit(solution)/shard_map/ppermute | solution.py:38
  19.0 2.3 %copy.27 = bf16[8,8,128,128]{3,2,1,0:T(8,128)(2,1)S(1)} copy(bf16[8,8,128,128]{3,1,2,0:T(8,128)(2,1)} %bitcast.29) | data formatting | bytes 4194304
  21.3 0.5 copy-done.5
  21.8 1.2 %copy.26 = bf16[16,8,128,128]{3,2,1,0:T(8,128)(2,1)S(1)} copy(bf16[16,8,128,128]{3,1,2,0:T(8,128)(2,1)S(1)} %bitcast.69) | data formatting | bytes 8388608
  23.2 12.7 %collective-permute-done.1.refs_1_ = bf16[32,16384]{1,0:T(8,128)(2,1)} collective-permute-done((bf16[32,16384]{1,0:T(8,128)(2,1)}, bf16[32,16384]{1,0:T(8,128)(2,1)}, u32[]{:S(2)}, u32[]{:S(2)}) %collective-permute-start.1) | collective-permute-done | bytes 1048608 | tf_op jit(solution)/shard_map/ppermute | solution.py:38
  36.0 0.8 collective-permute-done.refs_0_
  36.8 0.8 collective-permute-start.7
  37.6 0.5 collective-permute-start.11
  38.2 2.3 %collective-permute-start.9 = (bf16[32,16384]{1,0:T(8,128)(2,1)S(1)}, bf16[32,16384]{1,0:T(8,128)(2,1)S(1)}, u32[]{:S(2)}, u32[]{:S(2)}) collective-permute-start(bf16[32,16384]{1,0:T(8,128)(2,1)S(1)} %constant_dynamic-slice_fusion.8), channel_id=1, source_target_pairs={{0,1},{1,2},{2,3},{3,0},{8,11},{9,8},{10,9},{11,10},{4,5},{5,6},{6... | collective-permute-start | bytes 3145736 | tf_op jit(solution)/shard_map/ppermute | solution.py:33
  40.4 0.8 collective-permute-start.10
  41.2 0.6 copy.31
  41.8 0.6 copy.29
  42.4 1.4 %maximum_bitcast_fusion = bf16[8,8,128,128]{3,1,2,0:T(8,128)(2,1)S(1)} fusion(bf16[32,16384]{1,0:T(8,128)(2,1)S(1)} %collective-permute-done.7, bf16[32,16384]{1,0:T(8,128)(2,1)} %get-tuple-element.20), kind=kLoop, calls=%fused_computation | loop fusion | flops 4194304 | bytes 4194304
  43.8 0.6 copy.28
  44.4 1.4 %pad_maximum_fusion.refs_1_ = bf16[64,128,128]{2,1,0:T(8,128)(2,1)S(1)} fusion(bf16[32,128,128]{2,1,0:T(8,128)(2,1)S(1)} %collective-permute-done.8, bf16[32,128,128]{2,1,0:T(8,128)(2,1)} %get-tuple-element.21), kind=kLoop, calls=%fused_computation.1 | loop fusion | flops 1048576 | bytes 4194304 | tf_op jit(solution)/shard_map/concatenate | solution.py:274
  45.8 0.6 copy.30
  46.4 5.8 %collective-permute-done.9.refs_2_ = bf16[32,16384]{1,0:T(8,128)(2,1)S(1)} collective-permute-done((bf16[32,16384]{1,0:T(8,128)(2,1)S(1)}, bf16[32,16384]{1,0:T(8,128)(2,1)S(1)}, u32[]{:S(2)}, u32[]{:S(2)}) %collective-permute-start.9) | collective-permute-done | bytes 1048608 | tf_op jit(solution)/shard_map/ppermute | solution.py:33
  52.2 2.4 %collective-permute-done.10.refs_3_ = bf16[32,128,128]{2,1,0:T(8,128)(2,1)S(1)} collective-permute-done((bf16[32,128,128]{2,1,0:T(8,128)(2,1)}, bf16[32,128,128]{2,1,0:T(8,128)(2,1)S(1)}, u32[]{:S(2)}, u32[]{:S(2)}) %collective-permute-start.10) | collective-permute-done | bytes 1048608 | tf_op jit(solution)/shard_map/ppermute | solution.py:33
  54.6 0.2 copy.32
  54.8 1.5 %collective-permute-start.14 = (bf16[32,128,128]{2,1,0:T(8,128)(2,1)S(1)}, bf16[32,128,128]{2,1,0:T(8,128)(2,1)S(1)}, u32[]{:S(2)}, u32[]{:S(2)}) collective-permute-start(bf16[32,128,128]{2,1,0:T(8,128)(2,1)S(1)} %bitcast.53), channel_id=1, source_target_pairs={{0,4},{4,0},{1,5},{5,1},{2,6},{6,2},{3,7},{7,3},{8,12},{12,8},{9,1... | collective-permute-start | bytes 3145736 | tf_op jit(solution)/shard_map/ppermute | solution.py:38
  56.4 0.8 collective-permute-start.18
  57.2 2.6 %collective-permute-start.12 = (bf16[64,128,128]{2,1,0:T(8,128)(2,1)S(1)}, bf16[64,128,128]{2,1,0:T(8,128)(2,1)S(1)}, u32[]{:S(2)}, u32[]{:S(2)}) collective-permute-start(bf16[64,128,128]{2,1,0:T(8,128)(2,1)S(1)} %get-tuple-element.25.refs_6_), channel_id=1, source_target_pairs={{0,1},{1,2},{2,3},{3,0},{8,11},{9,8},{10,9},{11,10},{4,5},{5,6},{6... | collective-permute-start | bytes 6291464 | tf_op jit(solution)/shard_map/ppermute | solution.py:33
  59.8 0.3 collective-permute-start.13
  60.0 12.7 %product.2.refs_2_.refs_4_.refs_6_ = f32[64,128,128]{2,1,0:T(8,128)S(1)} custom-call(s32[1024]{0:T(1024)S(1)} %pad_add_fusion.refs_9_.refs_0_, s32[1024]{0:T(1024)S(1)} %pad_add_fusion.1.refs_10_.refs_1_, bf16[128,128,128]{2,1,0:T(8,128)(2,1)S(1)} %bitcast.49, bf16[64,128,128]{2,1,0:T(8,128)(2,1)S(1)} %bitcast.58, bf16[64,128,128]{2,1,0:T(8,128)(2,1)S(1)} %bitcast.60, ...), custom_call_target="tpu_custom_call" | custom-call | flops 8589934592 | bytes 20971520 | tf_op jit(solution)/shard_map/product/pallas_call | solution.py:184
  72.7 6.5 %collective-permute-done.14.refs_2_ = bf16[32,128,128]{2,1,0:T(8,128)(2,1)S(1)} collective-permute-done((bf16[32,128,128]{2,1,0:T(8,128)(2,1)S(1)}, bf16[32,128,128]{2,1,0:T(8,128)(2,1)S(1)}, u32[]{:S(2)}, u32[]{:S(2)}) %collective-permute-start.14) | collective-permute-done | bytes 1048608 | tf_op jit(solution)/shard_map/ppermute | solution.py:38
  79.2 1.3 %collective-permute-start.16 = (bf16[32,128,128]{2,1,0:T(8,128)(2,1)S(1)}, bf16[32,128,128]{2,1,0:T(8,128)(2,1)S(1)}, u32[]{:S(2)}, u32[]{:S(2)}) collective-permute-start(bf16[32,128,128]{2,1,0:T(8,128)(2,1)S(1)} %get-tuple-element.30.refs_4_), channel_id=1, source_target_pairs={{0,8},{8,0},{1,9},{9,1},{2,10},{10,2},{3,11},{11,3},{4,12},{12,4},... | collective-permute-start | bytes 3145736 | tf_op jit(solution)/shard_map/ppermute | solution.py:38
  80.5 0.3 collective-permute-start.17
  80.8 4.8 %collective-permute-done.15.refs_3_ = bf16[32,128,128]{2,1,0:T(8,128)(2,1)S(1)} collective-permute-done((bf16[32,128,128]{2,1,0:T(8,128)(2,1)S(1)}, bf16[32,128,128]{2,1,0:T(8,128)(2,1)S(1)}, u32[]{:S(2)}, u32[]{:S(2)}) %collective-permute-start.15) | collective-permute-done | bytes 1048608 | tf_op jit(solution)/shard_map/ppermute | solution.py:38
  85.6 0.4 collective-permute-start.19
  86.1 0.1 collective-permute-start.21
  86.2 0.4 collective-permute-start.20
  86.6 0.1 collective-permute-start.22
  86.7 6.7 %product.3.refs_10_ = f32[64,128,128]{2,1,0:T(8,128)S(1)} custom-call(s32[512]{0:T(512)S(1)} %get-tuple-element.78.refs_11_.refs_0_, s32[512]{0:T(512)S(1)} %pad_add_fusion.5.refs_12_.refs_1_, bf16[128,128,128]{2,1,0:T(8,128)(2,1)S(1)} %bitcast.50, bf16[64,128,128]{2,1,0:T(8,128)(2,1)S(1)} %get-tuple-element.32.refs_3_, ...), custom_call_target="tpu_custom_call" | custom-call | flops 4294967296 | bytes 16777216 | tf_op jit(solution)/shard_map/product/pallas_call | solution.py:184
  93.4 1.0 collective-permute-done.20.refs_9_
  94.4 1.5 %collective-permute-done.22.refs_24_ = bf16[32,128,128]{2,1,0:T(8,128)(2,1)S(1)} collective-permute-done((bf16[32,128,128]{2,1,0:T(8,128)(2,1)S(1)}, bf16[32,128,128]{2,1,0:T(8,128)(2,1)S(1)}, u32[]{:S(2)}, u32[]{:S(2)}) %collective-permute-start.22) | collective-permute-done | bytes 1048608 | tf_op jit(solution)/shard_map/ppermute | solution.py:38
  95.9 11.1 %final.1 = (bf16[64,128,128]{2,1,0:T(8,128)(2,1)S(1)}, f32[16,128]{1,0:T(8,128)S(1)}) custom-call(s32[512]{0:T(512)S(1)} %get-tuple-element.77.refs_13_.refs_0_, s32[512]{0:T(512)S(1)} %pad_add_fusion.3.refs_14_.refs_1_, s32[16]{0:T(128)S(1)} %select_reduce_fusion.refs_8_.refs_2_, s32[256]{0:T(256)S(1)} %get-tuple-element.79.refs_5_.refs_3_, ...), custom_call_target="tpu_custom_call" | custom-call | flops 8589934592 | bytes 41943040 | tf_op jit(solution)/shard_map/final/pallas_call | solution.py:205
  107.0 0.7 all_to_all.6
  107.7 4.5 %all-to-all-start = ((f32[128,1,16]{2,1,0:T(1,128)}), f32[128,1,16]{2,1,0:T(1,128)S(1)}, u32[]{:S(2)}, u32[]{:S(2)}) async-start(f32[128,1,16]{2,1,0:T(1,128)} %bitcast.20), calls=%async_computation | async-start | bytes 131072 | tf_op jit(solution)/shard_map/all_to_all | solution.py:290
  112.1 2.3 %reshape.287 = bf16[1,1,64,16384]{3,2,1,0:T(8,128)(2,1)} reshape(bf16[64,128,128]{2,1,0:T(8,128)(2,1)S(1)} %get-tuple-element.36) | data formatting | bytes 4194304 | tf_op jit(solution)/shard_map/reshape | solution.py:291
  114.4 7.6 %all-to-all-done = f32[128,1,16]{2,1,0:T(1,128)S(1)} async-done(((f32[128,1,16]{2,1,0:T(1,128)}), f32[128,1,16]{2,1,0:T(1,128)S(1)}, u32[]{:S(2)}, u32[]{:S(2)}) %all-to-all-start) | async-done | bytes 8224 | tf_op jit(solution)/shard_map/all_to_all | solution.py:290
  122.0 0.7 reduce_sum.19
  (59 shorter events, 0.9 us)
Async XLA Ops:
  0.6 12.8 %copy-start.7 = (s32[1,1,8,2,256]{4,3,2,1,0:T(2,128)S(1)}, s32[1,1,8,2,256]{4,3,2,1,0:T(2,128)}, u32[]{:S(2)}) copy-start(s32[1,1,8,2,256]{4,3,2,1,0:T(2,128)} %param.9) | copy-start | bytes 49156
  0.6 13.0 %copy-start.8 = (s32[1,1,16,16,3]{3,2,4,1,0:T(8,128)S(1)}, s32[1,1,16,16,3]{3,2,4,1,0:T(8,128)}, u32[]{:S(2)}) copy-start(s32[1,1,16,16,3]{3,2,4,1,0:T(8,128)} %param.10) | copy-start | bytes 9220
  0.6 13.0 %collective-permute-start.4 = (bf16[32,128,128]{2,1,0:T(8,128)(2,1)}, bf16[32,128,128]{2,1,0:T(8,128)(2,1)}, u32[]{:S(2)}, u32[]{:S(2)}) collective-permute-start(bf16[32,128,128]{2,1,0:T(8,128)(2,1)} %bitcast.65), channel_id=1, source_target_pairs={{0,8},{8,0},{1,9},{9,1},{2,10},{10,2},{3,11},{11,3},{4,12},{12,4},... | collective-permute-start | bytes 3145736 | tf_op jit(solution)/shard_map/ppermute | solution.py:38
  2.2 14.6 %collective-permute-start.3 = (bf16[32,128,128]{2,1,0:T(8,128)(2,1)}, bf16[32,128,128]{2,1,0:T(8,128)(2,1)}, u32[]{:S(2)}, u32[]{:S(2)}) collective-permute-start(bf16[32,128,128]{2,1,0:T(8,128)(2,1)} %bitcast.66), channel_id=1, source_target_pairs={{0,32},{32,64},{64,96},{96,0},{8,104},{40,8},{72,40},{104,72},{1,3... | collective-permute-start | bytes 3145736 | tf_op jit(solution)/shard_map/ppermute | solution.py:33
  4.7 31.3 %collective-permute-start.2 = (bf16[32,128,128]{2,1,0:T(8,128)(2,1)}, bf16[32,128,128]{2,1,0:T(8,128)(2,1)}, u32[]{:S(2)}, u32[]{:S(2)}) collective-permute-start(bf16[32,128,128]{2,1,0:T(8,128)(2,1)} %bitcast.67), channel_id=1, source_target_pairs={{0,20},{4,16},{16,4},{20,0},{1,21},{5,17},{17,5},{21,1},{2,22},{6,... | collective-permute-start | bytes 3145736 | tf_op jit(solution)/shard_map/ppermute | solution.py:38
  10.7 25.2 %collective-permute-start.1 = (bf16[32,16384]{1,0:T(8,128)(2,1)}, bf16[32,16384]{1,0:T(8,128)(2,1)}, u32[]{:S(2)}, u32[]{:S(2)}) collective-permute-start(bf16[32,16384]{1,0:T(8,128)(2,1)} %dynamic-slice_bitcast_fusion), channel_id=1, source_target_pairs={{0,4},{4,0},{1,5},{5,1},{2,6},{6,2},{3,7},{7,3},{8,12},{12,8},{9,1... | collective-permute-start | bytes 3145736 | tf_op jit(solution)/shard_map/ppermute | solution.py:38
  10.7 26.0 %collective-permute-start = (bf16[64,16384]{1,0:T(8,128)(2,1)}, bf16[64,16384]{1,0:T(8,128)(2,1)S(1)}, u32[]{:S(2)}, u32[]{:S(2)}) collective-permute-start(bf16[64,16384]{1,0:T(8,128)(2,1)} %bitcast.5), channel_id=1, source_target_pairs={{0,1},{1,2},{2,3},{3,0},{8,11},{9,8},{10,9},{11,10},{4,5},{5,6},{6... | collective-permute-start | bytes 6291464 | tf_op jit(solution)/shard_map/ppermute | solution.py:33
  13.7 22.3 %collective-permute-start.5 = (bf16[32,128,128]{2,1,0:T(8,128)(2,1)}, bf16[32,128,128]{2,1,0:T(8,128)(2,1)S(1)}, u32[]{:S(2)}, u32[]{:S(2)}) collective-permute-start(bf16[32,128,128]{2,1,0:T(8,128)(2,1)} %collective-permute-done.4.refs_13_), channel_id=1, source_target_pairs={{0,32},{32,64},{64,96},{96,0},{8,104},{40,8},{72,40},{104,72},{1,3... | collective-permute-start | bytes 3145736 | tf_op jit(solution)/shard_map/ppermute | solution.py:33
  16.8 19.2 %collective-permute-start.6 = (bf16[32,128,128]{2,1,0:T(8,128)(2,1)}, bf16[32,128,128]{2,1,0:T(8,128)(2,1)}, u32[]{:S(2)}, u32[]{:S(2)}) collective-permute-start(bf16[32,128,128]{2,1,0:T(8,128)(2,1)} %collective-permute-done.3.refs_3_), channel_id=1, source_target_pairs={{0,8},{8,0},{1,9},{9,1},{2,10},{10,2},{3,11},{11,3},{4,12},{12,4},... | collective-permute-start | bytes 3145736 | tf_op jit(solution)/shard_map/ppermute | solution.py:38
  19.0 2.8 %copy-start.5 = (bf16[1,1,128,16384]{3,2,1,0:T(8,128)(2,1)S(1)}, bf16[1,1,128,16384]{3,2,1,0:T(8,128)(2,1)}, u32[]{:S(2)}) copy-start(bf16[1,1,128,16384]{3,2,1,0:T(8,128)(2,1)} %param.6) | copy-start | bytes 12582916
  36.8 4.4 %copy-start.6 = (bf16[1,1,64,16384]{3,2,1,0:T(8,128)(2,1)S(1)}, bf16[1,1,64,16384]{3,2,1,0:T(8,128)(2,1)}, u32[]{:S(2)}) copy-start(bf16[1,1,64,16384]{3,2,1,0:T(8,128)(2,1)} %param.8) | copy-start | bytes 6291460
  36.8 5.6 %collective-permute-start.7 = (bf16[32,16384]{1,0:T(8,128)(2,1)}, bf16[32,16384]{1,0:T(8,128)(2,1)S(1)}, u32[]{:S(2)}, u32[]{:S(2)}) collective-permute-start(bf16[32,16384]{1,0:T(8,128)(2,1)} %get-tuple-element.20), channel_id=1, source_target_pairs={{0,8},{8,0},{1,9},{9,1},{2,10},{10,2},{3,11},{11,3},{4,12},{12,4},... | collective-permute-start | bytes 3145736 | tf_op jit(solution)/shard_map/ppermute | solution.py:38
  37.6 6.8 %collective-permute-start.8 = (bf16[32,128,128]{2,1,0:T(8,128)(2,1)}, bf16[32,128,128]{2,1,0:T(8,128)(2,1)S(1)}, u32[]{:S(2)}, u32[]{:S(2)}) collective-permute-start(bf16[32,128,128]{2,1,0:T(8,128)(2,1)} %get-tuple-element.21), channel_id=1, source_target_pairs={{0,8},{8,0},{1,9},{9,1},{2,10},{10,2},{3,11},{11,3},{4,12},{12,4},... | collective-permute-start | bytes 3145736 | tf_op jit(solution)/shard_map/ppermute | solution.py:38
  37.6 8.2 %collective-permute-start.11 = (bf16[64,16384]{1,0:T(8,128)(2,1)S(1)}, bf16[64,16384]{1,0:T(8,128)(2,1)S(1)}, u32[]{:S(2)}, u32[]{:S(2)}) collective-permute-start(bf16[64,16384]{1,0:T(8,128)(2,1)S(1)} %get-tuple-element.22), channel_id=1, source_target_pairs={{0,8},{8,0},{1,9},{9,1},{2,10},{10,2},{3,11},{11,3},{4,12},{12,4},... | collective-permute-start | bytes 6291464 | tf_op jit(solution)/shard_map/ppermute | solution.py:38
  38.2 14.0 %collective-permute-start.9 = (bf16[32,16384]{1,0:T(8,128)(2,1)S(1)}, bf16[32,16384]{1,0:T(8,128)(2,1)S(1)}, u32[]{:S(2)}, u32[]{:S(2)}) collective-permute-start(bf16[32,16384]{1,0:T(8,128)(2,1)S(1)} %constant_dynamic-slice_fusion.8), channel_id=1, source_target_pairs={{0,1},{1,2},{2,3},{3,0},{8,11},{9,8},{10,9},{11,10},{4,5},{5,6},{6... | collective-permute-start | bytes 3145736 | tf_op jit(solution)/shard_map/ppermute | solution.py:33
  40.4 14.2 %collective-permute-start.10 = (bf16[32,128,128]{2,1,0:T(8,128)(2,1)}, bf16[32,128,128]{2,1,0:T(8,128)(2,1)S(1)}, u32[]{:S(2)}, u32[]{:S(2)}) collective-permute-start(bf16[32,128,128]{2,1,0:T(8,128)(2,1)} %get-tuple-element.23.refs_14_), channel_id=1, source_target_pairs={{0,32},{32,64},{64,96},{96,0},{8,104},{40,8},{72,40},{104,72},{1,3... | collective-permute-start | bytes 3145736 | tf_op jit(solution)/shard_map/ppermute | solution.py:33
  54.6 18.1 %copy-start = (bf16[64,128,128]{2,1,0:T(8,128)(2,1)}, bf16[64,128,128]{2,1,0:T(8,128)(2,1)S(1)}, u32[]{:S(2)}) copy-start(bf16[64,128,128]{2,1,0:T(8,128)(2,1)S(1)} %get-tuple-element.26.refs_20_) | copy-start | bytes 6291460
  54.6 18.1 %copy-start.2 = (bf16[32,128,128]{2,1,0:T(8,128)(2,1)}, bf16[32,128,128]{2,1,0:T(8,128)(2,1)S(1)}, u32[]{:S(2)}) copy-start(bf16[32,128,128]{2,1,0:T(8,128)(2,1)S(1)} %get-tuple-element.28.refs_18_) | copy-start | bytes 3145732
  54.8 24.4 %collective-permute-start.14 = (bf16[32,128,128]{2,1,0:T(8,128)(2,1)S(1)}, bf16[32,128,128]{2,1,0:T(8,128)(2,1)S(1)}, u32[]{:S(2)}, u32[]{:S(2)}) collective-permute-start(bf16[32,128,128]{2,1,0:T(8,128)(2,1)S(1)} %bitcast.53), channel_id=1, source_target_pairs={{0,4},{4,0},{1,5},{5,1},{2,6},{6,2},{3,7},{7,3},{8,12},{12,8},{9,1... | collective-permute-start | bytes 3145736 | tf_op jit(solution)/shard_map/ppermute | solution.py:38
  56.4 24.1 %collective-permute-start.18 = (bf16[32,128,128]{2,1,0:T(8,128)(2,1)S(1)}, bf16[32,128,128]{2,1,0:T(8,128)(2,1)S(1)}, u32[]{:S(2)}, u32[]{:S(2)}) collective-permute-start(bf16[32,128,128]{2,1,0:T(8,128)(2,1)S(1)} %get-tuple-element.28.refs_18_), channel_id=1, source_target_pairs={{0,8},{8,0},{1,9},{9,1},{2,10},{10,2},{3,11},{11,3},{4,12},{12,4},... | collective-permute-start | bytes 3145736 | tf_op jit(solution)/shard_map/ppermute | solution.py:38
  57.2 28.4 %collective-permute-start.12 = (bf16[64,128,128]{2,1,0:T(8,128)(2,1)S(1)}, bf16[64,128,128]{2,1,0:T(8,128)(2,1)S(1)}, u32[]{:S(2)}, u32[]{:S(2)}) collective-permute-start(bf16[64,128,128]{2,1,0:T(8,128)(2,1)S(1)} %get-tuple-element.25.refs_6_), channel_id=1, source_target_pairs={{0,1},{1,2},{2,3},{3,0},{8,11},{9,8},{10,9},{11,10},{4,5},{5,6},{6... | collective-permute-start | bytes 6291464 | tf_op jit(solution)/shard_map/ppermute | solution.py:33
  59.8 25.8 %collective-permute-start.13 = (bf16[64,128,128]{2,1,0:T(8,128)(2,1)S(1)}, bf16[64,128,128]{2,1,0:T(8,128)(2,1)S(1)}, u32[]{:S(2)}, u32[]{:S(2)}) collective-permute-start(bf16[64,128,128]{2,1,0:T(8,128)(2,1)S(1)} %get-tuple-element.26.refs_20_), channel_id=1, source_target_pairs={{0,32},{32,64},{64,96},{96,0},{8,104},{40,8},{72,40},{104,72},{1,3... | collective-permute-start | bytes 6291464 | tf_op jit(solution)/shard_map/ppermute | solution.py:33
  60.0 25.6 %collective-permute-start.15 = (bf16[32,128,128]{2,1,0:T(8,128)(2,1)S(1)}, bf16[32,128,128]{2,1,0:T(8,128)(2,1)S(1)}, u32[]{:S(2)}, u32[]{:S(2)}) collective-permute-start(bf16[32,128,128]{2,1,0:T(8,128)(2,1)S(1)} %get-tuple-element.28.refs_18_), channel_id=1, source_target_pairs={{0,20},{4,16},{16,4},{20,0},{1,21},{5,17},{17,5},{21,1},{2,22},{6,... | collective-permute-start | bytes 3145736 | tf_op jit(solution)/shard_map/ppermute | solution.py:38
  79.2 6.4 %collective-permute-start.16 = (bf16[32,128,128]{2,1,0:T(8,128)(2,1)S(1)}, bf16[32,128,128]{2,1,0:T(8,128)(2,1)S(1)}, u32[]{:S(2)}, u32[]{:S(2)}) collective-permute-start(bf16[32,128,128]{2,1,0:T(8,128)(2,1)S(1)} %get-tuple-element.30.refs_4_), channel_id=1, source_target_pairs={{0,8},{8,0},{1,9},{9,1},{2,10},{10,2},{3,11},{11,3},{4,12},{12,4},... | collective-permute-start | bytes 3145736 | tf_op jit(solution)/shard_map/ppermute | solution.py:38
  80.5 5.1 %collective-permute-start.17 = (bf16[32,128,128]{2,1,0:T(8,128)(2,1)S(1)}, bf16[32,128,128]{2,1,0:T(8,128)(2,1)S(1)}, u32[]{:S(2)}, u32[]{:S(2)}) collective-permute-start(bf16[32,128,128]{2,1,0:T(8,128)(2,1)S(1)} %get-tuple-element.31.refs_15_), channel_id=1, source_target_pairs={{0,8},{8,0},{1,9},{9,1},{2,10},{10,2},{3,11},{11,3},{4,12},{12,4},... | collective-permute-start | bytes 3145736 | tf_op jit(solution)/shard_map/ppermute | solution.py:38
  85.6 10.2 %collective-permute-start.19 = (bf16[64,128,128]{2,1,0:T(8,128)(2,1)S(1)}, bf16[64,128,128]{2,1,0:T(8,128)(2,1)S(1)}, u32[]{:S(2)}, u32[]{:S(2)}) collective-permute-start(bf16[64,128,128]{2,1,0:T(8,128)(2,1)S(1)} %get-tuple-element.32.refs_3_), channel_id=1, source_target_pairs={{0,8},{8,0},{1,9},{9,1},{2,10},{10,2},{3,11},{11,3},{4,12},{12,4},... | collective-permute-start | bytes 6291464 | tf_op jit(solution)/shard_map/ppermute | solution.py:38
  86.1 9.8 %collective-permute-start.21 = (bf16[64,128,128]{2,1,0:T(8,128)(2,1)S(1)}, bf16[64,128,128]{2,1,0:T(8,128)(2,1)S(1)}, u32[]{:S(2)}, u32[]{:S(2)}) collective-permute-start(bf16[64,128,128]{2,1,0:T(8,128)(2,1)S(1)} %get-tuple-element.34.refs_21_), channel_id=1, source_target_pairs={{0,8},{8,0},{1,9},{9,1},{2,10},{10,2},{3,11},{11,3},{4,12},{12,4},... | collective-permute-start | bytes 6291464 | tf_op jit(solution)/shard_map/ppermute | solution.py:38
  86.2 8.1 %collective-permute-start.20 = (bf16[32,128,128]{2,1,0:T(8,128)(2,1)S(1)}, bf16[32,128,128]{2,1,0:T(8,128)(2,1)S(1)}, u32[]{:S(2)}, u32[]{:S(2)}) collective-permute-start(bf16[32,128,128]{2,1,0:T(8,128)(2,1)S(1)} %get-tuple-element.33.refs_8_), channel_id=1, source_target_pairs={{0,8},{8,0},{1,9},{9,1},{2,10},{10,2},{3,11},{11,3},{4,12},{12,4},... | collective-permute-start | bytes 3145736 | tf_op jit(solution)/shard_map/ppermute | solution.py:38
  86.6 9.3 %copy-start.1 = (bf16[64,128,128]{2,1,0:T(8,128)(2,1)S(1)}, bf16[64,128,128]{2,1,0:T(8,128)(2,1)}, u32[]{:S(2)}) copy-start(bf16[64,128,128]{2,1,0:T(8,128)(2,1)} %copy-done) | copy-start | bytes 6291460
  86.6 9.3 %copy-start.3 = (bf16[32,128,128]{2,1,0:T(8,128)(2,1)S(1)}, bf16[32,128,128]{2,1,0:T(8,128)(2,1)}, u32[]{:S(2)}) copy-start(bf16[32,128,128]{2,1,0:T(8,128)(2,1)} %copy-done.2) | copy-start | bytes 3145732
  86.6 9.3 %copy-start.4 = (bf16[1,32,128,128]{3,2,1,0:T(8,128)(2,1)S(1)}, bf16[1,32,128,128]{3,2,1,0:T(8,128)(2,1)}, u32[]{:S(2)}) copy-start(bf16[1,32,128,128]{3,2,1,0:T(8,128)(2,1)} %param.11) | copy-start | bytes 3145732
  86.6 9.3 %collective-permute-start.22 = (bf16[32,128,128]{2,1,0:T(8,128)(2,1)S(1)}, bf16[32,128,128]{2,1,0:T(8,128)(2,1)S(1)}, u32[]{:S(2)}, u32[]{:S(2)}) collective-permute-start(bf16[32,128,128]{2,1,0:T(8,128)(2,1)S(1)} %get-tuple-element.35.refs_23_), channel_id=1, source_target_pairs={{0,8},{8,0},{1,9},{9,1},{2,10},{10,2},{3,11},{11,3},{4,12},{12,4},... | collective-permute-start | bytes 3145736 | tf_op jit(solution)/shard_map/ppermute | solution.py:38
  107.7 14.3 %all-to-all-start = ((f32[128,1,16]{2,1,0:T(1,128)}), f32[128,1,16]{2,1,0:T(1,128)S(1)}, u32[]{:S(2)}, u32[]{:S(2)}) async-start(f32[128,1,16]{2,1,0:T(1,128)} %bitcast.20), calls=%async_computation | async-start | bytes 131072 | tf_op jit(solution)/shard_map/all_to_all | solution.py:290

commit v6 on v5

--- a/solution.py
+++ b/solution.py
@@ -44,6 +44,25 @@
 
 def half_of(share, core):
     return lax.dynamic_slice_in_dim(share, core * HALF, HALF, 0)
+
+
+def half_kernel(core_ref, share_ref, out_ref, sem):
+    at = pl.multiple_of(core_ref[0] * HALF, HALF)
+    copy = pltpu.make_async_copy(share_ref.at[pl.ds(at, HALF)], out_ref, sem)
+    copy.start()
+    copy.wait()
+
+
+def half_copied(share, core):
+    return pl.pallas_call(
+        half_kernel,
+        out_shape=jax.ShapeDtypeStruct((HALF,) + share.shape[1:], share.dtype),
+        in_specs=[smem(), hbm()],
+        out_specs=hbm(),
+        scratch_shapes=[pltpu.SemaphoreType.DMA(())],
+        compiler_params=pltpu.CompilerParams(vmem_limit_bytes=MIB),
+        name="half",
+    )(core.reshape(1), share)
 
 
 def matrices(flat):
@@ -263,7 +282,7 @@
     who = jnp.sum(jnp.where(place // NBAS == slots.T, owner, 0), axis=0)
     link, zz = ("zl",), ("zh", "zl")
     near, bnear_a = around(raw_share, "y"), around(slab, "x")
-    pair, bpair = across(half_of(raw_share, core), link), across(slab, zz)
+    pair, bpair = across(half_copied(raw_share, core), link), across(slab, zz)
     bother = swapped(slab)
     bnear_b = around(bother, "x")
     sbnear_a = swapped(bnear_a)

time: 123 us -> 126 us (1.024)
  local copies, waits for them, and re-layouts: 12.3 us -> 18.2 us
  waiting for transfers between devices: 45.6 us -> 42.5 us
    unnamed x25 -> x27, local copies, waits for them, and re-layouts: 6.61 us -> 14.8 us
    dynamic_slice x2 -> x1, local copies, waits for them, and re-layouts: 2.33 us -> 0.07 us  [half_of(): return lax.dynamic_slice_in_dim(share, core * HALF, HALF, 0)]
    ppermute x7, waiting for transfers between devices: 11.5 us -> 9.67 us  [around(): lax.ppermute(value, ('x', 'core') if axis == 'x' else ('core', axis), pairs)]
  transfers between devices with their start and end apart: 24 -> 24, of which waited for: 10 -> 9; matrix products, arithmetic and copies ran while one was open for 11% -> 12% of each run, Pallas kernels for 16% -> 16%
where the time goes in v6:
time: 126 us
  waiting for transfers between devices  42.5 us (34%)
  Pallas kernels  30.9 us (25%)
  starting transfers between devices  29.6 us (23%)
  local copies, waits for them, and re-layouts  18.2 us (14%)
  other arithmetic  3.77 us (3%)
    ppermute x16, waiting for transfers between devices, across(): return lax.ppermute(value, axes, [(i, count - 1 - i) for i in range(count)])  25.3 us
    pallas_call x2, Pallas kernels, product(): pl.pallas_call(lambda *refs: product_kernel(sizes, count, acc is None, *r...  19 us
    unnamed x27, local copies, waits for them, and re-layouts  14.8 us
    ppermute x16, starting transfers between devices, across(): return lax.ppermute(value, axes, [(i, count - 1 - i) for i in range(count)])  13.1 us
    ppermute x7, starting transfers between devices, around(): lax.ppermute(value, ('x', 'core') if axis == 'x' else ('core', axis), pairs)  11.5 us
    pallas_call x1, Pallas kernels, final(): pl.pallas_call(lambda *refs: final_kernel(sizes, count, slab_sizes, *refs...  10.9 us
    ppermute x7, waiting for transfers between devices, around(): lax.ppermute(value, ('x', 'core') if axis == 'x' else ('core', axis), pairs)  9.67 us
    all_to_all x1, waiting for transfers between devices, body(): lax.all_to_all(grid.reshape(128, 16), ROWS + BLK, split_axis=0, concat_ax...  7.53 us
  transfers between devices with their start and end apart: 24, of which 9 were waited for; matrix products, arithmetic and copies ran while one was open for 12% of the time, Pallas kernels for 16%

profile of v6, /device:TPU:1, one launch (start us, length us, event | category | flops | bytes accessed | tf_op | source)
XLA Modules:
  0.0 126.0 jit_solution(2693799123031433801)
XLA Ops:
  0.6 1.5 %collective-permute-start.4 = (bf16[32,128,128]{2,1,0:T(8,128)(2,1)}, bf16[32,128,128]{2,1,0:T(8,128)(2,1)}, u32[]{:S(2)}, u32[]{:S(2)}) collective-permute-start(bf16[32,128,128]{2,1,0:T(8,128)(2,1)} %bitcast.67), channel_id=1, source_target_pairs={{0,8},{8,0},{1,9},{9,1},{2,10},{10,2},{3,11},{11,3},{4,12},{12,4},... | collective-permute-start | bytes 3145736 | tf_op jit(solution)/shard_map/ppermute | solution.py:38
  2.1 2.6 %collective-permute-start.3 = (bf16[32,128,128]{2,1,0:T(8,128)(2,1)}, bf16[32,128,128]{2,1,0:T(8,128)(2,1)}, u32[]{:S(2)}, u32[]{:S(2)}) collective-permute-start(bf16[32,128,128]{2,1,0:T(8,128)(2,1)} %bitcast.68), channel_id=1, source_target_pairs={{0,32},{32,64},{64,96},{96,0},{8,104},{40,8},{72,40},{104,72},{1,3... | collective-permute-start | bytes 3145736 | tf_op jit(solution)/shard_map/ppermute | solution.py:33
  4.7 3.8 %collective-permute-start.2 = (bf16[32,128,128]{2,1,0:T(8,128)(2,1)}, bf16[32,128,128]{2,1,0:T(8,128)(2,1)}, u32[]{:S(2)}, u32[]{:S(2)}) collective-permute-start(bf16[32,128,128]{2,1,0:T(8,128)(2,1)} %bitcast.69), channel_id=1, source_target_pairs={{0,20},{4,16},{16,4},{20,0},{1,21},{5,17},{17,5},{21,1},{2,22},{6,... | collective-permute-start | bytes 3145736 | tf_op jit(solution)/shard_map/ppermute | solution.py:38
  8.5 2.7 %collective-permute-start = (bf16[64,16384]{1,0:T(8,128)(2,1)}, bf16[64,16384]{1,0:T(8,128)(2,1)S(1)}, u32[]{:S(2)}, u32[]{:S(2)}) collective-permute-start(bf16[64,16384]{1,0:T(8,128)(2,1)} %bitcast.54), channel_id=1, source_target_pairs={{0,1},{1,2},{2,3},{3,0},{8,11},{9,8},{10,9},{11,10},{4,5},{5,6},{6... | collective-permute-start | bytes 6291464 | tf_op jit(solution)/shard_map/ppermute | solution.py:33
  11.2 1.6 %copy-done.2 = bf16[1,64,16384]{2,1,0:T(8,128)(2,1)S(1)} copy-done((bf16[1,64,16384]{2,1,0:T(8,128)(2,1)S(1)}, bf16[1,64,16384]{2,1,0:T(8,128)(2,1)}, u32[]{:S(2)}) %copy-start.2) | copy-done | bytes 2097176
  12.8 1.0 half.1
  14.2 0.6 collective-permute-start.5
  14.8 1.9 %collective-permute-done.3.refs_3_ = bf16[32,128,128]{2,1,0:T(8,128)(2,1)} collective-permute-done((bf16[32,128,128]{2,1,0:T(8,128)(2,1)}, bf16[32,128,128]{2,1,0:T(8,128)(2,1)}, u32[]{:S(2)}, u32[]{:S(2)}) %collective-permute-start.3) | collective-permute-done | bytes 1048608 | tf_op jit(solution)/shard_map/ppermute | solution.py:33
  16.8 1.8 %collective-permute-start.6 = (bf16[32,128,128]{2,1,0:T(8,128)(2,1)}, bf16[32,128,128]{2,1,0:T(8,128)(2,1)}, u32[]{:S(2)}, u32[]{:S(2)}) collective-permute-start(bf16[32,128,128]{2,1,0:T(8,128)(2,1)} %collective-permute-done.3.refs_3_), channel_id=1, source_target_pairs={{0,8},{8,0},{1,9},{9,1},{2,10},{10,2},{3,11},{11,3},{4,12},{12,4},... | collective-permute-start | bytes 3145736 | tf_op jit(solution)/shard_map/ppermute | solution.py:38
  19.0 3.7 %copy.27 = bf16[8,8,128,128]{3,2,1,0:T(8,128)(2,1)} copy(bf16[8,8,128,128]{3,1,2,0:T(8,128)(2,1)} %bitcast.55) | data formatting | bytes 4194304
  22.6 3.2 %copy.26 = bf16[16,8,128,128]{3,2,1,0:T(8,128)(2,1)} copy(bf16[16,8,128,128]{3,1,2,0:T(8,128)(2,1)S(1)} %bitcast.71) | data formatting | bytes 8388608
  26.0 11.8 %collective-permute-done.1.refs_1_ = bf16[32,16384]{1,0:T(8,128)(2,1)} collective-permute-done((bf16[32,16384]{1,0:T(8,128)(2,1)}, bf16[32,16384]{1,0:T(8,128)(2,1)}, u32[]{:S(2)}, u32[]{:S(2)}) %collective-permute-start.1) | collective-permute-done | bytes 1048608 | tf_op jit(solution)/shard_map/ppermute | solution.py:38
  37.8 2.2 %copy-done = bf16[16,8,128,128]{3,2,1,0:T(8,128)(2,1)S(1)} copy-done((bf16[16,8,128,128]{3,2,1,0:T(8,128)(2,1)S(1)}, bf16[16,8,128,128]{3,2,1,0:T(8,128)(2,1)}, u32[]{:S(2)}) %copy-start) | copy-done | bytes 4194328
  40.0 1.6 %copy-done.3 = bf16[8,8,128,128]{3,2,1,0:T(8,128)(2,1)S(1)} copy-done((bf16[8,8,128,128]{3,2,1,0:T(8,128)(2,1)S(1)}, bf16[8,8,128,128]{3,2,1,0:T(8,128)(2,1)}, u32[]{:S(2)}) %copy-start.3) | copy-done | bytes 2097176
  41.6 0.5 collective-permute-start.8
  42.2 1.8 %collective-permute-start.9 = (bf16[32,16384]{1,0:T(8,128)(2,1)S(1)}, bf16[32,16384]{1,0:T(8,128)(2,1)S(1)}, u32[]{:S(2)}, u32[]{:S(2)}) collective-permute-start(bf16[32,16384]{1,0:T(8,128)(2,1)S(1)} %constant_dynamic-slice_fusion.8), channel_id=1, source_target_pairs={{0,1},{1,2},{2,3},{3,0},{8,11},{9,8},{10,9},{11,10},{4,5},{5,6},{6... | collective-permute-start | bytes 3145736 | tf_op jit(solution)/shard_map/ppermute | solution.py:33
  44.0 1.3 %collective-permute-start.10 = (bf16[32,128,128]{2,1,0:T(8,128)(2,1)}, bf16[32,128,128]{2,1,0:T(8,128)(2,1)S(1)}, u32[]{:S(2)}, u32[]{:S(2)}) collective-permute-start(bf16[32,128,128]{2,1,0:T(8,128)(2,1)} %get-tuple-element.23.refs_14_), channel_id=1, source_target_pairs={{0,32},{32,64},{64,96},{96,0},{8,104},{40,8},{72,40},{104,72},{1,3... | collective-permute-start | bytes 3145736 | tf_op jit(solution)/shard_map/ppermute | solution.py:33
  45.3 0.6 copy.31
  45.9 0.6 copy.29
  46.4 1.4 %maximum_bitcast_fusion = bf16[8,8,128,128]{3,1,2,0:T(8,128)(2,1)S(1)} fusion(bf16[32,16384]{1,0:T(8,128)(2,1)S(1)} %collective-permute-done.7, bf16[32,16384]{1,0:T(8,128)(2,1)} %get-tuple-element.20), kind=kLoop, calls=%fused_computation | loop fusion | flops 4194304 | bytes 4194304
  47.8 0.6 copy.28
  48.4 1.4 %pad_maximum_fusion.refs_1_ = bf16[64,128,128]{2,1,0:T(8,128)(2,1)S(1)} fusion(bf16[32,128,128]{2,1,0:T(8,128)(2,1)S(1)} %collective-permute-done.8, bf16[32,128,128]{2,1,0:T(8,128)(2,1)} %get-tuple-element.21), kind=kLoop, calls=%fused_computation.1 | loop fusion | flops 1048576 | bytes 4194304 | tf_op jit(solution)/shard_map/concatenate | solution.py:293
  49.8 0.6 copy.30
  50.4 5.8 %collective-permute-done.9.refs_2_ = bf16[32,16384]{1,0:T(8,128)(2,1)S(1)} collective-permute-done((bf16[32,16384]{1,0:T(8,128)(2,1)S(1)}, bf16[32,16384]{1,0:T(8,128)(2,1)S(1)}, u32[]{:S(2)}, u32[]{:S(2)}) %collective-permute-start.9) | collective-permute-done | bytes 1048608 | tf_op jit(solution)/shard_map/ppermute | solution.py:33
  56.2 2.0 %collective-permute-done.10.refs_3_ = bf16[32,128,128]{2,1,0:T(8,128)(2,1)S(1)} collective-permute-done((bf16[32,128,128]{2,1,0:T(8,128)(2,1)}, bf16[32,128,128]{2,1,0:T(8,128)(2,1)S(1)}, u32[]{:S(2)}, u32[]{:S(2)}) %collective-permute-start.10) | collective-permute-done | bytes 1048608 | tf_op jit(solution)/shard_map/ppermute | solution.py:33
  58.2 0.2 copy.32
  58.5 1.6 %collective-permute-start.18 = (bf16[32,128,128]{2,1,0:T(8,128)(2,1)S(1)}, bf16[32,128,128]{2,1,0:T(8,128)(2,1)S(1)}, u32[]{:S(2)}, u32[]{:S(2)}) collective-permute-start(bf16[32,128,128]{2,1,0:T(8,128)(2,1)S(1)} %get-tuple-element.28.refs_18_), channel_id=1, source_target_pairs={{0,8},{8,0},{1,9},{9,1},{2,10},{10,2},{3,11},{11,3},{4,12},{12,4},... | collective-permute-start | bytes 3145736 | tf_op jit(solution)/shard_map/ppermute | solution.py:38
  60.1 2.2 %collective-permute-start.12 = (bf16[64,128,128]{2,1,0:T(8,128)(2,1)S(1)}, bf16[64,128,128]{2,1,0:T(8,128)(2,1)S(1)}, u32[]{:S(2)}, u32[]{:S(2)}) collective-permute-start(bf16[64,128,128]{2,1,0:T(8,128)(2,1)S(1)} %get-tuple-element.25.refs_6_), channel_id=1, source_target_pairs={{0,1},{1,2},{2,3},{3,0},{8,11},{9,8},{10,9},{11,10},{4,5},{5,6},{6... | collective-permute-start | bytes 6291464 | tf_op jit(solution)/shard_map/ppermute | solution.py:33
  62.4 0.3 collective-permute-start.13
  62.6 0.1 collective-permute-start.15
  62.8 12.4 %product.2.refs_2_.refs_4_.refs_6_ = f32[64,128,128]{2,1,0:T(8,128)S(1)} custom-call(s32[1024]{0:T(1024)S(1)} %pad_add_fusion.refs_9_.refs_0_, s32[1024]{0:T(1024)S(1)} %pad_add_fusion.1.refs_10_.refs_1_, bf16[128,128,128]{2,1,0:T(8,128)(2,1)S(1)} %bitcast.48, bf16[64,128,128]{2,1,0:T(8,128)(2,1)S(1)} %bitcast.60, bf16[64,128,128]{2,1,0:T(8,128)(2,1)S(1)} %bitcast.62, ...), custom_call_target="tpu_custom_call" | custom-call | flops 8589934592 | bytes 20971520 | tf_op jit(solution)/shard_map/product/pallas_call | solution.py:203
  75.2 6.6 %collective-permute-done.14.refs_2_ = bf16[32,128,128]{2,1,0:T(8,128)(2,1)S(1)} collective-permute-done((bf16[32,128,128]{2,1,0:T(8,128)(2,1)S(1)}, bf16[32,128,128]{2,1,0:T(8,128)(2,1)S(1)}, u32[]{:S(2)}, u32[]{:S(2)}) %collective-permute-start.14) | collective-permute-done | bytes 1048608 | tf_op jit(solution)/shard_map/ppermute | solution.py:38
  81.8 2.3 %collective-permute-start.16 = (bf16[32,128,128]{2,1,0:T(8,128)(2,1)S(1)}, bf16[32,128,128]{2,1,0:T(8,128)(2,1)S(1)}, u32[]{:S(2)}, u32[]{:S(2)}) collective-permute-start(bf16[32,128,128]{2,1,0:T(8,128)(2,1)S(1)} %get-tuple-element.30.refs_4_), channel_id=1, source_target_pairs={{0,8},{8,0},{1,9},{9,1},{2,10},{10,2},{3,11},{11,3},{4,12},{12,4},... | collective-permute-start | bytes 3145736 | tf_op jit(solution)/shard_map/ppermute | solution.py:38
  84.1 0.3 collective-permute-start.17
  84.3 4.2 %collective-permute-done.15.refs_3_ = bf16[32,128,128]{2,1,0:T(8,128)(2,1)S(1)} collective-permute-done((bf16[32,128,128]{2,1,0:T(8,128)(2,1)S(1)}, bf16[32,128,128]{2,1,0:T(8,128)(2,1)S(1)}, u32[]{:S(2)}, u32[]{:S(2)}) %collective-permute-start.15) | collective-permute-done | bytes 1048608 | tf_op jit(solution)/shard_map/ppermute | solution.py:38
  88.6 0.4 collective-permute-start.19
  89.0 0.1 collective-permute-start.21
  89.2 0.4 collective-permute-start.20
  89.5 0.1 collective-permute-start.22
  89.7 6.5 %product.3.refs_10_ = f32[64,128,128]{2,1,0:T(8,128)S(1)} custom-call(s32[512]{0:T(512)S(1)} %get-tuple-element.78.refs_11_.refs_0_, s32[512]{0:T(512)S(1)} %pad_add_fusion.5.refs_12_.refs_1_, bf16[128,128,128]{2,1,0:T(8,128)(2,1)S(1)} %bitcast.49, bf16[64,128,128]{2,1,0:T(8,128)(2,1)S(1)} %get-tuple-element.32.refs_3_, ...), custom_call_target="tpu_custom_call" | custom-call | flops 4294967296 | bytes 16777216 | tf_op jit(solution)/shard_map/product/pallas_call | solution.py:203
  96.2 1.1 collective-permute-done.20.refs_9_
  97.3 1.5 %collective-permute-done.22.refs_24_ = bf16[32,128,128]{2,1,0:T(8,128)(2,1)S(1)} collective-permute-done((bf16[32,128,128]{2,1,0:T(8,128)(2,1)S(1)}, bf16[32,128,128]{2,1,0:T(8,128)(2,1)S(1)}, u32[]{:S(2)}, u32[]{:S(2)}) %collective-permute-start.22) | collective-permute-done | bytes 1048608 | tf_op jit(solution)/shard_map/ppermute | solution.py:38
  98.8 10.9 %final.1 = (bf16[64,128,128]{2,1,0:T(8,128)(2,1)S(1)}, f32[16,128]{1,0:T(8,128)S(1)}) custom-call(s32[512]{0:T(512)S(1)} %get-tuple-element.77.refs_13_.refs_0_, s32[512]{0:T(512)S(1)} %pad_add_fusion.3.refs_14_.refs_1_, s32[16]{0:T(128)S(1)} %select_reduce_fusion.refs_8_.refs_2_, s32[256]{0:T(256)S(1)} %get-tuple-element.79.refs_5_.refs_3_, ...), custom_call_target="tpu_custom_call" | custom-call | flops 8589934592 | bytes 41943040 | tf_op jit(solution)/shard_map/final/pallas_call | solution.py:224
  109.7 0.7 all_to_all.6
  110.4 5.0 %all-to-all-start = ((f32[128,1,16]{2,1,0:T(1,128)}), f32[128,1,16]{2,1,0:T(1,128)S(1)}, u32[]{:S(2)}, u32[]{:S(2)}) async-start(f32[128,1,16]{2,1,0:T(1,128)} %bitcast.20), calls=%async_computation | async-start | bytes 131072 | tf_op jit(solution)/shard_map/all_to_all | solution.py:309
  115.5 2.3 %reshape.290 = bf16[1,1,64,16384]{3,2,1,0:T(8,128)(2,1)} reshape(bf16[64,128,128]{2,1,0:T(8,128)(2,1)S(1)} %get-tuple-element.36) | data formatting | bytes 4194304 | tf_op jit(solution)/shard_map/reshape | solution.py:310
  117.8 7.5 %all-to-all-done = f32[128,1,16]{2,1,0:T(1,128)S(1)} async-done(((f32[128,1,16]{2,1,0:T(1,128)}), f32[128,1,16]{2,1,0:T(1,128)S(1)}, u32[]{:S(2)}, u32[]{:S(2)}) %all-to-all-start) | async-done | bytes 8224 | tf_op jit(solution)/shard_map/all_to_all | solution.py:309
  125.3 0.7 reduce_sum.19
  (61 shorter events, 1.0 us)
Async XLA Ops:
  0.6 13.6 %collective-permute-start.4 = (bf16[32,128,128]{2,1,0:T(8,128)(2,1)}, bf16[32,128,128]{2,1,0:T(8,128)(2,1)}, u32[]{:S(2)}, u32[]{:S(2)}) collective-permute-start(bf16[32,128,128]{2,1,0:T(8,128)(2,1)} %bitcast.67), channel_id=1, source_target_pairs={{0,8},{8,0},{1,9},{9,1},{2,10},{10,2},{3,11},{11,3},{4,12},{12,4},... | collective-permute-start | bytes 3145736 | tf_op jit(solution)/shard_map/ppermute | solution.py:38
  2.1 14.6 %collective-permute-start.3 = (bf16[32,128,128]{2,1,0:T(8,128)(2,1)}, bf16[32,128,128]{2,1,0:T(8,128)(2,1)}, u32[]{:S(2)}, u32[]{:S(2)}) collective-permute-start(bf16[32,128,128]{2,1,0:T(8,128)(2,1)} %bitcast.68), channel_id=1, source_target_pairs={{0,32},{32,64},{64,96},{96,0},{8,104},{40,8},{72,40},{104,72},{1,3... | collective-permute-start | bytes 3145736 | tf_op jit(solution)/shard_map/ppermute | solution.py:33
  4.7 33.1 %collective-permute-start.2 = (bf16[32,128,128]{2,1,0:T(8,128)(2,1)}, bf16[32,128,128]{2,1,0:T(8,128)(2,1)}, u32[]{:S(2)}, u32[]{:S(2)}) collective-permute-start(bf16[32,128,128]{2,1,0:T(8,128)(2,1)} %bitcast.69), channel_id=1, source_target_pairs={{0,20},{4,16},{16,4},{20,0},{1,21},{5,17},{17,5},{21,1},{2,22},{6,... | collective-permute-start | bytes 3145736 | tf_op jit(solution)/shard_map/ppermute | solution.py:38
  8.5 29.4 %collective-permute-start = (bf16[64,16384]{1,0:T(8,128)(2,1)}, bf16[64,16384]{1,0:T(8,128)(2,1)S(1)}, u32[]{:S(2)}, u32[]{:S(2)}) collective-permute-start(bf16[64,16384]{1,0:T(8,128)(2,1)} %bitcast.54), channel_id=1, source_target_pairs={{0,1},{1,2},{2,3},{3,0},{8,11},{9,8},{10,9},{11,10},{4,5},{5,6},{6... | collective-permute-start | bytes 6291464 | tf_op jit(solution)/shard_map/ppermute | solution.py:33
  11.2 1.6 %copy-start.2 = (bf16[1,64,16384]{2,1,0:T(8,128)(2,1)S(1)}, bf16[1,64,16384]{2,1,0:T(8,128)(2,1)}, u32[]{:S(2)}) copy-start(bf16[1,64,16384]{2,1,0:T(8,128)(2,1)} %param.7) | copy-start | bytes 6291460
  12.8 1.1 copy-start.8
  12.8 1.4 %copy-start.9 = (s32[1,1,16,16,3]{3,2,4,1,0:T(8,128)S(1)}, s32[1,1,16,16,3]{3,2,4,1,0:T(8,128)}, u32[]{:S(2)}) copy-start(s32[1,1,16,16,3]{3,2,4,1,0:T(8,128)} %param.10) | copy-start | bytes 9220
  13.8 24.0 %collective-permute-start.1 = (bf16[32,16384]{1,0:T(8,128)(2,1)}, bf16[32,16384]{1,0:T(8,128)(2,1)}, u32[]{:S(2)}, u32[]{:S(2)}) collective-permute-start(bf16[32,16384]{1,0:T(8,128)(2,1)} %half.1), channel_id=1, source_target_pairs={{0,4},{4,0},{1,5},{5,1},{2,6},{6,2},{3,7},{7,3},{8,12},{12,8},{9,1... | collective-permute-start | bytes 3145736 | tf_op jit(solution)/shard_map/ppermute | solution.py:38
  14.2 23.6 %collective-permute-start.5 = (bf16[32,128,128]{2,1,0:T(8,128)(2,1)}, bf16[32,128,128]{2,1,0:T(8,128)(2,1)S(1)}, u32[]{:S(2)}, u32[]{:S(2)}) collective-permute-start(bf16[32,128,128]{2,1,0:T(8,128)(2,1)} %collective-permute-done.4.refs_13_), channel_id=1, source_target_pairs={{0,32},{32,64},{64,96},{96,0},{8,104},{40,8},{72,40},{104,72},{1,3... | collective-permute-start | bytes 3145736 | tf_op jit(solution)/shard_map/ppermute | solution.py:33
  16.8 21.0 %collective-permute-start.6 = (bf16[32,128,128]{2,1,0:T(8,128)(2,1)}, bf16[32,128,128]{2,1,0:T(8,128)(2,1)}, u32[]{:S(2)}, u32[]{:S(2)}) collective-permute-start(bf16[32,128,128]{2,1,0:T(8,128)(2,1)} %collective-permute-done.3.refs_3_), channel_id=1, source_target_pairs={{0,8},{8,0},{1,9},{9,1},{2,10},{10,2},{3,11},{11,3},{4,12},{12,4},... | collective-permute-start | bytes 3145736 | tf_op jit(solution)/shard_map/ppermute | solution.py:38
  19.0 3.7 %copy-start.6 = (bf16[1,1,128,16384]{3,2,1,0:T(8,128)(2,1)S(1)}, bf16[1,1,128,16384]{3,2,1,0:T(8,128)(2,1)}, u32[]{:S(2)}) copy-start(bf16[1,1,128,16384]{3,2,1,0:T(8,128)(2,1)} %param.6) | copy-start | bytes 12582916
  37.8 2.2 %copy-start = (bf16[16,8,128,128]{3,2,1,0:T(8,128)(2,1)S(1)}, bf16[16,8,128,128]{3,2,1,0:T(8,128)(2,1)}, u32[]{:S(2)}) copy-start(bf16[16,8,128,128]{3,2,1,0:T(8,128)(2,1)} %copy.26) | copy-start | bytes 12582916
  40.0 1.6 %copy-start.3 = (bf16[8,8,128,128]{3,2,1,0:T(8,128)(2,1)S(1)}, bf16[8,8,128,128]{3,2,1,0:T(8,128)(2,1)}, u32[]{:S(2)}) copy-start(bf16[8,8,128,128]{3,2,1,0:T(8,128)(2,1)} %copy.27) | copy-start | bytes 6291460
  41.6 3.7 %copy-start.7 = (bf16[1,1,64,16384]{3,2,1,0:T(8,128)(2,1)S(1)}, bf16[1,1,64,16384]{3,2,1,0:T(8,128)(2,1)}, u32[]{:S(2)}) copy-start(bf16[1,1,64,16384]{3,2,1,0:T(8,128)(2,1)} %param.8) | copy-start | bytes 6291460
  41.6 4.8 %collective-permute-start.7 = (bf16[32,16384]{1,0:T(8,128)(2,1)}, bf16[32,16384]{1,0:T(8,128)(2,1)S(1)}, u32[]{:S(2)}, u32[]{:S(2)}) collective-permute-start(bf16[32,16384]{1,0:T(8,128)(2,1)} %get-tuple-element.20), channel_id=1, source_target_pairs={{0,8},{8,0},{1,9},{9,1},{2,10},{10,2},{3,11},{11,3},{4,12},{12,4},... | collective-permute-start | bytes 3145736 | tf_op jit(solution)/shard_map/ppermute | solution.py:38
  41.6 6.8 %collective-permute-start.8 = (bf16[32,128,128]{2,1,0:T(8,128)(2,1)}, bf16[32,128,128]{2,1,0:T(8,128)(2,1)S(1)}, u32[]{:S(2)}, u32[]{:S(2)}) collective-permute-start(bf16[32,128,128]{2,1,0:T(8,128)(2,1)} %get-tuple-element.21), channel_id=1, source_target_pairs={{0,8},{8,0},{1,9},{9,1},{2,10},{10,2},{3,11},{11,3},{4,12},{12,4},... | collective-permute-start | bytes 3145736 | tf_op jit(solution)/shard_map/ppermute | solution.py:38
  42.1 7.7 %collective-permute-start.11 = (bf16[64,16384]{1,0:T(8,128)(2,1)S(1)}, bf16[64,16384]{1,0:T(8,128)(2,1)S(1)}, u32[]{:S(2)}, u32[]{:S(2)}) collective-permute-start(bf16[64,16384]{1,0:T(8,128)(2,1)S(1)} %get-tuple-element.22), channel_id=1, source_target_pairs={{0,8},{8,0},{1,9},{9,1},{2,10},{10,2},{3,11},{11,3},{4,12},{12,4},... | collective-permute-start | bytes 6291464 | tf_op jit(solution)/shard_map/ppermute | solution.py:38
  42.2 14.0 %collective-permute-start.9 = (bf16[32,16384]{1,0:T(8,128)(2,1)S(1)}, bf16[32,16384]{1,0:T(8,128)(2,1)S(1)}, u32[]{:S(2)}, u32[]{:S(2)}) collective-permute-start(bf16[32,16384]{1,0:T(8,128)(2,1)S(1)} %constant_dynamic-slice_fusion.8), channel_id=1, source_target_pairs={{0,1},{1,2},{2,3},{3,0},{8,11},{9,8},{10,9},{11,10},{4,5},{5,6},{6... | collective-permute-start | bytes 3145736 | tf_op jit(solution)/shard_map/ppermute | solution.py:33
  44.0 14.2 %collective-permute-start.10 = (bf16[32,128,128]{2,1,0:T(8,128)(2,1)}, bf16[32,128,128]{2,1,0:T(8,128)(2,1)S(1)}, u32[]{:S(2)}, u32[]{:S(2)}) collective-permute-start(bf16[32,128,128]{2,1,0:T(8,128)(2,1)} %get-tuple-element.23.refs_14_), channel_id=1, source_target_pairs={{0,32},{32,64},{64,96},{96,0},{8,104},{40,8},{72,40},{104,72},{1,3... | collective-permute-start | bytes 3145736 | tf_op jit(solution)/shard_map/ppermute | solution.py:33
  58.2 4.6 %copy-start.1 = (bf16[16,8,128,128]{3,2,1,0:T(8,128)(2,1)S(1)}, bf16[16,8,128,128]{3,2,1,0:T(8,128)(2,1)}, u32[]{:S(2)}) copy-start(bf16[16,8,128,128]{3,2,1,0:T(8,128)(2,1)} %copy.26) | copy-start | bytes 12582916
  58.2 4.6 %copy-start.4 = (bf16[8,8,128,128]{3,2,1,0:T(8,128)(2,1)S(1)}, bf16[8,8,128,128]{3,2,1,0:T(8,128)(2,1)}, u32[]{:S(2)}) copy-start(bf16[8,8,128,128]{3,2,1,0:T(8,128)(2,1)} %copy.27) | copy-start | bytes 6291460
  58.4 23.4 %collective-permute-start.14 = (bf16[32,128,128]{2,1,0:T(8,128)(2,1)S(1)}, bf16[32,128,128]{2,1,0:T(8,128)(2,1)S(1)}, u32[]{:S(2)}, u32[]{:S(2)}) collective-permute-start(bf16[32,128,128]{2,1,0:T(8,128)(2,1)S(1)} %bitcast.52), channel_id=1, source_target_pairs={{0,4},{4,0},{1,5},{5,1},{2,6},{6,2},{3,7},{7,3},{8,12},{12,8},{9,1... | collective-permute-start | bytes 3145736 | tf_op jit(solution)/shard_map/ppermute | solution.py:38
  58.5 25.6 %collective-permute-start.18 = (bf16[32,128,128]{2,1,0:T(8,128)(2,1)S(1)}, bf16[32,128,128]{2,1,0:T(8,128)(2,1)S(1)}, u32[]{:S(2)}, u32[]{:S(2)}) collective-permute-start(bf16[32,128,128]{2,1,0:T(8,128)(2,1)S(1)} %get-tuple-element.28.refs_18_), channel_id=1, source_target_pairs={{0,8},{8,0},{1,9},{9,1},{2,10},{10,2},{3,11},{11,3},{4,12},{12,4},... | collective-permute-start | bytes 3145736 | tf_op jit(solution)/shard_map/ppermute | solution.py:38
  60.1 28.4 %collective-permute-start.12 = (bf16[64,128,128]{2,1,0:T(8,128)(2,1)S(1)}, bf16[64,128,128]{2,1,0:T(8,128)(2,1)S(1)}, u32[]{:S(2)}, u32[]{:S(2)}) collective-permute-start(bf16[64,128,128]{2,1,0:T(8,128)(2,1)S(1)} %get-tuple-element.25.refs_6_), channel_id=1, source_target_pairs={{0,1},{1,2},{2,3},{3,0},{8,11},{9,8},{10,9},{11,10},{4,5},{5,6},{6... | collective-permute-start | bytes 6291464 | tf_op jit(solution)/shard_map/ppermute | solution.py:33
  62.4 26.2 %collective-permute-start.13 = (bf16[64,128,128]{2,1,0:T(8,128)(2,1)S(1)}, bf16[64,128,128]{2,1,0:T(8,128)(2,1)S(1)}, u32[]{:S(2)}, u32[]{:S(2)}) collective-permute-start(bf16[64,128,128]{2,1,0:T(8,128)(2,1)S(1)} %get-tuple-element.26.refs_20_), channel_id=1, source_target_pairs={{0,32},{32,64},{64,96},{96,0},{8,104},{40,8},{72,40},{104,72},{1,3... | collective-permute-start | bytes 6291464 | tf_op jit(solution)/shard_map/ppermute | solution.py:33
  62.6 25.9 %collective-permute-start.15 = (bf16[32,128,128]{2,1,0:T(8,128)(2,1)S(1)}, bf16[32,128,128]{2,1,0:T(8,128)(2,1)S(1)}, u32[]{:S(2)}, u32[]{:S(2)}) collective-permute-start(bf16[32,128,128]{2,1,0:T(8,128)(2,1)S(1)} %get-tuple-element.28.refs_18_), channel_id=1, source_target_pairs={{0,20},{4,16},{16,4},{20,0},{1,21},{5,17},{17,5},{21,1},{2,22},{6,... | collective-permute-start | bytes 3145736 | tf_op jit(solution)/shard_map/ppermute | solution.py:38
  81.8 6.7 %collective-permute-start.16 = (bf16[32,128,128]{2,1,0:T(8,128)(2,1)S(1)}, bf16[32,128,128]{2,1,0:T(8,128)(2,1)S(1)}, u32[]{:S(2)}, u32[]{:S(2)}) collective-permute-start(bf16[32,128,128]{2,1,0:T(8,128)(2,1)S(1)} %get-tuple-element.30.refs_4_), channel_id=1, source_target_pairs={{0,8},{8,0},{1,9},{9,1},{2,10},{10,2},{3,11},{11,3},{4,12},{12,4},... | collective-permute-start | bytes 3145736 | tf_op jit(solution)/shard_map/ppermute | solution.py:38
  84.1 4.5 %collective-permute-start.17 = (bf16[32,128,128]{2,1,0:T(8,128)(2,1)S(1)}, bf16[32,128,128]{2,1,0:T(8,128)(2,1)S(1)}, u32[]{:S(2)}, u32[]{:S(2)}) collective-permute-start(bf16[32,128,128]{2,1,0:T(8,128)(2,1)S(1)} %get-tuple-element.31.refs_15_), channel_id=1, source_target_pairs={{0,8},{8,0},{1,9},{9,1},{2,10},{10,2},{3,11},{11,3},{4,12},{12,4},... | collective-permute-start | bytes 3145736 | tf_op jit(solution)/shard_map/ppermute | solution.py:38
  88.6 10.2 %collective-permute-start.19 = (bf16[64,128,128]{2,1,0:T(8,128)(2,1)S(1)}, bf16[64,128,128]{2,1,0:T(8,128)(2,1)S(1)}, u32[]{:S(2)}, u32[]{:S(2)}) collective-permute-start(bf16[64,128,128]{2,1,0:T(8,128)(2,1)S(1)} %get-tuple-element.32.refs_3_), channel_id=1, source_target_pairs={{0,8},{8,0},{1,9},{9,1},{2,10},{10,2},{3,11},{11,3},{4,12},{12,4},... | collective-permute-start | bytes 6291464 | tf_op jit(solution)/shard_map/ppermute | solution.py:38
  89.0 9.8 %collective-permute-start.21 = (bf16[64,128,128]{2,1,0:T(8,128)(2,1)S(1)}, bf16[64,128,128]{2,1,0:T(8,128)(2,1)S(1)}, u32[]{:S(2)}, u32[]{:S(2)}) collective-permute-start(bf16[64,128,128]{2,1,0:T(8,128)(2,1)S(1)} %get-tuple-element.34.refs_21_), channel_id=1, source_target_pairs={{0,8},{8,0},{1,9},{9,1},{2,10},{10,2},{3,11},{11,3},{4,12},{12,4},... | collective-permute-start | bytes 6291464 | tf_op jit(solution)/shard_map/ppermute | solution.py:38
  89.2 8.1 %collective-permute-start.20 = (bf16[32,128,128]{2,1,0:T(8,128)(2,1)S(1)}, bf16[32,128,128]{2,1,0:T(8,128)(2,1)S(1)}, u32[]{:S(2)}, u32[]{:S(2)}) collective-permute-start(bf16[32,128,128]{2,1,0:T(8,128)(2,1)S(1)} %get-tuple-element.33.refs_8_), channel_id=1, source_target_pairs={{0,8},{8,0},{1,9},{9,1},{2,10},{10,2},{3,11},{11,3},{4,12},{12,4},... | collective-permute-start | bytes 3145736 | tf_op jit(solution)/shard_map/ppermute | solution.py:38
  89.5 9.3 %copy-start.5 = (bf16[1,32,128,128]{3,2,1,0:T(8,128)(2,1)S(1)}, bf16[1,32,128,128]{3,2,1,0:T(8,128)(2,1)}, u32[]{:S(2)}) copy-start(bf16[1,32,128,128]{3,2,1,0:T(8,128)(2,1)} %param.11) | copy-start | bytes 3145732
  89.5 9.3 %collective-permute-start.22 = (bf16[32,128,128]{2,1,0:T(8,128)(2,1)S(1)}, bf16[32,128,128]{2,1,0:T(8,128)(2,1)S(1)}, u32[]{:S(2)}, u32[]{:S(2)}) collective-permute-start(bf16[32,128,128]{2,1,0:T(8,128)(2,1)S(1)} %get-tuple-element.35.refs_23_), channel_id=1, source_target_pairs={{0,8},{8,0},{1,9},{9,1},{2,10},{10,2},{3,11},{11,3},{4,12},{12,4},... | collective-permute-start | bytes 3145736 | tf_op jit(solution)/shard_map/ppermute | solution.py:38
  110.4 14.9 %all-to-all-start = ((f32[128,1,16]{2,1,0:T(1,128)}), f32[128,1,16]{2,1,0:T(1,128)S(1)}, u32[]{:S(2)}, u32[]{:S(2)}) async-start(f32[128,1,16]{2,1,0:T(1,128)} %bitcast.20), calls=%async_computation | async-start | bytes 131072 | tf_op jit(solution)/shard_map/all_to_all | solution.py:309
